TPU v7x, 32 devices: a whole 2x2x4 slice. The times are simulated.
32 devices in a mesh: row: 4 (over y, x), col: 8 (over z, core).
Axes of the slice: x: 2, y: 2, z: 4, core: 2. Of those that a mesh axis runs over, the one named last changes fastest.
Arguments:
- x_block: bfloat16 [64, 8192], P(None, ('col', 'row')), may hold values from -6 to 6
- tiles: bfloat16 [768, 256, 256], P(('row', 'col')), may hold values from -0.078125 to 0.078125
- coords: int32 [768, 2], P(('row', 'col')), may hold values from 0 to 7, as said below
- counts: int32 [32], P(('row', 'col')), may hold values from 9 to 24, as said below
Outputs:
- basis: float32 [64, 8192], P(None, ('row', 'col'))
- factor: float32 [64, 64], replicated
Inputs may be any that keep to these rules, and one draw needn't show every extreme that they name: `coords`: column 0 is a tile row below 8, column 1 a tile column below 4; at the device of place p = i * 8 + j, slot 0 names tile row j. `counts`: some device uses all 24 slots.
All inputs are finite; a program needn't handle non-finite values.
Results may differ from a plain program's by a relative error of at most 0.0003.
Values may be sent and summed in bfloat16 or wider, within the bound.
No kernel may reach another device: no remote copies, remote signals or barrier semaphores. Data moves between devices by JAX's collectives and lax.ppermute only.
A program may use at most 64 MiB of HBM per device.

v0:
```python
import jax
import jax.numpy as jnp
from jax import lax
from jax.sharding import PartitionSpec as P


def local(x_block, tiles, coords, counts):
    vector_count = x_block.shape[0]
    rows_dev = x_block.shape[1]
    tile_size = tiles.shape[1]
    slot_total = tiles.shape[0]
    row_tiles = rows_dev * lax.axis_size("col") // tile_size
    gathered = lax.all_gather(x_block, "row", axis=1, tiled=True)
    picked = jnp.take(gathered.reshape(vector_count, -1, tile_size), coords[:, 1], axis=1)
    live_slots = jnp.arange(slot_total, dtype=jnp.int32) < counts[0]
    onehot = (
        (coords[:, 0][None, :] == jnp.arange(row_tiles, dtype=jnp.int32)[:, None])
        & live_slots[None, :]
    ).astype(jnp.float32)
    contrib = jnp.einsum("ckj,kij->kci", picked, tiles, preferred_element_type=jnp.float32)
    summed = jnp.einsum("rk,kci->cri", onehot, contrib, precision=lax.Precision.HIGHEST)
    partial_rows = summed.reshape(vector_count, row_tiles * tile_size)
    rows_piece = lax.psum_scatter(partial_rows, "col", scatter_dimension=1, tiled=True)
    total_rows = rows_dev * lax.axis_size("row") * lax.axis_size("col")
    gram_local = (
        jnp.dot(
            rows_piece,
            rows_piece.T,
            precision=lax.Precision.HIGHEST,
            preferred_element_type=jnp.float32,
        )
        / total_rows
    )
    lower_factor = jnp.linalg.cholesky(lax.psum(gram_local, ("row", "col")))
    basis = jax.scipy.linalg.solve_triangular(lower_factor, rows_piece, lower=True)
    return (basis, lower_factor.T)


def solution(mesh):
    placed = (
        P(None, ("col", "row")),
        P(("row", "col"), None, None),
        P(("row", "col"), None),
        P(("row", "col")),
    )
    return jax.shard_map(
        local, mesh=mesh, in_specs=placed, out_specs=(P(None, ("row", "col")), P()), check_vma=False
    )
```

profile of v0, /device:TPU:0, one launch (start us, length us, event | category | flops | bytes accessed | tf_op | source)
XLA Modules:
  0.0 118.1 jit_solution(4191894164312084905)
XLA Ops:
  7.2 0.0 copy-start
  7.2 0.0 reduce-scatter.2.cloned.1.call-start
  7.2 0.9 slice_bitcast_fusion
  8.1 0.8 and_bitcast_fusion
  8.8 10.6 %all_gather.3 = bf16[64,1024]{1,0:T(8,128)(2,1)S(1)} all-gather(bf16[64,256]{1,0:T(8,128)(2,1)} %param.4), channel_id=1, replica_groups=mesh['row'=4,'col'=8] {'row'}, dimensions={1}, use_global_device_ids=true | all-gather | bytes 163840 | tf_op jit(solution)/shard_map/all_gather | solution.py:13
  20.2 1.5 %gather_fusion = bf16[24,64,256]{2,1,0:T(8,128)(2,1)} fusion(bf16[64,4,256]{2,0,1:T(8,128)(2,1)S(1)} %bitcast.36, s32[1024]{0:T(1024)S(1)} %pad_clamp_fusion), kind=kCustom, calls=%fused_computation | custom fusion | bytes 1572960 | tf_op jit(solution)/shard_map/jit(_take)/gather | solution.py:14
  21.7 0.0 copy-done
  21.7 2.2 %fusion.2 = f32[24,64,256]{2,1,0:T(8,128)S(1)} fusion(bf16[24,256,256]{2,1,0:T(8,128)(2,1)S(1)} %copy-done, bf16[24,64,256]{2,1,0:T(8,128)(2,1)} %gather_fusion, pred[24]{0:T(512)(128)(4,1)S(1)} %and_bitcast_fusion), kind=kOutput, calls=%fused_computation.4 | convolution fusion | flops 201719808 | bytes 5505048 | tf_op jit(solution)/shard_map/ckj,kij->kci/dot_general | solution.py:20
  23.9 1.5 %fusion = f32[64,256,8]{1,2,0:T(8,128)S(1)} fusion(f32[24,64,256]{2,1,0:T(8,128)S(1)} %fusion.2, s32[24]{0:T(128)S(1)} %get-tuple-element.10, pred[24]{0:T(512)(128)(4,1)S(1)} %iota_compare_fusion.3), kind=kOutput, calls=%fused_computation.1 | convolution fusion | flops 37749120 | bytes 2097272 | tf_op jit(solution)/shard_map/rk,kci->cri/dot_general | solution.py:21
  25.4 1.0 copy.19
  26.3 0.0 reduce-scatter.2.cloned.1.call-update
  26.3 31.2 %reduce-scatter.2.cloned.1.call-done = f32[64,256]{1,0:T(8,128)} async-done(((f32[64,2048]{1,0:T(8,128)}), f32[64,256]{1,0:T(8,128)}) %reduce-scatter.2.cloned.1.call-update) | async-done | bytes 65552 | tf_op jit(solution)/shard_map/reduce_scatter | solution.py:23
  57.5 1.1 convolution_multiply_fusion
  58.6 38.0 %psum.7 = f32[64,64]{0,1:T(8,128)S(1)} all-reduce(f32[64,64]{0,1:T(8,128)S(1)} %convolution_multiply_fusion), channel_id=1, replica_groups=mesh['row'=4,'col'=8] {'row','col'}, use_global_device_ids=true, to_apply=%region_1.2 | all-reduce | flops 4096 | bytes 32768 | tf_op jit(solution)/shard_map/psum | solution.py:34
  96.6 0.1 copy.15
  96.7 5.8 %cholesky.16 = f32[64,64]{1,0:T(8,128)S(1)} custom-call(f32[64,64]{1,0:T(8,128)S(1)} %fusion.9), custom_call_target="Cholesky" | custom-call | tf_op jit(solution)/shard_map/jit(cholesky)/cholesky | solution.py:34
  102.6 0.6 compare_reduce_fusion
  103.2 0.7 fusion.10
  103.9 4.9 %custom-call.7 = f32[1,64,64]{1,2,0:T(8,128)S(1)} custom-call(f32[1,64,64]{2,1,0:T(8,128)S(1)} %get-tuple-element.9), custom_call_target="InvertDiagBlocksLowerTriangular" | custom-call | tf_op jit(solution)/shard_map/jit(_solve_triangular)/triangular_solve | solution.py:35
  108.8 0.7 copy.16
  109.5 1.7 %fusion.7 = f32[64,256]{1,0:T(8,128)} fusion(f32[64,256]{1,0:T(8,128)} %reduce-scatter.2.cloned.1.call-done, f32[1,64,64]{1,2,0:T(8,128)S(1)} %custom-call.7), kind=kOutput, calls=%fused_computation.10 | convolution fusion | flops 12582912 | bytes 147456 | tf_op jit(solution)/shard_map/jit(_solve_triangular)/triangular_solve | solution.py:35
  (5 shorter events, 0.1 us)
Async XLA Ops:
  7.2 14.5 %copy-start = (bf16[24,256,256]{2,1,0:T(8,128)(2,1)S(1)}, bf16[24,256,256]{2,1,0:T(8,128)(2,1)}, u32[]{:S(2)}) copy-start(bf16[24,256,256]{2,1,0:T(8,128)(2,1)} %param.5) | copy-start | bytes 9437188
  7.2 50.3 %reduce-scatter.2.cloned.1.call-start = ((), (), s32[]{:S(2)}) async-start(), calls=%async_computation.1 | async-start | bytes 589824 | tf_op jit(solution)/shard_map/reduce_scatter | solution.py:23
Sparse Core Ops, SparseCore 0:
  26.5 31.0 reduce-scatter.1
where the time goes:
time: 119 us; the launch traced here: 118 us
  blocking collectives  48.6 us (41%)
  waiting for transfers between devices  31.2 us (26%)
  between operations  14.7 us (12%)
  other arithmetic  13.7 us (12%)
  matrix products  6.54 us (5%)
  local copies, waits for them, and re-layouts  3.26 us (3%)
    psum x1, blocking collectives, local(): lower_factor = jnp.linalg.cholesky(lax.psum(gram_local, ('row', 'col')))  38 us
    reduce_scatter x1, waiting for transfers between devices, local(): lax.psum_scatter(partial_rows, 'col', scatter_dimension=1, tiled=True)  31.2 us
    all_gather x1, blocking collectives, local(): gathered = lax.all_gather(x_block, 'row', axis=1, tiled=True)  10.6 us
    another operation x3, other arithmetic, local(): lower_factor = jnp.linalg.cholesky(lax.psum(gram_local, ('row', 'col')))  6.52 us
    another operation x1, other arithmetic, local(): jax.scipy.linalg.solve_triangular(lower_factor, rows_piece, lower=True)  4.9 us
  transfers between devices with their start and end apart: 1, of which 1 were waited for; matrix products, arithmetic and copies ran while one was open for 0% of the time, Pallas kernels for 0%

commit v1 on v0

v1 whole, which is shorter than its diff:
```python
import functools

import jax
import jax.numpy as jnp
from jax import lax
from jax.experimental import pallas as pl
from jax.experimental.pallas import tpu as pltpu
from jax.sharding import PartitionSpec as P

F32 = jnp.float32
VMEM = pl.BlockSpec(memory_space=pltpu.VMEM)
SMEM = pl.BlockSpec(memory_space=pltpu.SMEM)
EXACT = lax.Precision.HIGHEST
PANEL = 8


def swap(x, axis, bits):
    return lax.ppermute(x, axis, [(i, i ^ bits) for i in range(lax.axis_size(axis))])


def total(x, axis, low):
    size = lax.axis_size(axis)
    while low < size:
        masks = [low, 2 * low, 3 * low] if 2 * low < size else [low]
        parts = [swap(x, axis, mask) for mask in reversed(masks)]
        x = functools.reduce(jnp.add, parts, x)
        low *= 4
    return x


def product_kernel(blocks, select, tiles, *refs):
    pieces, (keep, send, x_all, rows) = refs[:blocks], refs[blocks:]
    for k in range(blocks):
        x_all[k] = pieces[k][...]
    rows[...] = jnp.zeros_like(rows)
    for s in range(tiles.shape[0]):
        rows[select[1, s]] += lax.dot_general(
            x_all[select[0, s]], tiles[s], (((1,), (1,)), ((), ())), preferred_element_type=F32
        )
    half = keep.shape[0]
    keep[...] = rows[:half]
    send[...] = rows[half : 2 * half]


def gram_kernel(scale, *refs):
    parts, (y_out, gram_out) = refs[:-2], refs[-2:]
    y = functools.reduce(jnp.add, [part[...] for part in parts])
    y_out[...] = y
    gram_out[...] = scale * lax.dot_general(
        y, y, (((1,), (1,)), ((), ())), precision=EXACT, preferred_element_type=F32
    )


def factor_kernel(y_ref, *refs):
    grams, (basis, factor) = refs[:-2], refs[-2:]
    gram = functools.reduce(jnp.add, [g[...] for g in grams])
    order = gram.shape[0]
    width = y_ref.shape[1]
    rest = jnp.concatenate([y_ref[...], gram], axis=1)
    lanes = 128
    sub = lax.broadcasted_iota(jnp.int32, (PANEL, 1), 0)
    col = lax.broadcasted_iota(jnp.int32, (PANEL, order), 1)
    for p in range(0, order, PANEL):
        live = order - p
        columns = [
            jnp.broadcast_to(rest[:, width + p + m : width + p + m + 1], (live, lanes))
            for m in range(PANEL)
        ]
        top = rest[:PANEL]
        lower = []
        done = jnp.zeros_like(top)
        for m in range(PANEL):
            inverse = lax.rsqrt(columns[m][m : m + 1])
            low = columns[m] * inverse
            lower.append(low)
            for n in range(m + 1, PANEL):
                columns[n] = columns[n] - low * low[n : n + 1]
            wide = inverse[:, :1]
            row = top[m : m + 1] * wide
            done = jnp.where(sub == m, row, done)
            if m + 1 < PANEL:
                top = top - low[:PANEL, :1] * row
        basis[p : p + PANEL, :] = done[:, :width]
        factor[p : p + PANEL, :] = jnp.where(col >= sub + p, done[:, width:], 0.0)
        if live > PANEL:
            rest = rest[PANEL:]
            for m in range(PANEL):
                rest = rest - lower[m][PANEL:, :1] * done[m : m + 1]


def local(x_block, tiles, coords, counts):
    vectors, width = x_block.shape
    slots = tiles.shape[0]
    n_row, n_col = lax.axis_size("row"), lax.axis_size("col")
    chips = n_col // 2
    me_row, me_col = lax.axis_index("row"), lax.axis_index("col")

    pieces = [x_block] + [swap(x_block, "row", k) for k in range(n_row - 1, 0, -1)][::-1]
    place = coords[:, 0] ^ me_col
    live = jnp.arange(slots, dtype=jnp.int32) < counts[0]
    place = jnp.where(live, (place & 1) * chips + (place >> 1), n_col)
    select = jnp.stack([coords[:, 1] ^ me_row, place])
    part = jax.ShapeDtypeStruct((chips, vectors, width), F32)
    keep, send = pl.pallas_call(
        functools.partial(product_kernel, n_row),
        out_shape=(part, part),
        in_specs=[SMEM] + [VMEM] * (1 + n_row),
        out_specs=(VMEM, VMEM),
        scratch_shapes=[
            pltpu.VMEM((n_row, vectors, width), x_block.dtype),
            pltpu.VMEM((n_col + 1, vectors, width), F32),
        ],
        name="product",
    )(select, tiles, *pieces)

    chip = keep + swap(send, "col", 1)
    parts = [chip[0]] + [swap(chip[k], "col", 2 * k) for k in range(chips - 1, 0, -1)]
    y, gram = pl.pallas_call(
        functools.partial(gram_kernel, 1.0 / (width * n_row * n_col)),
        out_shape=(
            jax.ShapeDtypeStruct((vectors, width), F32),
            jax.ShapeDtypeStruct((vectors, vectors), F32),
        ),
        in_specs=[VMEM] * chips,
        out_specs=(VMEM, VMEM),
        name="gram",
    )(*parts)
    gram = gram + swap(gram, "col", 1)
    gram = total(gram, "row", 1)
    gram = total(gram, "col", 2)
    return pl.pallas_call(
        factor_kernel,
        out_shape=(
            jax.ShapeDtypeStruct((vectors, width), F32),
            jax.ShapeDtypeStruct((vectors, vectors), F32),
        ),
        in_specs=[VMEM, VMEM],
        out_specs=(VMEM, VMEM),
        name="factor",
    )(y, gram)


def solution(mesh):
    placed = (
        P(None, ("col", "row")),
        P(("row", "col"), None, None),
        P(("row", "col"), None),
        P(("row", "col")),
    )
    return jax.shard_map(
        local, mesh=mesh, in_specs=placed, out_specs=(P(None, ("row", "col")), P()), check_vma=False
    )
```

time: 119 us -> 51.8 us (0.44)
  blocking collectives: 48.6 us -> 0 us
  starting transfers between devices: 0.04 us -> 16.9 us
  between operations: 14.7 us -> 1.31 us
  waiting for transfers between devices: 31.2 us -> 18.4 us
  other arithmetic: 13.7 us -> 4.35 us
  Pallas kernels: 0 us -> 8.65 us
  matrix products: 6.54 us -> 0 us
  local copies, waits for them, and re-layouts: 3.26 us -> 1.9 us
    psum x1 -> x0, blocking collectives: 38 us -> none  [local(): lower_factor = jnp.linalg.cholesky(lax.psum(gram_local, ('row', 'col')))]
    reduce_scatter x1 -> x0, waiting for transfers between devices: 31.2 us -> none  [local(): lax.psum_scatter(partial_rows, 'col', scatter_dimension=1, tiled=True)]
    ppermute x0 -> x14, waiting for transfers between devices: none -> 18.4 us  [swap(): lax.ppermute(x, axis, [(i, i ^ bits) for i in range(lax.axis_size(axis))])]
    ppermute x0 -> x14, starting transfers between devices: none -> 16.9 us  [swap(): lax.ppermute(x, axis, [(i, i ^ bits) for i in range(lax.axis_size(axis))])]
    another operation x4 -> x1, other arithmetic: 11.4 us -> 0.59 us  [local(): select = jnp.stack([coords[:, 1] ^ me_row, place])]
    all_gather x1 -> x0, blocking collectives: 10.6 us -> none  [local(): gathered = lax.all_gather(x_block, 'row', axis=1, tiled=True)]
    pallas_call x0 -> x3, Pallas kernels: none -> 8.65 us  [the longest x1 3.85 us: local(): pl.pallas_call(functools.partial(product_kernel, n_row), out_shape=(part,...]
    dot_general x3 -> x0, matrix products: 4.82 us -> none  [the longest x1 2.21 us: local(): jnp.einsum('ckj,kij->kci', picked, tiles, preferred_element_type=jnp.floa...]
  transfers between devices with their start and end apart: 1 -> 14, of which waited for: 1 -> 11; matrix products, arithmetic and copies ran while one was open for 0% -> 4% of each run, Pallas kernels for 0% -> 0%
where the time goes in v1:
time: 51.8 us; the launch traced here: 51.5 us
  waiting for transfers between devices  18.4 us (36%)
  starting transfers between devices  16.9 us (33%)
  Pallas kernels  8.65 us (17%)
  other arithmetic  4.35 us (8%)
  local copies, waits for them, and re-layouts  1.9 us (4%)
  between operations  1.31 us (3%)
    ppermute x14, waiting for transfers between devices, swap(): lax.ppermute(x, axis, [(i, i ^ bits) for i in range(lax.axis_size(axis))])  18.4 us
    ppermute x14, starting transfers between devices, swap(): lax.ppermute(x, axis, [(i, i ^ bits) for i in range(lax.axis_size(axis))])  16.9 us
    pallas_call x1, Pallas kernels, local(): pl.pallas_call(functools.partial(product_kernel, n_row), out_shape=(part,...  3.85 us
    pallas_call x1, Pallas kernels, local(): pl.pallas_call(factor_kernel, out_shape=(jax.ShapeDtypeStruct((vectors, w...  3.04 us
    pallas_call x1, Pallas kernels, local(): pl.pallas_call(functools.partial(gram_kernel, 1.0 / (width * n_row * n_co...  1.76 us
    unnamed x12, local copies, waits for them, and re-layouts  1.25 us
  transfers between devices with their start and end apart: 14, of which 11 were waited for; matrix products, arithmetic and copies ran while one was open for 4% of the time, Pallas kernels for 0%

profile of v1, /device:TPU:0, one launch (start us, length us, event | category | flops | bytes accessed | tf_op | source)
XLA Modules:
  0.0 51.5 jit_solution(5062208365558855539)
XLA Ops:
  0.6 3.0 %collective-permute-start.1 = (bf16[64,256]{1,0:T(8,128)(2,1)}, bf16[64,256]{1,0:T(8,128)(2,1)S(1)}, u32[]{:S(2)}, u32[]{:S(2)}) collective-permute-start(bf16[64,256]{1,0:T(8,128)(2,1)} %refs_0_.1), channel_id=1, source_target_pairs={{0,16},{8,24},{16,0},{24,8},{1,17},{9,25},{17,1},{25,9},{2,18},{10... | collective-permute-start | bytes 98312 | tf_op jit(solution)/shard_map/ppermute | solution.py:18
  3.7 1.5 %collective-permute-start = (bf16[64,256]{1,0:T(8,128)(2,1)}, bf16[64,256]{1,0:T(8,128)(2,1)S(1)}, u32[]{:S(2)}, u32[]{:S(2)}) collective-permute-start(bf16[64,256]{1,0:T(8,128)(2,1)} %refs_0_.1), channel_id=1, source_target_pairs={{0,8},{8,0},{16,24},{24,16},{1,9},{9,1},{17,25},{25,17},{2,10},{10... | collective-permute-start | bytes 98312 | tf_op jit(solution)/shard_map/ppermute | solution.py:18
  5.9 0.7 %xor_bitcast_fusion = s32[1,24]{1,0:T(1,128)S(1)} fusion(s32[24,2]{0,1:T(2,128)} %param.6, s32[]{:T(128)S(6)} %axis_index.23), kind=kLoop, calls=%fused_computation.8 | loop fusion | flops 24 | bytes 196 | tf_op jit(solution)/shard_map/xor | solution.py:102
  6.5 0.7 %compare_select_fusion = s32[1,24]{1,0:T(1,128)S(1)} fusion(s32[24,2]{0,1:T(2,128)} %param.6, s32[]{:T(128)S(6)} %axis_index.25, s32[]{:T(128)} %bitcast.13), kind=kLoop, calls=%fused_computation.6 | loop fusion | flops 168 | bytes 200 | tf_op jit(solution)/shard_map/jit(_where)/select_n | solution.py:101
  7.2 0.6 %pad_add_fusion.select = s32[2,24]{1,0:T(2,128)} fusion(s32[1,24]{1,0:T(1,128)S(1)} %compare_select_fusion, s32[1,24]{1,0:T(1,128)S(1)} %xor_bitcast_fusion), kind=kLoop, calls=%fused_computation.7 | loop fusion | flops 48 | bytes 384 | tf_op jit(solution)/shard_map/stack | solution.py:102
  7.9 2.3 %collective-permute-done.2.refs_3_ = bf16[64,256]{1,0:T(8,128)(2,1)S(1)} collective-permute-done((bf16[64,256]{1,0:T(8,128)(2,1)}, bf16[64,256]{1,0:T(8,128)(2,1)S(1)}, u32[]{:S(2)}, u32[]{:S(2)}) %collective-permute-start.2) | collective-permute-done | bytes 32800 | tf_op jit(solution)/shard_map/ppermute | solution.py:18
  10.2 0.6 %copy-done.5 = bf16[64,256]{1,0:T(8,128)(2,1)} copy-done((bf16[64,256]{1,0:T(8,128)(2,1)}, bf16[64,256]{1,0:T(8,128)(2,1)S(1)}, u32[]{:S(2)}) %copy-start.5) | copy-done | bytes 32792
  10.8 3.9 %product.1 = (f32[4,64,256]{2,1,0:T(8,128)}, f32[4,64,256]{2,1,0:T(8,128)}) custom-call(s32[2,24]{1,0:T(2,128)} %pad_add_fusion.select, bf16[24,256,256]{2,1,0:T(8,128)(2,1)} %tiles.1, bf16[64,256]{1,0:T(8,128)(2,1)} %refs_0_.1, bf16[64,256]{1,0:T(8,128)(2,1)} %copy-done.4, bf16[64,256]{1,0:T(8,128)(2,1)} %copy-done.3, bf16[64,256]{1,0:T(8,128)(2,1)} %copy-done.5), custom_call_target="tpu_custom_call" | custom-call | tf_op jit(solution)/shard_map/product/pallas_call | solution.py:104
  14.6 1.7 %collective-permute-done.3 = f32[4,64,256]{2,1,0:T(8,128)S(1)} collective-permute-done((f32[4,64,256]{2,1,0:T(8,128)}, f32[4,64,256]{2,1,0:T(8,128)S(1)}, u32[]{:S(2)}, u32[]{:S(2)}) %collective-permute-start.3) | collective-permute-done | bytes 262176 | tf_op jit(solution)/shard_map/ppermute | solution.py:18
  16.4 1.0 %add.39 = f32[4,64,256]{2,1,0:T(8,128)S(1)} add(f32[4,64,256]{2,1,0:T(8,128)} %get-tuple-element.6, f32[4,64,256]{2,1,0:T(8,128)S(1)} %collective-permute-done.3) | non-fusion elementwise | flops 65536 | bytes 786432 | tf_op jit(solution)/shard_map/add | solution.py:116
  17.4 0.6 %slice_bitcast_fusion = (f32[64,256]{1,0:T(8,128)S(1)}, f32[64,256]{1,0:T(8,128)S(1)}, f32[64,256]{1,0:T(8,128)S(1)}, f32[64,256]{1,0:T(8,128)}) fusion(f32[4,64,256]{2,1,0:T(8,128)S(1)} %add.39), kind=kLoop, calls=%fused_computation | loop fusion | bytes 524288 | tf_op jit(solution)/shard_map/squeeze | solution.py:117
  18.0 1.6 %collective-permute-start.6 = (f32[64,256]{1,0:T(8,128)S(1)}, f32[64,256]{1,0:T(8,128)S(1)}, u32[]{:S(2)}, u32[]{:S(2)}) collective-permute-start(f32[64,256]{1,0:T(8,128)S(1)} %get-tuple-element.10), channel_id=1, source_target_pairs={{0,2},{1,3},{2,0},{3,1},{4,6},{5,7},{6,4},{7,5},{8,10},{9,11},{10,... | collective-permute-start | bytes 196616 | tf_op jit(solution)/shard_map/ppermute | solution.py:18
  19.6 2.6 %collective-permute-start.5 = (f32[64,256]{1,0:T(8,128)S(1)}, f32[64,256]{1,0:T(8,128)S(1)}, u32[]{:S(2)}, u32[]{:S(2)}) collective-permute-start(f32[64,256]{1,0:T(8,128)S(1)} %get-tuple-element.11), channel_id=1, source_target_pairs={{0,4},{1,5},{2,6},{3,7},{4,0},{5,1},{6,2},{7,3},{8,12},{9,13},{10,... | collective-permute-start | bytes 196616 | tf_op jit(solution)/shard_map/ppermute | solution.py:18
  22.4 4.7 %collective-permute-done.5.refs_2_ = f32[64,256]{1,0:T(8,128)S(1)} collective-permute-done((f32[64,256]{1,0:T(8,128)S(1)}, f32[64,256]{1,0:T(8,128)S(1)}, u32[]{:S(2)}, u32[]{:S(2)}) %collective-permute-start.5) | collective-permute-done | bytes 65568 | tf_op jit(solution)/shard_map/ppermute | solution.py:18
  27.1 1.2 %collective-permute-done.4.refs_1_ = f32[64,256]{1,0:T(8,128)S(1)} collective-permute-done((f32[64,256]{1,0:T(8,128)S(1)}, f32[64,256]{1,0:T(8,128)S(1)}, u32[]{:S(2)}, u32[]{:S(2)}) %collective-permute-start.4) | collective-permute-done | bytes 65568 | tf_op jit(solution)/shard_map/ppermute | solution.py:18
  28.4 0.6 %copy-done.2 = f32[64,256]{1,0:T(8,128)} copy-done((f32[64,256]{1,0:T(8,128)}, f32[64,256]{1,0:T(8,128)S(1)}, u32[]{:S(2)}) %copy-start.2) | copy-done | bytes 65560
  29.0 1.8 %gram.1 = (f32[64,256]{1,0:T(8,128)}, f32[64,64]{1,0:T(8,128)}) custom-call(f32[64,256]{1,0:T(8,128)} %get-tuple-element.13.refs_0_, f32[64,256]{1,0:T(8,128)} %copy-done.2, f32[64,256]{1,0:T(8,128)} %copy-done.1, f32[64,256]{1,0:T(8,128)} %copy-done), custom_call_target="tpu_custom_call" | custom-call | tf_op jit(solution)/shard_map/gram/pallas_call | solution.py:118
  30.8 1.4 %collective-permute-done.7 = f32[64,64]{1,0:T(8,128)S(1)} collective-permute-done((f32[64,64]{1,0:T(8,128)}, f32[64,64]{1,0:T(8,128)S(1)}, u32[]{:S(2)}, u32[]{:S(2)}) %collective-permute-start.7) | collective-permute-done | bytes 16416 | tf_op jit(solution)/shard_map/ppermute | solution.py:18
  32.2 0.8 %add.40 = f32[64,64]{1,0:T(8,128)S(1)} add(f32[64,64]{1,0:T(8,128)} %get-tuple-element.9, f32[64,64]{1,0:T(8,128)S(1)} %collective-permute-done.7) | non-fusion elementwise | flops 4096 | bytes 49152 | tf_op jit(solution)/shard_map/add | solution.py:128
  32.9 0.5 %collective-permute-start.10 = (f32[64,64]{1,0:T(8,128)S(1)}, f32[64,64]{1,0:T(8,128)S(1)}, u32[]{:S(2)}, u32[]{:S(2)}) collective-permute-start(f32[64,64]{1,0:T(8,128)S(1)} %add.40), channel_id=1, source_target_pairs={{0,8},{8,0},{16,24},{24,16},{1,9},{9,1},{17,25},{25,17},{2,10},{10... | collective-permute-start | bytes 49160 | tf_op jit(solution)/shard_map/ppermute | solution.py:18
  33.5 1.2 %collective-permute-start.9 = (f32[64,64]{1,0:T(8,128)S(1)}, f32[64,64]{1,0:T(8,128)S(1)}, u32[]{:S(2)}, u32[]{:S(2)}) collective-permute-start(f32[64,64]{1,0:T(8,128)S(1)} %add.40), channel_id=1, source_target_pairs={{0,16},{8,24},{16,0},{24,8},{1,17},{9,25},{17,1},{25,9},{2,18},{10... | collective-permute-start | bytes 49160 | tf_op jit(solution)/shard_map/ppermute | solution.py:18
  34.6 1.8 %collective-permute-start.8 = (f32[64,64]{1,0:T(8,128)S(1)}, f32[64,64]{1,0:T(8,128)S(1)}, u32[]{:S(2)}, u32[]{:S(2)}) collective-permute-start(f32[64,64]{1,0:T(8,128)S(1)} %add.40), channel_id=1, source_target_pairs={{0,24},{8,16},{16,8},{24,0},{1,25},{9,17},{17,9},{25,1},{2,26},{10... | collective-permute-start | bytes 49160 | tf_op jit(solution)/shard_map/ppermute | solution.py:18
  36.4 0.4 collective-permute-done.10
  36.9 0.5 %collective-permute-done.9 = f32[64,64]{1,0:T(8,128)S(1)} collective-permute-done((f32[64,64]{1,0:T(8,128)S(1)}, f32[64,64]{1,0:T(8,128)S(1)}, u32[]{:S(2)}, u32[]{:S(2)}) %collective-permute-start.9) | collective-permute-done | bytes 16416 | tf_op jit(solution)/shard_map/ppermute | solution.py:18
  37.4 2.1 %collective-permute-done.8 = f32[64,64]{1,0:T(8,128)S(1)} collective-permute-done((f32[64,64]{1,0:T(8,128)S(1)}, f32[64,64]{1,0:T(8,128)S(1)}, u32[]{:S(2)}, u32[]{:S(2)}) %collective-permute-start.8) | collective-permute-done | bytes 16416 | tf_op jit(solution)/shard_map/ppermute | solution.py:18
  39.5 0.9 %collective-permute-start.13 = (f32[64,64]{1,0:T(8,128)S(1)}, f32[64,64]{1,0:T(8,128)S(1)}, u32[]{:S(2)}, u32[]{:S(2)}) collective-permute-start(f32[64,64]{1,0:T(8,128)S(1)} %add_add_fusion.1), channel_id=1, source_target_pairs={{0,2},{1,3},{2,0},{3,1},{4,6},{5,7},{6,4},{7,5},{8,10},{9,11},{10,... | collective-permute-start | bytes 49160 | tf_op jit(solution)/shard_map/ppermute | solution.py:18
  40.4 1.7 %collective-permute-start.12 = (f32[64,64]{1,0:T(8,128)S(1)}, f32[64,64]{1,0:T(8,128)S(1)}, u32[]{:S(2)}, u32[]{:S(2)}) collective-permute-start(f32[64,64]{1,0:T(8,128)S(1)} %add_add_fusion.1), channel_id=1, source_target_pairs={{0,4},{1,5},{2,6},{3,7},{4,0},{5,1},{6,2},{7,3},{8,12},{9,13},{10,... | collective-permute-start | bytes 49160 | tf_op jit(solution)/shard_map/ppermute | solution.py:18
  42.1 1.8 %collective-permute-start.11 = (f32[64,64]{1,0:T(8,128)S(1)}, f32[64,64]{1,0:T(8,128)S(1)}, u32[]{:S(2)}, u32[]{:S(2)}) collective-permute-start(f32[64,64]{1,0:T(8,128)S(1)} %add_add_fusion.1), channel_id=1, source_target_pairs={{0,6},{1,7},{2,4},{3,5},{4,2},{5,3},{6,0},{7,1},{8,14},{9,15},{10,... | collective-permute-start | bytes 49160 | tf_op jit(solution)/shard_map/ppermute | solution.py:18
  43.9 1.4 %collective-permute-done.12 = f32[64,64]{1,0:T(8,128)S(1)} collective-permute-done((f32[64,64]{1,0:T(8,128)S(1)}, f32[64,64]{1,0:T(8,128)S(1)}, u32[]{:S(2)}, u32[]{:S(2)}) %collective-permute-start.12) | collective-permute-done | bytes 16416 | tf_op jit(solution)/shard_map/ppermute | solution.py:18
  45.3 2.5 %collective-permute-done.11 = f32[64,64]{1,0:T(8,128)S(1)} collective-permute-done((f32[64,64]{1,0:T(8,128)S(1)}, f32[64,64]{1,0:T(8,128)S(1)}, u32[]{:S(2)}, u32[]{:S(2)}) %collective-permute-start.11) | collective-permute-done | bytes 16416 | tf_op jit(solution)/shard_map/ppermute | solution.py:18
  47.8 0.6 %add_add_fusion.refs_0_ = f32[64,64]{1,0:T(8,128)} fusion(f32[64,64]{1,0:T(8,128)S(1)} %collective-permute-done.13, f32[64,64]{1,0:T(8,128)S(1)} %collective-permute-done.12, f32[64,64]{1,0:T(8,128)S(1)} %add_add_fusion.1, f32[64,64]{1,0:T(8,128)S(1)} %collective-permute-done.11), kind=kLoop, calls=%fused_computation.4 | loop fusion | flops 12288 | bytes 81920 | tf_op jit(solution)/shard_map/add | solution.py:26
  48.4 3.0 %factor.1 = (f32[64,256]{1,0:T(8,128)}, f32[64,64]{1,0:T(8,128)}) custom-call(f32[64,256]{1,0:T(8,128)} %get-tuple-element.8.y_ref, f32[64,64]{1,0:T(8,128)} %add_add_fusion.refs_0_), custom_call_target="tpu_custom_call" | custom-call | tf_op jit(solution)/shard_map/factor/pallas_call | solution.py:131
  (19 shorter events, 0.4 us)
Async XLA Ops:
  0.6 7.2 %collective-permute-start.1 = (bf16[64,256]{1,0:T(8,128)(2,1)}, bf16[64,256]{1,0:T(8,128)(2,1)S(1)}, u32[]{:S(2)}, u32[]{:S(2)}) collective-permute-start(bf16[64,256]{1,0:T(8,128)(2,1)} %refs_0_.1), channel_id=1, source_target_pairs={{0,16},{8,24},{16,0},{24,8},{1,17},{9,25},{17,1},{25,9},{2,18},{10... | collective-permute-start | bytes 98312 | tf_op jit(solution)/shard_map/ppermute | solution.py:18
  3.7 4.2 %collective-permute-start = (bf16[64,256]{1,0:T(8,128)(2,1)}, bf16[64,256]{1,0:T(8,128)(2,1)S(1)}, u32[]{:S(2)}, u32[]{:S(2)}) collective-permute-start(bf16[64,256]{1,0:T(8,128)(2,1)} %refs_0_.1), channel_id=1, source_target_pairs={{0,8},{8,0},{16,24},{24,16},{1,9},{9,1},{17,25},{25,17},{2,10},{10... | collective-permute-start | bytes 98312 | tf_op jit(solution)/shard_map/ppermute | solution.py:18
  5.2 5.0 %collective-permute-start.2 = (bf16[64,256]{1,0:T(8,128)(2,1)}, bf16[64,256]{1,0:T(8,128)(2,1)S(1)}, u32[]{:S(2)}, u32[]{:S(2)}) collective-permute-start(bf16[64,256]{1,0:T(8,128)(2,1)} %refs_0_.1), channel_id=1, source_target_pairs={{0,24},{8,16},{16,8},{24,0},{1,25},{9,17},{17,9},{25,1},{2,26},{10... | collective-permute-start | bytes 98312 | tf_op jit(solution)/shard_map/ppermute | solution.py:18
  7.8 2.4 %copy-start.3 = (bf16[64,256]{1,0:T(8,128)(2,1)}, bf16[64,256]{1,0:T(8,128)(2,1)S(1)}, u32[]{:S(2)}) copy-start(bf16[64,256]{1,0:T(8,128)(2,1)S(1)} %collective-permute-done.1.refs_2_) | copy-start | bytes 98308
  7.9 2.3 %copy-start.4 = (bf16[64,256]{1,0:T(8,128)(2,1)}, bf16[64,256]{1,0:T(8,128)(2,1)S(1)}, u32[]{:S(2)}) copy-start(bf16[64,256]{1,0:T(8,128)(2,1)S(1)} %collective-permute-done.refs_1_) | copy-start | bytes 98308
  10.2 0.6 %copy-start.5 = (bf16[64,256]{1,0:T(8,128)(2,1)}, bf16[64,256]{1,0:T(8,128)(2,1)S(1)}, u32[]{:S(2)}) copy-start(bf16[64,256]{1,0:T(8,128)(2,1)S(1)} %collective-permute-done.2.refs_3_) | copy-start | bytes 98308
  14.6 1.7 %collective-permute-start.3 = (f32[4,64,256]{2,1,0:T(8,128)}, f32[4,64,256]{2,1,0:T(8,128)S(1)}, u32[]{:S(2)}, u32[]{:S(2)}) collective-permute-start(f32[4,64,256]{2,1,0:T(8,128)} %get-tuple-element.7), channel_id=1, source_target_pairs={{0,1},{1,0},{2,3},{3,2},{4,5},{5,4},{6,7},{7,6},{8,9},{9,8},{10,11... | collective-permute-start | bytes 786440 | tf_op jit(solution)/shard_map/ppermute | solution.py:18
  18.0 4.4 %collective-permute-start.6 = (f32[64,256]{1,0:T(8,128)S(1)}, f32[64,256]{1,0:T(8,128)S(1)}, u32[]{:S(2)}, u32[]{:S(2)}) collective-permute-start(f32[64,256]{1,0:T(8,128)S(1)} %get-tuple-element.10), channel_id=1, source_target_pairs={{0,2},{1,3},{2,0},{3,1},{4,6},{5,7},{6,4},{7,5},{8,10},{9,11},{10,... | collective-permute-start | bytes 196616 | tf_op jit(solution)/shard_map/ppermute | solution.py:18
  19.6 7.5 %collective-permute-start.5 = (f32[64,256]{1,0:T(8,128)S(1)}, f32[64,256]{1,0:T(8,128)S(1)}, u32[]{:S(2)}, u32[]{:S(2)}) collective-permute-start(f32[64,256]{1,0:T(8,128)S(1)} %get-tuple-element.11), channel_id=1, source_target_pairs={{0,4},{1,5},{2,6},{3,7},{4,0},{5,1},{6,2},{7,3},{8,12},{9,13},{10,... | collective-permute-start | bytes 196616 | tf_op jit(solution)/shard_map/ppermute | solution.py:18
  22.2 6.2 %collective-permute-start.4 = (f32[64,256]{1,0:T(8,128)S(1)}, f32[64,256]{1,0:T(8,128)S(1)}, u32[]{:S(2)}, u32[]{:S(2)}) collective-permute-start(f32[64,256]{1,0:T(8,128)S(1)} %get-tuple-element.12), channel_id=1, source_target_pairs={{0,6},{1,7},{2,4},{3,5},{4,2},{5,3},{6,0},{7,1},{8,14},{9,15},{10,... | collective-permute-start | bytes 196616 | tf_op jit(solution)/shard_map/ppermute | solution.py:18
  22.4 5.9 %copy-start = (f32[64,256]{1,0:T(8,128)}, f32[64,256]{1,0:T(8,128)S(1)}, u32[]{:S(2)}) copy-start(f32[64,256]{1,0:T(8,128)S(1)} %collective-permute-done.6.refs_3_) | copy-start | bytes 196612
  27.1 1.2 %copy-start.1 = (f32[64,256]{1,0:T(8,128)}, f32[64,256]{1,0:T(8,128)S(1)}, u32[]{:S(2)}) copy-start(f32[64,256]{1,0:T(8,128)S(1)} %collective-permute-done.5.refs_2_) | copy-start | bytes 196612
  28.4 0.6 %copy-start.2 = (f32[64,256]{1,0:T(8,128)}, f32[64,256]{1,0:T(8,128)S(1)}, u32[]{:S(2)}) copy-start(f32[64,256]{1,0:T(8,128)S(1)} %collective-permute-done.4.refs_1_) | copy-start | bytes 196612
  30.8 1.4 %collective-permute-start.7 = (f32[64,64]{1,0:T(8,128)}, f32[64,64]{1,0:T(8,128)S(1)}, u32[]{:S(2)}, u32[]{:S(2)}) collective-permute-start(f32[64,64]{1,0:T(8,128)} %get-tuple-element.9), channel_id=1, source_target_pairs={{0,1},{1,0},{2,3},{3,2},{4,5},{5,4},{6,7},{7,6},{8,9},{9,8},{10,11... | collective-permute-start | bytes 49160 | tf_op jit(solution)/shard_map/ppermute | solution.py:18
  32.9 3.9 %collective-permute-start.10 = (f32[64,64]{1,0:T(8,128)S(1)}, f32[64,64]{1,0:T(8,128)S(1)}, u32[]{:S(2)}, u32[]{:S(2)}) collective-permute-start(f32[64,64]{1,0:T(8,128)S(1)} %add.40), channel_id=1, source_target_pairs={{0,8},{8,0},{16,24},{24,16},{1,9},{9,1},{17,25},{25,17},{2,10},{10... | collective-permute-start | bytes 49160 | tf_op jit(solution)/shard_map/ppermute | solution.py:18
  33.5 3.9 %collective-permute-start.9 = (f32[64,64]{1,0:T(8,128)S(1)}, f32[64,64]{1,0:T(8,128)S(1)}, u32[]{:S(2)}, u32[]{:S(2)}) collective-permute-start(f32[64,64]{1,0:T(8,128)S(1)} %add.40), channel_id=1, source_target_pairs={{0,16},{8,24},{16,0},{24,8},{1,17},{9,25},{17,1},{25,9},{2,18},{10... | collective-permute-start | bytes 49160 | tf_op jit(solution)/shard_map/ppermute | solution.py:18
  34.6 4.8 %collective-permute-start.8 = (f32[64,64]{1,0:T(8,128)S(1)}, f32[64,64]{1,0:T(8,128)S(1)}, u32[]{:S(2)}, u32[]{:S(2)}) collective-permute-start(f32[64,64]{1,0:T(8,128)S(1)} %add.40), channel_id=1, source_target_pairs={{0,24},{8,16},{16,8},{24,0},{1,25},{9,17},{17,9},{25,1},{2,26},{10... | collective-permute-start | bytes 49160 | tf_op jit(solution)/shard_map/ppermute | solution.py:18
  39.5 4.5 %collective-permute-start.13 = (f32[64,64]{1,0:T(8,128)S(1)}, f32[64,64]{1,0:T(8,128)S(1)}, u32[]{:S(2)}, u32[]{:S(2)}) collective-permute-start(f32[64,64]{1,0:T(8,128)S(1)} %add_add_fusion.1), channel_id=1, source_target_pairs={{0,2},{1,3},{2,0},{3,1},{4,6},{5,7},{6,4},{7,5},{8,10},{9,11},{10,... | collective-permute-start | bytes 49160 | tf_op jit(solution)/shard_map/ppermute | solution.py:18
  40.4 4.9 %collective-permute-start.12 = (f32[64,64]{1,0:T(8,128)S(1)}, f32[64,64]{1,0:T(8,128)S(1)}, u32[]{:S(2)}, u32[]{:S(2)}) collective-permute-start(f32[64,64]{1,0:T(8,128)S(1)} %add_add_fusion.1), channel_id=1, source_target_pairs={{0,4},{1,5},{2,6},{3,7},{4,0},{5,1},{6,2},{7,3},{8,12},{9,13},{10,... | collective-permute-start | bytes 49160 | tf_op jit(solution)/shard_map/ppermute | solution.py:18
  42.1 5.7 %collective-permute-start.11 = (f32[64,64]{1,0:T(8,128)S(1)}, f32[64,64]{1,0:T(8,128)S(1)}, u32[]{:S(2)}, u32[]{:S(2)}) collective-permute-start(f32[64,64]{1,0:T(8,128)S(1)} %add_add_fusion.1), channel_id=1, source_target_pairs={{0,6},{1,7},{2,4},{3,5},{4,2},{5,3},{6,0},{7,1},{8,14},{9,15},{10,... | collective-permute-start | bytes 49160 | tf_op jit(solution)/shard_map/ppermute | solution.py:18

commit v2 on v1

--- a/solution.py
+++ b/solution.py
@@ -11,7 +11,7 @@
 VMEM = pl.BlockSpec(memory_space=pltpu.VMEM)
 SMEM = pl.BlockSpec(memory_space=pltpu.SMEM)
 EXACT = lax.Precision.HIGHEST
-PANEL = 8
+PANEL = 16
 
 
 def swap(x, axis, bits):
@@ -22,20 +22,30 @@
     size = lax.axis_size(axis)
     while low < size:
         masks = [low, 2 * low, 3 * low] if 2 * low < size else [low]
-        parts = [swap(x, axis, mask) for mask in reversed(masks)]
+        parts = [swap(x, axis, mask) for mask in masks]
         x = functools.reduce(jnp.add, parts, x)
         low *= 4
     return x
 
 
-def product_kernel(blocks, select, tiles, *refs):
-    pieces, (keep, send, x_all, rows) = refs[:blocks], refs[blocks:]
-    for k in range(blocks):
-        x_all[k] = pieces[k][...]
+def select_kernel(coords, select):
+    me_row, me_col = lax.axis_index("row"), lax.axis_index("col")
+    n_col = lax.axis_size("col")
+    apart = coords[0:1, :] ^ me_col
+    place = (apart & 1) * (n_col // 2) + (apart >> 1)
+    select[0:1, :] = place
+    select[1:2, :] = coords[1:2, :] ^ me_row
+
+
+def product_kernel(order, select, counts, tiles, *refs):
+    pieces, (keep, send, x_all, rows) = refs[: len(order)], refs[len(order) :]
+    for k, piece in zip(order, pieces):
+        x_all[k] = piece[...]
     rows[...] = jnp.zeros_like(rows)
     for s in range(tiles.shape[0]):
-        rows[select[1, s]] += lax.dot_general(
-            x_all[select[0, s]], tiles[s], (((1,), (1,)), ((), ())), preferred_element_type=F32
+        place = jnp.where(s < counts[0], select[0, s], rows.shape[0] - 1)
+        rows[place] += lax.dot_general(
+            x_all[select[1, s]], tiles[s], (((1,), (1,)), ((), ())), preferred_element_type=F32
         )
     half = keep.shape[0]
     keep[...] = rows[:half]
@@ -46,15 +56,22 @@
     parts, (y_out, gram_out) = refs[:-2], refs[-2:]
     y = functools.reduce(jnp.add, [part[...] for part in parts])
     y_out[...] = y
-    gram_out[...] = scale * lax.dot_general(
-        y, y, (((1,), (1,)), ((), ())), precision=EXACT, preferred_element_type=F32
-    )
+    half = y.shape[0] // 2
+    for k in range(2):
+        gram_out[:, k * 2 * half : (k + 1) * 2 * half] = scale * lax.dot_general(
+            y[k * half : (k + 1) * half],
+            y,
+            (((1,), (1,)), ((), ())),
+            precision=EXACT,
+            preferred_element_type=F32,
+        )
 
 
 def factor_kernel(y_ref, *refs):
     grams, (basis, factor) = refs[:-2], refs[-2:]
     gram = functools.reduce(jnp.add, [g[...] for g in grams])
-    order = gram.shape[0]
+    order = y_ref.shape[0]
+    gram = jnp.concatenate([gram[:, :order], gram[:, order:]], axis=0)
     width = y_ref.shape[1]
     rest = jnp.concatenate([y_ref[...], gram], axis=1)
     lanes = 128
@@ -90,39 +107,46 @@
 
 def local(x_block, tiles, coords, counts):
     vectors, width = x_block.shape
-    slots = tiles.shape[0]
     n_row, n_col = lax.axis_size("row"), lax.axis_size("col")
     chips = n_col // 2
-    me_row, me_col = lax.axis_index("row"), lax.axis_index("col")
 
-    pieces = [x_block] + [swap(x_block, "row", k) for k in range(n_row - 1, 0, -1)][::-1]
-    place = coords[:, 0] ^ me_col
-    live = jnp.arange(slots, dtype=jnp.int32) < counts[0]
-    place = jnp.where(live, (place & 1) * chips + (place >> 1), n_col)
-    select = jnp.stack([coords[:, 1] ^ me_row, place])
+    order = (*range(2, n_row), 1)
+    pieces = [swap(x_block, "row", k) for k in order]
+    select = pl.pallas_call(
+        select_kernel,
+        out_shape=jax.ShapeDtypeStruct(coords.shape[::-1], jnp.int32),
+        in_specs=[VMEM],
+        out_specs=VMEM,
+        compiler_params=pltpu.CompilerParams(vmem_limit_bytes=1 << 20),
+        cost_estimate=pl.CostEstimate(flops=4 * 10**9, bytes_accessed=0, transcendentals=0),
+        name="select",
+    )(coords.T)
+    select, counts = lax.optimization_barrier((select, counts))
     part = jax.ShapeDtypeStruct((chips, vectors, width), F32)
     keep, send = pl.pallas_call(
-        functools.partial(product_kernel, n_row),
+        functools.partial(product_kernel, (0, *order)),
         out_shape=(part, part),
-        in_specs=[SMEM] + [VMEM] * (1 + n_row),
+        in_specs=[SMEM, SMEM] + [VMEM] * (1 + n_row),
         out_specs=(VMEM, VMEM),
         scratch_shapes=[
             pltpu.VMEM((n_row, vectors, width), x_block.dtype),
             pltpu.VMEM((n_col + 1, vectors, width), F32),
         ],
+        compiler_params=pltpu.CompilerParams(vmem_limit_bytes=12 << 20),
         name="product",
-    )(select, tiles, *pieces)
+    )(select, counts, tiles, x_block, *pieces)
 
     chip = keep + swap(send, "col", 1)
-    parts = [chip[0]] + [swap(chip[k], "col", 2 * k) for k in range(chips - 1, 0, -1)]
+    parts = [chip[0]] + [swap(chip[k], "col", 2 * k) for k in (1, *range(chips - 1, 1, -1))]
     y, gram = pl.pallas_call(
         functools.partial(gram_kernel, 1.0 / (width * n_row * n_col)),
         out_shape=(
             jax.ShapeDtypeStruct((vectors, width), F32),
-            jax.ShapeDtypeStruct((vectors, vectors), F32),
+            jax.ShapeDtypeStruct((vectors // 2, 2 * vectors), F32),
         ),
         in_specs=[VMEM] * chips,
         out_specs=(VMEM, VMEM),
+        compiler_params=pltpu.CompilerParams(vmem_limit_bytes=4 << 20),
         name="gram",
     )(*parts)
     gram = gram + swap(gram, "col", 1)
@@ -136,6 +160,7 @@
         ),
         in_specs=[VMEM, VMEM],
         out_specs=(VMEM, VMEM),
+        compiler_params=pltpu.CompilerParams(vmem_limit_bytes=4 << 20),
         name="factor",
     )(y, gram)
 

time: 51.8 us -> 39.2 us (0.76)
  Pallas kernels: 8.65 us -> 3.97 us
  other arithmetic: 4.35 us -> 0.05 us
  waiting for transfers between devices: 18.4 us -> 16 us
  local copies, waits for them, and re-layouts: 1.9 us -> 0.71 us
    ppermute x14, waiting for transfers between devices: 18.4 us -> 16 us  [swap(): lax.ppermute(x, axis, [(i, i ^ bits) for i in range(lax.axis_size(axis))])]
    pallas_call x1 -> x2, Pallas kernels: 3.85 us -> 1.67 us  [the longest x1 1.67 us: local(): pl.pallas_call(functools.partial(product_kernel, (0, *order)), out_shape=...]
    pallas_call x1, Pallas kernels: 1.76 us -> 0.29 us  [local(): pl.pallas_call(functools.partial(gram_kernel, 1.0 / (width * n_row * n_co...]
    pallas_call x1, Pallas kernels: 3.04 us -> 2 us  [local(): pl.pallas_call(factor_kernel, out_shape=(jax.ShapeDtypeStruct((vectors, w...]
    add x1, other arithmetic: 0.99 us -> 0.03 us  [local(): chip = keep + swap(send, 'col', 1)]
    add x1, other arithmetic: 0.77 us -> 0.01 us  [local(): gram = gram + swap(gram, 'col', 1)]
    xor x1 -> x0, other arithmetic: 0.69 us -> none  [local(): select = jnp.stack([coords[:, 1] ^ me_row, place])]
    select_n x1 -> x0, other arithmetic: 0.68 us -> none  [local(): place = jnp.where(live, (place & 1) * chips + (place >> 1), n_col)]
  transfers between devices with their start and end apart: 14 -> 14, of which waited for: 11 -> 12; matrix products, arithmetic and copies ran while one was open for 4% -> 0% of each run, Pallas kernels for 0% -> 0%
where the time goes in v2:
time: 39.2 us; the launch traced here: 39 us
  starting transfers between devices  16.8 us (43%)
  waiting for transfers between devices  16 us (41%)
  Pallas kernels  3.97 us (10%)
  between operations  1.5 us (4%)
  local copies, waits for them, and re-layouts  0.71 us (2%)
    ppermute x14, starting transfers between devices, swap(): lax.ppermute(x, axis, [(i, i ^ bits) for i in range(lax.axis_size(axis))])  16.8 us
    ppermute x14, waiting for transfers between devices, swap(): lax.ppermute(x, axis, [(i, i ^ bits) for i in range(lax.axis_size(axis))])  16 us
    pallas_call x1, Pallas kernels, local(): pl.pallas_call(factor_kernel, out_shape=(jax.ShapeDtypeStruct((vectors, w...  2 us
    pallas_call x1, Pallas kernels, local(): pl.pallas_call(functools.partial(product_kernel, (0, *order)), out_shape=...  1.67 us
  transfers between devices with their start and end apart: 14, of which 12 were waited for; matrix products, arithmetic and copies ran while one was open for 0% of the time, Pallas kernels for 0%

profile of v2, /device:TPU:0, one launch (start us, length us, event | category | flops | bytes accessed | tf_op | source)
XLA Modules:
  0.0 39.0 jit_solution(16143869548079111256)
XLA Ops:
  0.6 4.0 %collective-permute-start.1 = (bf16[64,256]{1,0:T(8,128)(2,1)}, bf16[64,256]{1,0:T(8,128)(2,1)S(1)}, u32[]{:S(2)}, u32[]{:S(2)}) collective-permute-start(bf16[64,256]{1,0:T(8,128)(2,1)} %refs_0_.1), channel_id=1, source_target_pairs={{0,24},{8,16},{16,8},{24,0},{1,25},{9,17},{17,9},{25,1},{2,26},{10... | collective-permute-start | bytes 98312 | tf_op jit(solution)/shard_map/ppermute | solution.py:18
  4.6 0.5 %collective-permute-start = (bf16[64,256]{1,0:T(8,128)(2,1)}, bf16[64,256]{1,0:T(8,128)(2,1)S(1)}, u32[]{:S(2)}, u32[]{:S(2)}) collective-permute-start(bf16[64,256]{1,0:T(8,128)(2,1)} %refs_0_.1), channel_id=1, source_target_pairs={{0,16},{8,24},{16,0},{24,8},{1,17},{9,25},{17,1},{25,9},{2,18},{10... | collective-permute-start | bytes 98312 | tf_op jit(solution)/shard_map/ppermute | solution.py:18
  5.1 0.1 collective-permute-start.2
  5.2 0.7 %copy-done.2 = s32[24,2]{0,1:T(2,128)S(1)} copy-done((s32[24,2]{0,1:T(2,128)S(1)}, s32[24,2]{0,1:T(2,128)}, u32[]{:S(2)}) %copy-start.2) | copy-done | bytes 216
  6.7 0.0 collective-permute-done.1.refs_2_
  6.7 2.0 %collective-permute-done.refs_1_ = bf16[64,256]{1,0:T(8,128)(2,1)S(1)} collective-permute-done((bf16[64,256]{1,0:T(8,128)(2,1)}, bf16[64,256]{1,0:T(8,128)(2,1)S(1)}, u32[]{:S(2)}, u32[]{:S(2)}) %collective-permute-start) | collective-permute-done | bytes 32800 | tf_op jit(solution)/shard_map/ppermute | solution.py:18
  8.7 0.5 %collective-permute-done.2.refs_3_ = bf16[64,256]{1,0:T(8,128)(2,1)S(1)} collective-permute-done((bf16[64,256]{1,0:T(8,128)(2,1)}, bf16[64,256]{1,0:T(8,128)(2,1)S(1)}, u32[]{:S(2)}, u32[]{:S(2)}) %collective-permute-start.2) | collective-permute-done | bytes 32800 | tf_op jit(solution)/shard_map/ppermute | solution.py:18
  9.2 1.7 %product.1 = (f32[4,64,256]{2,1,0:T(8,128)S(1)}, f32[4,64,256]{2,1,0:T(8,128)S(1)}) custom-call(s32[2,24]{1,0:T(2,128)S(1)} %select.1, s32[1]{0:T(128)S(6)} %copy.6.counts, bf16[24,256,256]{2,1,0:T(8,128)(2,1)S(1)} %copy-done, bf16[64,256]{1,0:T(8,128)(2,1)S(1)} %copy-done.1, bf16[64,256]{1,0:T(8,128)(2,1)S(1)} %collective-permute-done.refs_1_, ...), custom_call_target="tpu_custom_call" | custom-call | tf_op jit(solution)/shard_map/product/pallas_call | solution.py:126
  10.9 0.1 collective-permute-start.3
  11.0 1.5 %collective-permute-done.3 = f32[4,64,256]{2,1,0:T(8,128)S(1)} collective-permute-done((f32[4,64,256]{2,1,0:T(8,128)S(1)}, f32[4,64,256]{2,1,0:T(8,128)S(1)}, u32[]{:S(2)}, u32[]{:S(2)}) %collective-permute-start.3) | collective-permute-done | bytes 262176 | tf_op jit(solution)/shard_map/ppermute | solution.py:18
  12.6 2.7 %collective-permute-start.6 = (f32[64,256]{1,0:T(8,128)S(1)}, f32[64,256]{1,0:T(8,128)S(1)}, u32[]{:S(2)}, u32[]{:S(2)}) collective-permute-start(f32[64,256]{1,0:T(8,128)S(1)} %get-tuple-element.14), channel_id=1, source_target_pairs={{0,4},{1,5},{2,6},{3,7},{4,0},{5,1},{6,2},{7,3},{8,12},{9,13},{10,... | collective-permute-start | bytes 196616 | tf_op jit(solution)/shard_map/ppermute | solution.py:18
  15.2 1.3 %collective-permute-start.5 = (f32[64,256]{1,0:T(8,128)S(1)}, f32[64,256]{1,0:T(8,128)S(1)}, u32[]{:S(2)}, u32[]{:S(2)}) collective-permute-start(f32[64,256]{1,0:T(8,128)S(1)} %get-tuple-element.15), channel_id=1, source_target_pairs={{0,6},{1,7},{2,4},{3,5},{4,2},{5,3},{6,0},{7,1},{8,14},{9,15},{10,... | collective-permute-start | bytes 196616 | tf_op jit(solution)/shard_map/ppermute | solution.py:18
  16.6 0.2 collective-permute-start.4
  16.8 3.5 %collective-permute-done.6.refs_3_ = f32[64,256]{1,0:T(8,128)S(1)} collective-permute-done((f32[64,256]{1,0:T(8,128)S(1)}, f32[64,256]{1,0:T(8,128)S(1)}, u32[]{:S(2)}, u32[]{:S(2)}) %collective-permute-start.6) | collective-permute-done | bytes 65568 | tf_op jit(solution)/shard_map/ppermute | solution.py:18
  20.3 1.3 %collective-permute-done.5.refs_2_ = f32[64,256]{1,0:T(8,128)S(1)} collective-permute-done((f32[64,256]{1,0:T(8,128)S(1)}, f32[64,256]{1,0:T(8,128)S(1)}, u32[]{:S(2)}, u32[]{:S(2)}) %collective-permute-start.5) | collective-permute-done | bytes 65568 | tf_op jit(solution)/shard_map/ppermute | solution.py:18
  21.6 0.3 collective-permute-done.4.refs_1_
  22.0 0.3 gram.1
  22.3 0.0 collective-permute-start.7
  22.3 1.2 %collective-permute-done.7 = f32[32,128]{1,0:T(8,128)S(1)} collective-permute-done((f32[32,128]{1,0:T(8,128)S(1)}, f32[32,128]{1,0:T(8,128)S(1)}, u32[]{:S(2)}, u32[]{:S(2)}) %collective-permute-start.7) | collective-permute-done | bytes 16416 | tf_op jit(solution)/shard_map/ppermute | solution.py:18
  23.5 1.5 %collective-permute-start.10 = (f32[32,128]{1,0:T(8,128)S(1)}, f32[32,128]{1,0:T(8,128)S(1)}, u32[]{:S(2)}, u32[]{:S(2)}) collective-permute-start(f32[32,128]{1,0:T(8,128)S(1)} %add.25), channel_id=1, source_target_pairs={{0,24},{8,16},{16,8},{24,0},{1,25},{9,17},{17,9},{25,1},{2,26},{10... | collective-permute-start | bytes 49160 | tf_op jit(solution)/shard_map/ppermute | solution.py:18
  25.0 0.5 %collective-permute-start.9 = (f32[32,128]{1,0:T(8,128)S(1)}, f32[32,128]{1,0:T(8,128)S(1)}, u32[]{:S(2)}, u32[]{:S(2)}) collective-permute-start(f32[32,128]{1,0:T(8,128)S(1)} %add.25), channel_id=1, source_target_pairs={{0,16},{8,24},{16,0},{24,8},{1,17},{9,25},{17,1},{25,9},{2,18},{10... | collective-permute-start | bytes 49160 | tf_op jit(solution)/shard_map/ppermute | solution.py:18
  25.4 1.5 %collective-permute-start.8 = (f32[32,128]{1,0:T(8,128)S(1)}, f32[32,128]{1,0:T(8,128)S(1)}, u32[]{:S(2)}, u32[]{:S(2)}) collective-permute-start(f32[32,128]{1,0:T(8,128)S(1)} %add.25), channel_id=1, source_target_pairs={{0,8},{8,0},{16,24},{24,16},{1,9},{9,1},{17,25},{25,17},{2,10},{10... | collective-permute-start | bytes 49160 | tf_op jit(solution)/shard_map/ppermute | solution.py:18
  27.0 1.1 %collective-permute-done.10 = f32[32,128]{1,0:T(8,128)S(1)} collective-permute-done((f32[32,128]{1,0:T(8,128)S(1)}, f32[32,128]{1,0:T(8,128)S(1)}, u32[]{:S(2)}, u32[]{:S(2)}) %collective-permute-start.10) | collective-permute-done | bytes 16416 | tf_op jit(solution)/shard_map/ppermute | solution.py:18
  28.1 0.6 %collective-permute-done.9 = f32[32,128]{1,0:T(8,128)S(1)} collective-permute-done((f32[32,128]{1,0:T(8,128)S(1)}, f32[32,128]{1,0:T(8,128)S(1)}, u32[]{:S(2)}, u32[]{:S(2)}) %collective-permute-start.9) | collective-permute-done | bytes 16416 | tf_op jit(solution)/shard_map/ppermute | solution.py:18
  28.7 0.5 %collective-permute-done.8 = f32[32,128]{1,0:T(8,128)S(1)} collective-permute-done((f32[32,128]{1,0:T(8,128)S(1)}, f32[32,128]{1,0:T(8,128)S(1)}, u32[]{:S(2)}, u32[]{:S(2)}) %collective-permute-start.8) | collective-permute-done | bytes 16416 | tf_op jit(solution)/shard_map/ppermute | solution.py:18
  29.2 3.2 %collective-permute-start.13 = (f32[32,128]{1,0:T(8,128)S(1)}, f32[32,128]{1,0:T(8,128)S(1)}, u32[]{:S(2)}, u32[]{:S(2)}) collective-permute-start(f32[32,128]{1,0:T(8,128)S(1)} %add_add_fusion.1), channel_id=1, source_target_pairs={{0,6},{1,7},{2,4},{3,5},{4,2},{5,3},{6,0},{7,1},{8,14},{9,15},{10,... | collective-permute-start | bytes 49160 | tf_op jit(solution)/shard_map/ppermute | solution.py:18
  32.4 0.0 collective-permute-start.12
  32.4 1.2 %collective-permute-start.11 = (f32[32,128]{1,0:T(8,128)S(1)}, f32[32,128]{1,0:T(8,128)S(1)}, u32[]{:S(2)}, u32[]{:S(2)}) collective-permute-start(f32[32,128]{1,0:T(8,128)S(1)} %add_add_fusion.1), channel_id=1, source_target_pairs={{0,2},{1,3},{2,0},{3,1},{4,6},{5,7},{6,4},{7,5},{8,10},{9,11},{10,... | collective-permute-start | bytes 49160 | tf_op jit(solution)/shard_map/ppermute | solution.py:18
  33.6 1.1 %collective-permute-done.13 = f32[32,128]{1,0:T(8,128)S(1)} collective-permute-done((f32[32,128]{1,0:T(8,128)S(1)}, f32[32,128]{1,0:T(8,128)S(1)}, u32[]{:S(2)}, u32[]{:S(2)}) %collective-permute-start.13) | collective-permute-done | bytes 16416 | tf_op jit(solution)/shard_map/ppermute | solution.py:18
  34.7 2.3 %collective-permute-done.12 = f32[32,128]{1,0:T(8,128)S(1)} collective-permute-done((f32[32,128]{1,0:T(8,128)S(1)}, f32[32,128]{1,0:T(8,128)S(1)}, u32[]{:S(2)}, u32[]{:S(2)}) %collective-permute-start.12) | collective-permute-done | bytes 16416 | tf_op jit(solution)/shard_map/ppermute | solution.py:18
  37.0 0.0 collective-permute-done.11
  37.0 2.0 %factor.1 = (f32[64,256]{1,0:T(8,128)}, f32[64,64]{1,0:T(8,128)}) custom-call(f32[64,256]{1,0:T(8,128)S(1)} %get-tuple-element.12.y_ref, f32[32,128]{1,0:T(8,128)S(1)} %add_add_fusion.refs_0_), custom_call_target="tpu_custom_call" | custom-call | tf_op jit(solution)/shard_map/factor/pallas_call | solution.py:155
  (11 shorter events, 0.1 us)
Async XLA Ops:
  0.6 6.1 %collective-permute-start.1 = (bf16[64,256]{1,0:T(8,128)(2,1)}, bf16[64,256]{1,0:T(8,128)(2,1)S(1)}, u32[]{:S(2)}, u32[]{:S(2)}) collective-permute-start(bf16[64,256]{1,0:T(8,128)(2,1)} %refs_0_.1), channel_id=1, source_target_pairs={{0,24},{8,16},{16,8},{24,0},{1,25},{9,17},{17,9},{25,1},{2,26},{10... | collective-permute-start | bytes 98312 | tf_op jit(solution)/shard_map/ppermute | solution.py:18
  4.6 4.1 %collective-permute-start = (bf16[64,256]{1,0:T(8,128)(2,1)}, bf16[64,256]{1,0:T(8,128)(2,1)S(1)}, u32[]{:S(2)}, u32[]{:S(2)}) collective-permute-start(bf16[64,256]{1,0:T(8,128)(2,1)} %refs_0_.1), channel_id=1, source_target_pairs={{0,16},{8,24},{16,0},{24,8},{1,17},{9,25},{17,1},{25,9},{2,18},{10... | collective-permute-start | bytes 98312 | tf_op jit(solution)/shard_map/ppermute | solution.py:18
  5.1 4.1 %collective-permute-start.2 = (bf16[64,256]{1,0:T(8,128)(2,1)}, bf16[64,256]{1,0:T(8,128)(2,1)S(1)}, u32[]{:S(2)}, u32[]{:S(2)}) collective-permute-start(bf16[64,256]{1,0:T(8,128)(2,1)} %refs_0_.1), channel_id=1, source_target_pairs={{0,8},{8,0},{16,24},{24,16},{1,9},{9,1},{17,25},{25,17},{2,10},{10... | collective-permute-start | bytes 98312 | tf_op jit(solution)/shard_map/ppermute | solution.py:18
  5.2 0.7 %copy-start.2 = (s32[24,2]{0,1:T(2,128)S(1)}, s32[24,2]{0,1:T(2,128)}, u32[]{:S(2)}) copy-start(s32[24,2]{0,1:T(2,128)} %param.6) | copy-start | bytes 580
  5.9 3.3 %copy-start = (bf16[24,256,256]{2,1,0:T(8,128)(2,1)S(1)}, bf16[24,256,256]{2,1,0:T(8,128)(2,1)}, u32[]{:S(2)}) copy-start(bf16[24,256,256]{2,1,0:T(8,128)(2,1)} %tiles.1) | copy-start | bytes 9437188
  5.9 3.3 %copy-start.1 = (bf16[64,256]{1,0:T(8,128)(2,1)S(1)}, bf16[64,256]{1,0:T(8,128)(2,1)}, u32[]{:S(2)}) copy-start(bf16[64,256]{1,0:T(8,128)(2,1)} %refs_0_.1) | copy-start | bytes 98308
  10.9 1.6 %collective-permute-start.3 = (f32[4,64,256]{2,1,0:T(8,128)S(1)}, f32[4,64,256]{2,1,0:T(8,128)S(1)}, u32[]{:S(2)}, u32[]{:S(2)}) collective-permute-start(f32[4,64,256]{2,1,0:T(8,128)S(1)} %get-tuple-element.11), channel_id=1, source_target_pairs={{0,1},{1,0},{2,3},{3,2},{4,5},{5,4},{6,7},{7,6},{8,9},{9,8},{10,11... | collective-permute-start | bytes 786440 | tf_op jit(solution)/shard_map/ppermute | solution.py:18
  12.6 7.8 %collective-permute-start.6 = (f32[64,256]{1,0:T(8,128)S(1)}, f32[64,256]{1,0:T(8,128)S(1)}, u32[]{:S(2)}, u32[]{:S(2)}) collective-permute-start(f32[64,256]{1,0:T(8,128)S(1)} %get-tuple-element.14), channel_id=1, source_target_pairs={{0,4},{1,5},{2,6},{3,7},{4,0},{5,1},{6,2},{7,3},{8,12},{9,13},{10,... | collective-permute-start | bytes 196616 | tf_op jit(solution)/shard_map/ppermute | solution.py:18
  15.2 6.4 %collective-permute-start.5 = (f32[64,256]{1,0:T(8,128)S(1)}, f32[64,256]{1,0:T(8,128)S(1)}, u32[]{:S(2)}, u32[]{:S(2)}) collective-permute-start(f32[64,256]{1,0:T(8,128)S(1)} %get-tuple-element.15), channel_id=1, source_target_pairs={{0,6},{1,7},{2,4},{3,5},{4,2},{5,3},{6,0},{7,1},{8,14},{9,15},{10,... | collective-permute-start | bytes 196616 | tf_op jit(solution)/shard_map/ppermute | solution.py:18
  16.6 5.4 %collective-permute-start.4 = (f32[64,256]{1,0:T(8,128)S(1)}, f32[64,256]{1,0:T(8,128)S(1)}, u32[]{:S(2)}, u32[]{:S(2)}) collective-permute-start(f32[64,256]{1,0:T(8,128)S(1)} %get-tuple-element.16), channel_id=1, source_target_pairs={{0,2},{1,3},{2,0},{3,1},{4,6},{5,7},{6,4},{7,5},{8,10},{9,11},{10,... | collective-permute-start | bytes 196616 | tf_op jit(solution)/shard_map/ppermute | solution.py:18
  22.3 1.2 %collective-permute-start.7 = (f32[32,128]{1,0:T(8,128)S(1)}, f32[32,128]{1,0:T(8,128)S(1)}, u32[]{:S(2)}, u32[]{:S(2)}) collective-permute-start(f32[32,128]{1,0:T(8,128)S(1)} %get-tuple-element.13), channel_id=1, source_target_pairs={{0,1},{1,0},{2,3},{3,2},{4,5},{5,4},{6,7},{7,6},{8,9},{9,8},{10,11... | collective-permute-start | bytes 49160 | tf_op jit(solution)/shard_map/ppermute | solution.py:18
  23.5 4.6 %collective-permute-start.10 = (f32[32,128]{1,0:T(8,128)S(1)}, f32[32,128]{1,0:T(8,128)S(1)}, u32[]{:S(2)}, u32[]{:S(2)}) collective-permute-start(f32[32,128]{1,0:T(8,128)S(1)} %add.25), channel_id=1, source_target_pairs={{0,24},{8,16},{16,8},{24,0},{1,25},{9,17},{17,9},{25,1},{2,26},{10... | collective-permute-start | bytes 49160 | tf_op jit(solution)/shard_map/ppermute | solution.py:18
  25.0 3.7 %collective-permute-start.9 = (f32[32,128]{1,0:T(8,128)S(1)}, f32[32,128]{1,0:T(8,128)S(1)}, u32[]{:S(2)}, u32[]{:S(2)}) collective-permute-start(f32[32,128]{1,0:T(8,128)S(1)} %add.25), channel_id=1, source_target_pairs={{0,16},{8,24},{16,0},{24,8},{1,17},{9,25},{17,1},{25,9},{2,18},{10... | collective-permute-start | bytes 49160 | tf_op jit(solution)/shard_map/ppermute | solution.py:18
  25.4 3.7 %collective-permute-start.8 = (f32[32,128]{1,0:T(8,128)S(1)}, f32[32,128]{1,0:T(8,128)S(1)}, u32[]{:S(2)}, u32[]{:S(2)}) collective-permute-start(f32[32,128]{1,0:T(8,128)S(1)} %add.25), channel_id=1, source_target_pairs={{0,8},{8,0},{16,24},{24,16},{1,9},{9,1},{17,25},{25,17},{2,10},{10... | collective-permute-start | bytes 49160 | tf_op jit(solution)/shard_map/ppermute | solution.py:18
  29.2 5.5 %collective-permute-start.13 = (f32[32,128]{1,0:T(8,128)S(1)}, f32[32,128]{1,0:T(8,128)S(1)}, u32[]{:S(2)}, u32[]{:S(2)}) collective-permute-start(f32[32,128]{1,0:T(8,128)S(1)} %add_add_fusion.1), channel_id=1, source_target_pairs={{0,6},{1,7},{2,4},{3,5},{4,2},{5,3},{6,0},{7,1},{8,14},{9,15},{10,... | collective-permute-start | bytes 49160 | tf_op jit(solution)/shard_map/ppermute | solution.py:18
  32.4 4.6 %collective-permute-start.12 = (f32[32,128]{1,0:T(8,128)S(1)}, f32[32,128]{1,0:T(8,128)S(1)}, u32[]{:S(2)}, u32[]{:S(2)}) collective-permute-start(f32[32,128]{1,0:T(8,128)S(1)} %add_add_fusion.1), channel_id=1, source_target_pairs={{0,4},{1,5},{2,6},{3,7},{4,0},{5,1},{6,2},{7,3},{8,12},{9,13},{10,... | collective-permute-start | bytes 49160 | tf_op jit(solution)/shard_map/ppermute | solution.py:18
  32.4 4.6 %collective-permute-start.11 = (f32[32,128]{1,0:T(8,128)S(1)}, f32[32,128]{1,0:T(8,128)S(1)}, u32[]{:S(2)}, u32[]{:S(2)}) collective-permute-start(f32[32,128]{1,0:T(8,128)S(1)} %add_add_fusion.1), channel_id=1, source_target_pairs={{0,2},{1,3},{2,0},{3,1},{4,6},{5,7},{6,4},{7,5},{8,10},{9,11},{10,... | collective-permute-start | bytes 49160 | tf_op jit(solution)/shard_map/ppermute | solution.py:18

commit v3 on v2

--- a/solution.py
+++ b/solution.py
@@ -14,21 +14,27 @@
 PANEL = 16
 
 
-def swap(x, axis, bits):
-    return lax.ppermute(x, axis, [(i, i ^ bits) for i in range(lax.axis_size(axis))])
+def swap(x, row, col):
+    n_row, n_col = lax.axis_size("row"), lax.axis_size("col")
+    pairs = [
+        (i * n_col + j, (i ^ row) * n_col + (j ^ col)) for i in range(n_row) for j in range(n_col)
+    ]
+    return lax.ppermute(x, ("row", "col"), pairs)
 
 
-def total(x, axis, low):
-    size = lax.axis_size(axis)
+def rounds(axis):
+    size, low = lax.axis_size(axis), 1 if axis == "row" else 2
     while low < size:
         masks = [low, 2 * low, 3 * low] if 2 * low < size else [low]
-        parts = [swap(x, axis, mask) for mask in masks]
-        x = functools.reduce(jnp.add, parts, x)
+        yield [(0, mask | 1) if axis == "col" else (mask, 1) for mask in masks]
         low *= 4
-    return x
 
 
-def select_kernel(coords, select):
+def mark_kernel(out):
+    out[...] = jnp.zeros_like(out)
+
+
+def select_kernel(coords, mark, select):
     me_row, me_col = lax.axis_index("row"), lax.axis_index("col")
     n_col = lax.axis_size("col")
     apart = coords[0:1, :] ^ me_col
@@ -110,17 +116,25 @@
     n_row, n_col = lax.axis_size("row"), lax.axis_size("col")
     chips = n_col // 2
 
-    order = (*range(2, n_row), 1)
-    pieces = [swap(x_block, "row", k) for k in order]
+    order = sorted(range(1, n_row), key=lambda k: (k != 3, k))
+    mate = swap(x_block, 0, 1)
+    pieces = [swap(mate, k, 1) if k == 1 else swap(x_block, k, 0) for k in order]
+    mark = pl.pallas_call(
+        mark_kernel,
+        out_shape=jax.ShapeDtypeStruct((8, 128), F32),
+        out_specs=VMEM,
+        compiler_params=pltpu.CompilerParams(vmem_limit_bytes=1 << 20),
+        cost_estimate=pl.CostEstimate(flops=4 * 10**9, bytes_accessed=0, transcendentals=0),
+        name="mark",
+    )()
     select = pl.pallas_call(
         select_kernel,
         out_shape=jax.ShapeDtypeStruct(coords.shape[::-1], jnp.int32),
-        in_specs=[VMEM],
+        in_specs=[VMEM, VMEM],
         out_specs=VMEM,
         compiler_params=pltpu.CompilerParams(vmem_limit_bytes=1 << 20),
-        cost_estimate=pl.CostEstimate(flops=4 * 10**9, bytes_accessed=0, transcendentals=0),
         name="select",
-    )(coords.T)
+    )(coords.T, mark)
     select, counts = lax.optimization_barrier((select, counts))
     part = jax.ShapeDtypeStruct((chips, vectors, width), F32)
     keep, send = pl.pallas_call(
@@ -136,8 +150,9 @@
         name="product",
     )(select, counts, tiles, x_block, *pieces)
 
-    chip = keep + swap(send, "col", 1)
-    parts = [chip[0]] + [swap(chip[k], "col", 2 * k) for k in (1, *range(chips - 1, 1, -1))]
+    chip = keep + swap(send, 0, 1)
+    far = sorted(range(1, chips), key=lambda k: (k != 2, k))
+    parts = [chip[0]] + [swap(chip[k], 0, 2 * k) for k in far]
     y, gram = pl.pallas_call(
         functools.partial(gram_kernel, 1.0 / (width * n_row * n_col)),
         out_shape=(
@@ -149,20 +164,21 @@
         compiler_params=pltpu.CompilerParams(vmem_limit_bytes=4 << 20),
         name="gram",
     )(*parts)
-    gram = gram + swap(gram, "col", 1)
-    gram = total(gram, "row", 1)
-    gram = total(gram, "col", 2)
+    grams = [gram, swap(gram, 0, 1)]
+    for masks in (*rounds("row"), *rounds("col")):
+        gram = functools.reduce(jnp.add, grams)
+        grams = [gram] + [swap(gram, row, col) for row, col in masks]
     return pl.pallas_call(
         factor_kernel,
         out_shape=(
             jax.ShapeDtypeStruct((vectors, width), F32),
             jax.ShapeDtypeStruct((vectors, vectors), F32),
         ),
-        in_specs=[VMEM, VMEM],
+        in_specs=[VMEM] * (1 + len(grams)),
         out_specs=(VMEM, VMEM),
         compiler_params=pltpu.CompilerParams(vmem_limit_bytes=4 << 20),
         name="factor",
-    )(y, gram)
+    )(y, *grams)
 
 
 def solution(mesh):

time: 39.2 us -> 36.4 us (0.929)
  waiting for transfers between devices: 16 us -> 14.7 us
  starting transfers between devices: 16.8 us -> 16.1 us
  local copies, waits for them, and re-layouts: 0.71 us -> 0.03 us
    ppermute x14 -> x15, waiting for transfers between devices: 16 us -> 14.7 us  [swap(): return lax.ppermute(x, ('row', 'col'), pairs)]
    ppermute x14 -> x15, starting transfers between devices: 16.8 us -> 16.1 us  [swap(): return lax.ppermute(x, ('row', 'col'), pairs)]
    unnamed x6, local copies, waits for them, and re-layouts: 0.69 us -> 0.01 us
  transfers between devices with their start and end apart: 14 -> 15, of which waited for: 12 -> 12; matrix products, arithmetic and copies ran while one was open for 0% -> 0% of each run, Pallas kernels for 0% -> 0%
where the time goes in v3:
time: 36.4 us; the launch traced here: 36.3 us
  starting transfers between devices  16.1 us (44%)
  waiting for transfers between devices  14.7 us (40%)
  Pallas kernels  3.98 us (11%)
  between operations  1.37 us (4%)
    ppermute x15, starting transfers between devices, swap(): return lax.ppermute(x, ('row', 'col'), pairs)  16.1 us
    ppermute x15, waiting for transfers between devices, swap(): return lax.ppermute(x, ('row', 'col'), pairs)  14.7 us
    pallas_call x1, Pallas kernels, local(): pl.pallas_call(factor_kernel, out_shape=(jax.ShapeDtypeStruct((vectors, w...  2 us
    pallas_call x1, Pallas kernels, local(): pl.pallas_call(functools.partial(product_kernel, (0, *order)), out_shape=...  1.67 us
  transfers between devices with their start and end apart: 15, of which 12 were waited for; matrix products, arithmetic and copies ran while one was open for 0% of the time, Pallas kernels for 0%

profile of v3, /device:TPU:0, one launch (start us, length us, event | category | flops | bytes accessed | tf_op | source)
XLA Modules:
  0.0 36.3 jit_solution(17871977761205776774)
XLA Ops:
  0.7 0.5 %collective-permute-start.1 = (bf16[64,256]{1,0:T(8,128)(2,1)}, bf16[64,256]{1,0:T(8,128)(2,1)S(1)}, u32[]{:S(2)}, u32[]{:S(2)}) collective-permute-start(bf16[64,256]{1,0:T(8,128)(2,1)} %refs_0_.1), channel_id=1, source_target_pairs={{0,1},{1,0},{2,3},{3,2},{4,5},{5,4},{6,7},{7,6},{8,9},{9,8},{10,11... | collective-permute-start | bytes 98312 | tf_op jit(solution)/shard_map/ppermute | solution.py:22
  1.2 3.5 %collective-permute-start = (bf16[64,256]{1,0:T(8,128)(2,1)}, bf16[64,256]{1,0:T(8,128)(2,1)S(1)}, u32[]{:S(2)}, u32[]{:S(2)}) collective-permute-start(bf16[64,256]{1,0:T(8,128)(2,1)} %refs_0_.1), channel_id=1, source_target_pairs={{0,24},{1,25},{2,26},{3,27},{4,28},{5,29},{6,30},{7,31},{8,16},{9,... | collective-permute-start | bytes 98312 | tf_op jit(solution)/shard_map/ppermute | solution.py:22
  4.7 0.5 %collective-permute-start.3 = (bf16[64,256]{1,0:T(8,128)(2,1)}, bf16[64,256]{1,0:T(8,128)(2,1)S(1)}, u32[]{:S(2)}, u32[]{:S(2)}) collective-permute-start(bf16[64,256]{1,0:T(8,128)(2,1)} %refs_0_.1), channel_id=1, source_target_pairs={{0,16},{1,17},{2,18},{3,19},{4,20},{5,21},{6,22},{7,23},{8,24},{9,... | collective-permute-start | bytes 98312 | tf_op jit(solution)/shard_map/ppermute | solution.py:22
  5.2 0.0 collective-permute-done.1
  5.2 0.0 collective-permute-start.2
  5.9 1.0 %collective-permute-done.refs_1_ = bf16[64,256]{1,0:T(8,128)(2,1)S(1)} collective-permute-done((bf16[64,256]{1,0:T(8,128)(2,1)}, bf16[64,256]{1,0:T(8,128)(2,1)S(1)}, u32[]{:S(2)}, u32[]{:S(2)}) %collective-permute-start) | collective-permute-done | bytes 32800 | tf_op jit(solution)/shard_map/ppermute | solution.py:22
  6.9 1.9 %collective-permute-done.3.refs_3_ = bf16[64,256]{1,0:T(8,128)(2,1)S(1)} collective-permute-done((bf16[64,256]{1,0:T(8,128)(2,1)}, bf16[64,256]{1,0:T(8,128)(2,1)S(1)}, u32[]{:S(2)}, u32[]{:S(2)}) %collective-permute-start.3) | collective-permute-done | bytes 32800 | tf_op jit(solution)/shard_map/ppermute | solution.py:22
  8.8 0.0 collective-permute-done.2.refs_2_
  8.8 1.7 %product.1 = (f32[4,64,256]{2,1,0:T(8,128)S(1)}, f32[4,64,256]{2,1,0:T(8,128)S(1)}) custom-call(s32[2,24]{1,0:T(2,128)S(1)} %select.1, s32[1]{0:T(128)S(6)} %copy.6.counts, bf16[24,256,256]{2,1,0:T(8,128)(2,1)S(1)} %copy-done, bf16[64,256]{1,0:T(8,128)(2,1)S(1)} %copy-done.1, bf16[64,256]{1,0:T(8,128)(2,1)S(1)} %collective-permute-done.refs_1_, ...), custom_call_target="tpu_custom_call" | custom-call | tf_op jit(solution)/shard_map/product/pallas_call | solution.py:140
  10.5 0.2 collective-permute-start.4
  10.7 1.4 %collective-permute-done.4 = f32[4,64,256]{2,1,0:T(8,128)S(1)} collective-permute-done((f32[4,64,256]{2,1,0:T(8,128)S(1)}, f32[4,64,256]{2,1,0:T(8,128)S(1)}, u32[]{:S(2)}, u32[]{:S(2)}) %collective-permute-start.4) | collective-permute-done | bytes 262176 | tf_op jit(solution)/shard_map/ppermute | solution.py:22
  12.2 3.7 %collective-permute-start.7 = (f32[64,256]{1,0:T(8,128)S(1)}, f32[64,256]{1,0:T(8,128)S(1)}, u32[]{:S(2)}, u32[]{:S(2)}) collective-permute-start(f32[64,256]{1,0:T(8,128)S(1)} %get-tuple-element.14), channel_id=1, source_target_pairs={{0,6},{1,7},{2,4},{3,5},{4,2},{5,3},{6,0},{7,1},{8,14},{9,15},{10,... | collective-permute-start | bytes 196616 | tf_op jit(solution)/shard_map/ppermute | solution.py:22
  15.8 0.0 collective-permute-start.6
  15.9 0.8 %collective-permute-start.5 = (f32[64,256]{1,0:T(8,128)S(1)}, f32[64,256]{1,0:T(8,128)S(1)}, u32[]{:S(2)}, u32[]{:S(2)}) collective-permute-start(f32[64,256]{1,0:T(8,128)S(1)} %get-tuple-element.16), channel_id=1, source_target_pairs={{0,4},{1,5},{2,6},{3,7},{4,0},{5,1},{6,2},{7,3},{8,12},{9,13},{10,... | collective-permute-start | bytes 196616 | tf_op jit(solution)/shard_map/ppermute | solution.py:22
  16.6 2.4 %collective-permute-done.7.refs_3_ = f32[64,256]{1,0:T(8,128)S(1)} collective-permute-done((f32[64,256]{1,0:T(8,128)S(1)}, f32[64,256]{1,0:T(8,128)S(1)}, u32[]{:S(2)}, u32[]{:S(2)}) %collective-permute-start.7) | collective-permute-done | bytes 65568 | tf_op jit(solution)/shard_map/ppermute | solution.py:22
  19.0 1.9 %collective-permute-done.6.refs_2_ = f32[64,256]{1,0:T(8,128)S(1)} collective-permute-done((f32[64,256]{1,0:T(8,128)S(1)}, f32[64,256]{1,0:T(8,128)S(1)}, u32[]{:S(2)}, u32[]{:S(2)}) %collective-permute-start.6) | collective-permute-done | bytes 65568 | tf_op jit(solution)/shard_map/ppermute | solution.py:22
  20.9 0.8 %collective-permute-done.5.refs_1_ = f32[64,256]{1,0:T(8,128)S(1)} collective-permute-done((f32[64,256]{1,0:T(8,128)S(1)}, f32[64,256]{1,0:T(8,128)S(1)}, u32[]{:S(2)}, u32[]{:S(2)}) %collective-permute-start.5) | collective-permute-done | bytes 65568 | tf_op jit(solution)/shard_map/ppermute | solution.py:22
  21.7 0.3 gram.1
  22.0 0.0 collective-permute-start.8
  22.0 1.2 %collective-permute-done.8 = f32[32,128]{1,0:T(8,128)S(1)} collective-permute-done((f32[32,128]{1,0:T(8,128)S(1)}, f32[32,128]{1,0:T(8,128)S(1)}, u32[]{:S(2)}, u32[]{:S(2)}) %collective-permute-start.8) | collective-permute-done | bytes 16416 | tf_op jit(solution)/shard_map/ppermute | solution.py:22
  23.2 1.3 %collective-permute-start.11 = (f32[32,128]{1,0:T(8,128)S(1)}, f32[32,128]{1,0:T(8,128)S(1)}, u32[]{:S(2)}, u32[]{:S(2)}) collective-permute-start(f32[32,128]{1,0:T(8,128)S(1)} %add.16), channel_id=1, source_target_pairs={{0,25},{1,24},{2,27},{3,26},{4,29},{5,28},{6,31},{7,30},{8,17},{9,... | collective-permute-start | bytes 49160 | tf_op jit(solution)/shard_map/ppermute | solution.py:22
  24.5 0.5 %collective-permute-start.10 = (f32[32,128]{1,0:T(8,128)S(1)}, f32[32,128]{1,0:T(8,128)S(1)}, u32[]{:S(2)}, u32[]{:S(2)}) collective-permute-start(f32[32,128]{1,0:T(8,128)S(1)} %add.16), channel_id=1, source_target_pairs={{0,17},{1,16},{2,19},{3,18},{4,21},{5,20},{6,23},{7,22},{8,25},{9,... | collective-permute-start | bytes 49160 | tf_op jit(solution)/shard_map/ppermute | solution.py:22
  25.0 1.2 %collective-permute-start.9 = (f32[32,128]{1,0:T(8,128)S(1)}, f32[32,128]{1,0:T(8,128)S(1)}, u32[]{:S(2)}, u32[]{:S(2)}) collective-permute-start(f32[32,128]{1,0:T(8,128)S(1)} %add.16), channel_id=1, source_target_pairs={{0,9},{1,8},{2,11},{3,10},{4,13},{5,12},{6,15},{7,14},{8,1},{9,0},... | collective-permute-start | bytes 49160 | tf_op jit(solution)/shard_map/ppermute | solution.py:22
  26.2 1.1 %collective-permute-done.11 = f32[32,128]{1,0:T(8,128)S(1)} collective-permute-done((f32[32,128]{1,0:T(8,128)S(1)}, f32[32,128]{1,0:T(8,128)S(1)}, u32[]{:S(2)}, u32[]{:S(2)}) %collective-permute-start.11) | collective-permute-done | bytes 16416 | tf_op jit(solution)/shard_map/ppermute | solution.py:22
  27.3 0.5 %collective-permute-done.10 = f32[32,128]{1,0:T(8,128)S(1)} collective-permute-done((f32[32,128]{1,0:T(8,128)S(1)}, f32[32,128]{1,0:T(8,128)S(1)}, u32[]{:S(2)}, u32[]{:S(2)}) %collective-permute-start.10) | collective-permute-done | bytes 16416 | tf_op jit(solution)/shard_map/ppermute | solution.py:22
  27.8 0.4 collective-permute-done.9
  28.2 2.0 %collective-permute-start.14 = (f32[32,128]{1,0:T(8,128)S(1)}, f32[32,128]{1,0:T(8,128)S(1)}, u32[]{:S(2)}, u32[]{:S(2)}) collective-permute-start(f32[32,128]{1,0:T(8,128)S(1)} %add_add_fusion.refs_0_), channel_id=1, source_target_pairs={{0,7},{1,6},{2,5},{3,4},{4,3},{5,2},{6,1},{7,0},{8,15},{9,14},{10,... | collective-permute-start | bytes 49160 | tf_op jit(solution)/shard_map/ppermute | solution.py:22
  30.2 0.5 %collective-permute-start.13 = (f32[32,128]{1,0:T(8,128)S(1)}, f32[32,128]{1,0:T(8,128)S(1)}, u32[]{:S(2)}, u32[]{:S(2)}) collective-permute-start(f32[32,128]{1,0:T(8,128)S(1)} %add_add_fusion.refs_0_), channel_id=1, source_target_pairs={{0,5},{1,4},{2,7},{3,6},{4,1},{5,0},{6,3},{7,2},{8,13},{9,12},{10,... | collective-permute-start | bytes 49160 | tf_op jit(solution)/shard_map/ppermute | solution.py:22
  30.7 1.4 %collective-permute-start.12 = (f32[32,128]{1,0:T(8,128)S(1)}, f32[32,128]{1,0:T(8,128)S(1)}, u32[]{:S(2)}, u32[]{:S(2)}) collective-permute-start(f32[32,128]{1,0:T(8,128)S(1)} %add_add_fusion.refs_0_), channel_id=1, source_target_pairs={{0,3},{1,2},{2,1},{3,0},{4,7},{5,6},{6,5},{7,4},{8,11},{9,10},{10,... | collective-permute-start | bytes 49160 | tf_op jit(solution)/shard_map/ppermute | solution.py:22
  32.1 1.0 %collective-permute-done.14.refs_3_ = f32[32,128]{1,0:T(8,128)S(1)} collective-permute-done((f32[32,128]{1,0:T(8,128)S(1)}, f32[32,128]{1,0:T(8,128)S(1)}, u32[]{:S(2)}, u32[]{:S(2)}) %collective-permute-start.14) | collective-permute-done | bytes 16416 | tf_op jit(solution)/shard_map/ppermute | solution.py:22
  33.1 1.1 %collective-permute-done.13.refs_2_ = f32[32,128]{1,0:T(8,128)S(1)} collective-permute-done((f32[32,128]{1,0:T(8,128)S(1)}, f32[32,128]{1,0:T(8,128)S(1)}, u32[]{:S(2)}, u32[]{:S(2)}) %collective-permute-start.13) | collective-permute-done | bytes 16416 | tf_op jit(solution)/shard_map/ppermute | solution.py:22
  34.2 2.0 %factor.1 = (f32[64,256]{1,0:T(8,128)}, f32[64,64]{1,0:T(8,128)}) custom-call(f32[64,256]{1,0:T(8,128)S(1)} %get-tuple-element.12.y_ref, f32[32,128]{1,0:T(8,128)S(1)} %add_add_fusion.refs_0_, f32[32,128]{1,0:T(8,128)S(1)} %collective-permute-done.12.refs_1_, f32[32,128]{1,0:T(8,128)S(1)} %collective-permute-done.13.refs_2_, ...), custom_call_target="tpu_custom_call" | custom-call | tf_op jit(solution)/shard_map/factor/pallas_call | solution.py:171
  (13 shorter events, 0.1 us)
Async XLA Ops:
  0.6 8.2 %copy-start.1 = (bf16[64,256]{1,0:T(8,128)(2,1)S(1)}, bf16[64,256]{1,0:T(8,128)(2,1)}, u32[]{:S(2)}) copy-start(bf16[64,256]{1,0:T(8,128)(2,1)} %refs_0_.1) | copy-start | bytes 98308
  0.6 5.2 %copy-start.2 = (s32[24,2]{0,1:T(2,128)S(1)}, s32[24,2]{0,1:T(2,128)}, u32[]{:S(2)}) copy-start(s32[24,2]{0,1:T(2,128)} %param.6) | copy-start | bytes 580
  0.6 8.2 %copy-start = (bf16[24,256,256]{2,1,0:T(8,128)(2,1)S(1)}, bf16[24,256,256]{2,1,0:T(8,128)(2,1)}, u32[]{:S(2)}) copy-start(bf16[24,256,256]{2,1,0:T(8,128)(2,1)} %tiles.1) | copy-start | bytes 9437188
  0.7 4.5 %collective-permute-start.1 = (bf16[64,256]{1,0:T(8,128)(2,1)}, bf16[64,256]{1,0:T(8,128)(2,1)S(1)}, u32[]{:S(2)}, u32[]{:S(2)}) collective-permute-start(bf16[64,256]{1,0:T(8,128)(2,1)} %refs_0_.1), channel_id=1, source_target_pairs={{0,1},{1,0},{2,3},{3,2},{4,5},{5,4},{6,7},{7,6},{8,9},{9,8},{10,11... | collective-permute-start | bytes 98312 | tf_op jit(solution)/shard_map/ppermute | solution.py:22
  1.2 5.7 %collective-permute-start = (bf16[64,256]{1,0:T(8,128)(2,1)}, bf16[64,256]{1,0:T(8,128)(2,1)S(1)}, u32[]{:S(2)}, u32[]{:S(2)}) collective-permute-start(bf16[64,256]{1,0:T(8,128)(2,1)} %refs_0_.1), channel_id=1, source_target_pairs={{0,24},{1,25},{2,26},{3,27},{4,28},{5,29},{6,30},{7,31},{8,16},{9,... | collective-permute-start | bytes 98312 | tf_op jit(solution)/shard_map/ppermute | solution.py:22
  4.7 4.1 %collective-permute-start.3 = (bf16[64,256]{1,0:T(8,128)(2,1)}, bf16[64,256]{1,0:T(8,128)(2,1)S(1)}, u32[]{:S(2)}, u32[]{:S(2)}) collective-permute-start(bf16[64,256]{1,0:T(8,128)(2,1)} %refs_0_.1), channel_id=1, source_target_pairs={{0,16},{1,17},{2,18},{3,19},{4,20},{5,21},{6,22},{7,23},{8,24},{9,... | collective-permute-start | bytes 98312 | tf_op jit(solution)/shard_map/ppermute | solution.py:22
  5.2 3.6 %collective-permute-start.2 = (bf16[64,256]{1,0:T(8,128)(2,1)S(1)}, bf16[64,256]{1,0:T(8,128)(2,1)S(1)}, u32[]{:S(2)}, u32[]{:S(2)}) collective-permute-start(bf16[64,256]{1,0:T(8,128)(2,1)S(1)} %collective-permute-done.1), channel_id=1, source_target_pairs={{0,9},{1,8},{2,11},{3,10},{4,13},{5,12},{6,15},{7,14},{8,1},{9,0},... | collective-permute-start | bytes 98312 | tf_op jit(solution)/shard_map/ppermute | solution.py:22
  10.5 1.6 %collective-permute-start.4 = (f32[4,64,256]{2,1,0:T(8,128)S(1)}, f32[4,64,256]{2,1,0:T(8,128)S(1)}, u32[]{:S(2)}, u32[]{:S(2)}) collective-permute-start(f32[4,64,256]{2,1,0:T(8,128)S(1)} %get-tuple-element.11), channel_id=1, source_target_pairs={{0,1},{1,0},{2,3},{3,2},{4,5},{5,4},{6,7},{7,6},{8,9},{9,8},{10,11... | collective-permute-start | bytes 786440 | tf_op jit(solution)/shard_map/ppermute | solution.py:22
  12.2 6.9 %collective-permute-start.7 = (f32[64,256]{1,0:T(8,128)S(1)}, f32[64,256]{1,0:T(8,128)S(1)}, u32[]{:S(2)}, u32[]{:S(2)}) collective-permute-start(f32[64,256]{1,0:T(8,128)S(1)} %get-tuple-element.14), channel_id=1, source_target_pairs={{0,6},{1,7},{2,4},{3,5},{4,2},{5,3},{6,0},{7,1},{8,14},{9,15},{10,... | collective-permute-start | bytes 196616 | tf_op jit(solution)/shard_map/ppermute | solution.py:22
  15.8 5.1 %collective-permute-start.6 = (f32[64,256]{1,0:T(8,128)S(1)}, f32[64,256]{1,0:T(8,128)S(1)}, u32[]{:S(2)}, u32[]{:S(2)}) collective-permute-start(f32[64,256]{1,0:T(8,128)S(1)} %get-tuple-element.15), channel_id=1, source_target_pairs={{0,2},{1,3},{2,0},{3,1},{4,6},{5,7},{6,4},{7,5},{8,10},{9,11},{10,... | collective-permute-start | bytes 196616 | tf_op jit(solution)/shard_map/ppermute | solution.py:22
  15.9 5.9 %collective-permute-start.5 = (f32[64,256]{1,0:T(8,128)S(1)}, f32[64,256]{1,0:T(8,128)S(1)}, u32[]{:S(2)}, u32[]{:S(2)}) collective-permute-start(f32[64,256]{1,0:T(8,128)S(1)} %get-tuple-element.16), channel_id=1, source_target_pairs={{0,4},{1,5},{2,6},{3,7},{4,0},{5,1},{6,2},{7,3},{8,12},{9,13},{10,... | collective-permute-start | bytes 196616 | tf_op jit(solution)/shard_map/ppermute | solution.py:22
  22.0 1.2 %collective-permute-start.8 = (f32[32,128]{1,0:T(8,128)S(1)}, f32[32,128]{1,0:T(8,128)S(1)}, u32[]{:S(2)}, u32[]{:S(2)}) collective-permute-start(f32[32,128]{1,0:T(8,128)S(1)} %get-tuple-element.13), channel_id=1, source_target_pairs={{0,1},{1,0},{2,3},{3,2},{4,5},{5,4},{6,7},{7,6},{8,9},{9,8},{10,11... | collective-permute-start | bytes 49160 | tf_op jit(solution)/shard_map/ppermute | solution.py:22
  23.2 4.1 %collective-permute-start.11 = (f32[32,128]{1,0:T(8,128)S(1)}, f32[32,128]{1,0:T(8,128)S(1)}, u32[]{:S(2)}, u32[]{:S(2)}) collective-permute-start(f32[32,128]{1,0:T(8,128)S(1)} %add.16), channel_id=1, source_target_pairs={{0,25},{1,24},{2,27},{3,26},{4,29},{5,28},{6,31},{7,30},{8,17},{9,... | collective-permute-start | bytes 49160 | tf_op jit(solution)/shard_map/ppermute | solution.py:22
  24.5 3.3 %collective-permute-start.10 = (f32[32,128]{1,0:T(8,128)S(1)}, f32[32,128]{1,0:T(8,128)S(1)}, u32[]{:S(2)}, u32[]{:S(2)}) collective-permute-start(f32[32,128]{1,0:T(8,128)S(1)} %add.16), channel_id=1, source_target_pairs={{0,17},{1,16},{2,19},{3,18},{4,21},{5,20},{6,23},{7,22},{8,25},{9,... | collective-permute-start | bytes 49160 | tf_op jit(solution)/shard_map/ppermute | solution.py:22
  25.0 3.2 %collective-permute-start.9 = (f32[32,128]{1,0:T(8,128)S(1)}, f32[32,128]{1,0:T(8,128)S(1)}, u32[]{:S(2)}, u32[]{:S(2)}) collective-permute-start(f32[32,128]{1,0:T(8,128)S(1)} %add.16), channel_id=1, source_target_pairs={{0,9},{1,8},{2,11},{3,10},{4,13},{5,12},{6,15},{7,14},{8,1},{9,0},... | collective-permute-start | bytes 49160 | tf_op jit(solution)/shard_map/ppermute | solution.py:22
  28.2 5.0 %collective-permute-start.14 = (f32[32,128]{1,0:T(8,128)S(1)}, f32[32,128]{1,0:T(8,128)S(1)}, u32[]{:S(2)}, u32[]{:S(2)}) collective-permute-start(f32[32,128]{1,0:T(8,128)S(1)} %add_add_fusion.refs_0_), channel_id=1, source_target_pairs={{0,7},{1,6},{2,5},{3,4},{4,3},{5,2},{6,1},{7,0},{8,15},{9,14},{10,... | collective-permute-start | bytes 49160 | tf_op jit(solution)/shard_map/ppermute | solution.py:22
  30.2 4.1 %collective-permute-start.13 = (f32[32,128]{1,0:T(8,128)S(1)}, f32[32,128]{1,0:T(8,128)S(1)}, u32[]{:S(2)}, u32[]{:S(2)}) collective-permute-start(f32[32,128]{1,0:T(8,128)S(1)} %add_add_fusion.refs_0_), channel_id=1, source_target_pairs={{0,5},{1,4},{2,7},{3,6},{4,1},{5,0},{6,3},{7,2},{8,13},{9,12},{10,... | collective-permute-start | bytes 49160 | tf_op jit(solution)/shard_map/ppermute | solution.py:22
  30.7 3.6 %collective-permute-start.12 = (f32[32,128]{1,0:T(8,128)S(1)}, f32[32,128]{1,0:T(8,128)S(1)}, u32[]{:S(2)}, u32[]{:S(2)}) collective-permute-start(f32[32,128]{1,0:T(8,128)S(1)} %add_add_fusion.refs_0_), channel_id=1, source_target_pairs={{0,3},{1,2},{2,1},{3,0},{4,7},{5,6},{6,5},{7,4},{8,11},{9,10},{10,... | collective-permute-start | bytes 49160 | tf_op jit(solution)/shard_map/ppermute | solution.py:22

commit v4 on v3

--- a/solution.py
+++ b/solution.py
@@ -34,25 +34,28 @@
     out[...] = jnp.zeros_like(out)
 
 
-def select_kernel(coords, mark, select):
+def select_kernel(coords, counts, mark, select):
     me_row, me_col = lax.axis_index("row"), lax.axis_index("col")
     n_col = lax.axis_size("col")
     apart = coords[0:1, :] ^ me_col
     place = (apart & 1) * (n_col // 2) + (apart >> 1)
-    select[0:1, :] = place
+    slot = lax.broadcasted_iota(jnp.int32, apart.shape, 1)
+    select[0:1, :] = jnp.where(slot < counts[0], place, n_col)
     select[1:2, :] = coords[1:2, :] ^ me_row
 
 
-def product_kernel(order, select, counts, tiles, *refs):
+def turn_kernel(tiles, turned):
+    for s in range(tiles.shape[0]):
+        turned[s] = tiles[s].T
+
+
+def product_kernel(order, select, turned, *refs):
     pieces, (keep, send, x_all, rows) = refs[: len(order)], refs[len(order) :]
     for k, piece in zip(order, pieces):
         x_all[k] = piece[...]
     rows[...] = jnp.zeros_like(rows)
-    for s in range(tiles.shape[0]):
-        place = jnp.where(s < counts[0], select[0, s], rows.shape[0] - 1)
-        rows[place] += lax.dot_general(
-            x_all[select[1, s]], tiles[s], (((1,), (1,)), ((), ())), preferred_element_type=F32
-        )
+    for s in range(turned.shape[0]):
+        rows[select[0, s]] += jnp.dot(x_all[select[1, s]], turned[s], preferred_element_type=F32)
     half = keep.shape[0]
     keep[...] = rows[:half]
     send[...] = rows[half : 2 * half]
@@ -127,20 +130,29 @@
         cost_estimate=pl.CostEstimate(flops=4 * 10**9, bytes_accessed=0, transcendentals=0),
         name="mark",
     )()
+    mark, counts = lax.optimization_barrier((mark, counts))
     select = pl.pallas_call(
         select_kernel,
         out_shape=jax.ShapeDtypeStruct(coords.shape[::-1], jnp.int32),
-        in_specs=[VMEM, VMEM],
+        in_specs=[VMEM, SMEM, VMEM],
         out_specs=VMEM,
         compiler_params=pltpu.CompilerParams(vmem_limit_bytes=1 << 20),
         name="select",
-    )(coords.T, mark)
-    select, counts = lax.optimization_barrier((select, counts))
+    )(coords.T, counts, mark)
+    turned = pl.pallas_call(
+        turn_kernel,
+        out_shape=jax.ShapeDtypeStruct(tiles.shape[:1] + tiles.shape[:0:-1], tiles.dtype),
+        in_specs=[VMEM],
+        out_specs=VMEM,
+        compiler_params=pltpu.CompilerParams(vmem_limit_bytes=8 << 20),
+        cost_estimate=pl.CostEstimate(flops=10**9, bytes_accessed=0, transcendentals=0),
+        name="turn",
+    )(tiles)
     part = jax.ShapeDtypeStruct((chips, vectors, width), F32)
     keep, send = pl.pallas_call(
         functools.partial(product_kernel, (0, *order)),
         out_shape=(part, part),
-        in_specs=[SMEM, SMEM] + [VMEM] * (1 + n_row),
+        in_specs=[VMEM] * (2 + n_row),
         out_specs=(VMEM, VMEM),
         scratch_shapes=[
             pltpu.VMEM((n_row, vectors, width), x_block.dtype),
@@ -148,7 +160,7 @@
         ],
         compiler_params=pltpu.CompilerParams(vmem_limit_bytes=12 << 20),
         name="product",
-    )(select, counts, tiles, x_block, *pieces)
+    )(select, turned, x_block, *pieces)
 
     chip = keep + swap(send, 0, 1)
     far = sorted(range(1, chips), key=lambda k: (k != 2, k))

time: 36.4 us -> 35.5 us (0.975)
  waiting for transfers between devices: 14.7 us -> 13.8 us
    ppermute x15, waiting for transfers between devices: 14.7 us -> 13.8 us  [swap(): return lax.ppermute(x, ('row', 'col'), pairs)]
    pallas_call x1, Pallas kernels: 1.67 us -> 0.79 us  [local(): pl.pallas_call(functools.partial(product_kernel, (0, *order)), out_shape=...]
    pallas_call x0 -> x1, Pallas kernels: none -> 0.86 us  [local(): pl.pallas_call(turn_kernel, out_shape=jax.ShapeDtypeStruct(tiles.shape[:1...]
  transfers between devices with their start and end apart: 15 -> 15, of which waited for: 12 -> 12; matrix products, arithmetic and copies ran while one was open for 0% -> 0% of each run, Pallas kernels for 0% -> 2%
where the time goes in v4:
time: 35.5 us; the launch traced here: 35.4 us
  starting transfers between devices  16.2 us (46%)
  waiting for transfers between devices  13.8 us (39%)
  Pallas kernels  3.96 us (11%)
  between operations  1.38 us (4%)
    ppermute x15, starting transfers between devices, swap(): return lax.ppermute(x, ('row', 'col'), pairs)  16.2 us
    ppermute x15, waiting for transfers between devices, swap(): return lax.ppermute(x, ('row', 'col'), pairs)  13.8 us
    pallas_call x1, Pallas kernels, local(): pl.pallas_call(factor_kernel, out_shape=(jax.ShapeDtypeStruct((vectors, w...  2 us
    pallas_call x1, Pallas kernels, local(): pl.pallas_call(turn_kernel, out_shape=jax.ShapeDtypeStruct(tiles.shape[:1...  0.86 us
    pallas_call x1, Pallas kernels, local(): pl.pallas_call(functools.partial(product_kernel, (0, *order)), out_shape=...  0.79 us
  transfers between devices with their start and end apart: 15, of which 12 were waited for; matrix products, arithmetic and copies ran while one was open for 0% of the time, Pallas kernels for 2%

profile of v4, /device:TPU:0, one launch (start us, length us, event | category | flops | bytes accessed | tf_op | source)
XLA Modules:
  0.0 35.4 jit_solution(6104196574915310493)
XLA Ops:
  0.6 0.5 %collective-permute-start.1 = (bf16[64,256]{1,0:T(8,128)(2,1)}, bf16[64,256]{1,0:T(8,128)(2,1)S(1)}, u32[]{:S(2)}, u32[]{:S(2)}) collective-permute-start(bf16[64,256]{1,0:T(8,128)(2,1)} %refs_0_.1), channel_id=1, source_target_pairs={{0,1},{1,0},{2,3},{3,2},{4,5},{5,4},{6,7},{7,6},{8,9},{9,8},{10,11... | collective-permute-start | bytes 98312 | tf_op jit(solution)/shard_map/ppermute | solution.py:22
  1.2 3.5 %collective-permute-start = (bf16[64,256]{1,0:T(8,128)(2,1)}, bf16[64,256]{1,0:T(8,128)(2,1)S(1)}, u32[]{:S(2)}, u32[]{:S(2)}) collective-permute-start(bf16[64,256]{1,0:T(8,128)(2,1)} %refs_0_.1), channel_id=1, source_target_pairs={{0,24},{1,25},{2,26},{3,27},{4,28},{5,29},{6,30},{7,31},{8,16},{9,... | collective-permute-start | bytes 98312 | tf_op jit(solution)/shard_map/ppermute | solution.py:22
  4.7 0.5 %collective-permute-start.3 = (bf16[64,256]{1,0:T(8,128)(2,1)}, bf16[64,256]{1,0:T(8,128)(2,1)S(1)}, u32[]{:S(2)}, u32[]{:S(2)}) collective-permute-start(bf16[64,256]{1,0:T(8,128)(2,1)} %refs_0_.1), channel_id=1, source_target_pairs={{0,16},{1,17},{2,18},{3,19},{4,20},{5,21},{6,22},{7,23},{8,24},{9,... | collective-permute-start | bytes 98312 | tf_op jit(solution)/shard_map/ppermute | solution.py:22
  5.2 0.0 collective-permute-done.1
  5.2 0.1 collective-permute-start.2
  5.3 0.9 %turn.1.turned = bf16[24,256,256]{2,1,0:T(8,128)(2,1)S(1)} custom-call(bf16[24,256,256]{2,1,0:T(8,128)(2,1)S(1)} %copy-done), custom_call_target="tpu_custom_call" | custom-call | flops 1000000000 | tf_op jit(solution)/shard_map/turn/pallas_call | solution.py:142
  6.8 0.0 collective-permute-done.refs_1_
  6.9 1.9 %collective-permute-done.3.refs_3_ = bf16[64,256]{1,0:T(8,128)(2,1)S(1)} collective-permute-done((bf16[64,256]{1,0:T(8,128)(2,1)}, bf16[64,256]{1,0:T(8,128)(2,1)S(1)}, u32[]{:S(2)}, u32[]{:S(2)}) %collective-permute-start.3) | collective-permute-done | bytes 32800 | tf_op jit(solution)/shard_map/ppermute | solution.py:22
  8.8 0.1 collective-permute-done.2.refs_2_
  8.9 0.8 %product.1 = (f32[4,64,256]{2,1,0:T(8,128)S(1)}, f32[4,64,256]{2,1,0:T(8,128)S(1)}) custom-call(s32[2,24]{1,0:T(2,128)S(1)} %select.1, bf16[24,256,256]{2,1,0:T(8,128)(2,1)S(1)} %turn.1.turned, bf16[64,256]{1,0:T(8,128)(2,1)S(1)} %copy-done.1, bf16[64,256]{1,0:T(8,128)(2,1)S(1)} %collective-permute-done.refs_1_, ...), custom_call_target="tpu_custom_call" | custom-call | tf_op jit(solution)/shard_map/product/pallas_call | solution.py:152
  9.7 0.2 collective-permute-start.4
  9.9 1.4 %collective-permute-done.4 = f32[4,64,256]{2,1,0:T(8,128)S(1)} collective-permute-done((f32[4,64,256]{2,1,0:T(8,128)S(1)}, f32[4,64,256]{2,1,0:T(8,128)S(1)}, u32[]{:S(2)}, u32[]{:S(2)}) %collective-permute-start.4) | collective-permute-done | bytes 262176 | tf_op jit(solution)/shard_map/ppermute | solution.py:22
  11.4 3.7 %collective-permute-start.7 = (f32[64,256]{1,0:T(8,128)S(1)}, f32[64,256]{1,0:T(8,128)S(1)}, u32[]{:S(2)}, u32[]{:S(2)}) collective-permute-start(f32[64,256]{1,0:T(8,128)S(1)} %get-tuple-element.14), channel_id=1, source_target_pairs={{0,6},{1,7},{2,4},{3,5},{4,2},{5,3},{6,0},{7,1},{8,14},{9,15},{10,... | collective-permute-start | bytes 196616 | tf_op jit(solution)/shard_map/ppermute | solution.py:22
  15.0 0.8 %collective-permute-start.5 = (f32[64,256]{1,0:T(8,128)S(1)}, f32[64,256]{1,0:T(8,128)S(1)}, u32[]{:S(2)}, u32[]{:S(2)}) collective-permute-start(f32[64,256]{1,0:T(8,128)S(1)} %get-tuple-element.16), channel_id=1, source_target_pairs={{0,4},{1,5},{2,6},{3,7},{4,0},{5,1},{6,2},{7,3},{8,12},{9,13},{10,... | collective-permute-start | bytes 196616 | tf_op jit(solution)/shard_map/ppermute | solution.py:22
  15.8 2.4 %collective-permute-done.7.refs_3_ = f32[64,256]{1,0:T(8,128)S(1)} collective-permute-done((f32[64,256]{1,0:T(8,128)S(1)}, f32[64,256]{1,0:T(8,128)S(1)}, u32[]{:S(2)}, u32[]{:S(2)}) %collective-permute-start.7) | collective-permute-done | bytes 65568 | tf_op jit(solution)/shard_map/ppermute | solution.py:22
  18.2 1.9 %collective-permute-done.6.refs_2_ = f32[64,256]{1,0:T(8,128)S(1)} collective-permute-done((f32[64,256]{1,0:T(8,128)S(1)}, f32[64,256]{1,0:T(8,128)S(1)}, u32[]{:S(2)}, u32[]{:S(2)}) %collective-permute-start.6) | collective-permute-done | bytes 65568 | tf_op jit(solution)/shard_map/ppermute | solution.py:22
  20.1 0.8 %collective-permute-done.5.refs_1_ = f32[64,256]{1,0:T(8,128)S(1)} collective-permute-done((f32[64,256]{1,0:T(8,128)S(1)}, f32[64,256]{1,0:T(8,128)S(1)}, u32[]{:S(2)}, u32[]{:S(2)}) %collective-permute-start.5) | collective-permute-done | bytes 65568 | tf_op jit(solution)/shard_map/ppermute | solution.py:22
  20.9 0.3 gram.1
  21.2 0.0 collective-permute-start.8
  21.2 1.2 %collective-permute-done.8 = f32[32,128]{1,0:T(8,128)S(1)} collective-permute-done((f32[32,128]{1,0:T(8,128)S(1)}, f32[32,128]{1,0:T(8,128)S(1)}, u32[]{:S(2)}, u32[]{:S(2)}) %collective-permute-start.8) | collective-permute-done | bytes 16416 | tf_op jit(solution)/shard_map/ppermute | solution.py:22
  22.4 1.3 %collective-permute-start.11 = (f32[32,128]{1,0:T(8,128)S(1)}, f32[32,128]{1,0:T(8,128)S(1)}, u32[]{:S(2)}, u32[]{:S(2)}) collective-permute-start(f32[32,128]{1,0:T(8,128)S(1)} %add.16), channel_id=1, source_target_pairs={{0,25},{1,24},{2,27},{3,26},{4,29},{5,28},{6,31},{7,30},{8,17},{9,... | collective-permute-start | bytes 49160 | tf_op jit(solution)/shard_map/ppermute | solution.py:22
  23.7 0.5 %collective-permute-start.10 = (f32[32,128]{1,0:T(8,128)S(1)}, f32[32,128]{1,0:T(8,128)S(1)}, u32[]{:S(2)}, u32[]{:S(2)}) collective-permute-start(f32[32,128]{1,0:T(8,128)S(1)} %add.16), channel_id=1, source_target_pairs={{0,17},{1,16},{2,19},{3,18},{4,21},{5,20},{6,23},{7,22},{8,25},{9,... | collective-permute-start | bytes 49160 | tf_op jit(solution)/shard_map/ppermute | solution.py:22
  24.2 1.2 %collective-permute-start.9 = (f32[32,128]{1,0:T(8,128)S(1)}, f32[32,128]{1,0:T(8,128)S(1)}, u32[]{:S(2)}, u32[]{:S(2)}) collective-permute-start(f32[32,128]{1,0:T(8,128)S(1)} %add.16), channel_id=1, source_target_pairs={{0,9},{1,8},{2,11},{3,10},{4,13},{5,12},{6,15},{7,14},{8,1},{9,0},... | collective-permute-start | bytes 49160 | tf_op jit(solution)/shard_map/ppermute | solution.py:22
  25.4 1.1 %collective-permute-done.11 = f32[32,128]{1,0:T(8,128)S(1)} collective-permute-done((f32[32,128]{1,0:T(8,128)S(1)}, f32[32,128]{1,0:T(8,128)S(1)}, u32[]{:S(2)}, u32[]{:S(2)}) %collective-permute-start.11) | collective-permute-done | bytes 16416 | tf_op jit(solution)/shard_map/ppermute | solution.py:22
  26.5 0.5 %collective-permute-done.10 = f32[32,128]{1,0:T(8,128)S(1)} collective-permute-done((f32[32,128]{1,0:T(8,128)S(1)}, f32[32,128]{1,0:T(8,128)S(1)}, u32[]{:S(2)}, u32[]{:S(2)}) %collective-permute-start.10) | collective-permute-done | bytes 16416 | tf_op jit(solution)/shard_map/ppermute | solution.py:22
  27.0 0.3 collective-permute-done.9
  27.3 2.0 %collective-permute-start.14 = (f32[32,128]{1,0:T(8,128)S(1)}, f32[32,128]{1,0:T(8,128)S(1)}, u32[]{:S(2)}, u32[]{:S(2)}) collective-permute-start(f32[32,128]{1,0:T(8,128)S(1)} %add_add_fusion.refs_0_), channel_id=1, source_target_pairs={{0,7},{1,6},{2,5},{3,4},{4,3},{5,2},{6,1},{7,0},{8,15},{9,14},{10,... | collective-permute-start | bytes 49160 | tf_op jit(solution)/shard_map/ppermute | solution.py:22
  29.3 0.5 %collective-permute-start.13 = (f32[32,128]{1,0:T(8,128)S(1)}, f32[32,128]{1,0:T(8,128)S(1)}, u32[]{:S(2)}, u32[]{:S(2)}) collective-permute-start(f32[32,128]{1,0:T(8,128)S(1)} %add_add_fusion.refs_0_), channel_id=1, source_target_pairs={{0,5},{1,4},{2,7},{3,6},{4,1},{5,0},{6,3},{7,2},{8,13},{9,12},{10,... | collective-permute-start | bytes 49160 | tf_op jit(solution)/shard_map/ppermute | solution.py:22
  29.8 1.4 %collective-permute-start.12 = (f32[32,128]{1,0:T(8,128)S(1)}, f32[32,128]{1,0:T(8,128)S(1)}, u32[]{:S(2)}, u32[]{:S(2)}) collective-permute-start(f32[32,128]{1,0:T(8,128)S(1)} %add_add_fusion.refs_0_), channel_id=1, source_target_pairs={{0,3},{1,2},{2,1},{3,0},{4,7},{5,6},{6,5},{7,4},{8,11},{9,10},{10,... | collective-permute-start | bytes 49160 | tf_op jit(solution)/shard_map/ppermute | solution.py:22
  31.3 1.0 %collective-permute-done.14.refs_3_ = f32[32,128]{1,0:T(8,128)S(1)} collective-permute-done((f32[32,128]{1,0:T(8,128)S(1)}, f32[32,128]{1,0:T(8,128)S(1)}, u32[]{:S(2)}, u32[]{:S(2)}) %collective-permute-start.14) | collective-permute-done | bytes 16416 | tf_op jit(solution)/shard_map/ppermute | solution.py:22
  32.3 1.1 %collective-permute-done.13.refs_2_ = f32[32,128]{1,0:T(8,128)S(1)} collective-permute-done((f32[32,128]{1,0:T(8,128)S(1)}, f32[32,128]{1,0:T(8,128)S(1)}, u32[]{:S(2)}, u32[]{:S(2)}) %collective-permute-start.13) | collective-permute-done | bytes 16416 | tf_op jit(solution)/shard_map/ppermute | solution.py:22
  33.4 2.0 %factor.1 = (f32[64,256]{1,0:T(8,128)}, f32[64,64]{1,0:T(8,128)}) custom-call(f32[64,256]{1,0:T(8,128)S(1)} %get-tuple-element.12.y_ref, f32[32,128]{1,0:T(8,128)S(1)} %add_add_fusion.refs_0_, f32[32,128]{1,0:T(8,128)S(1)} %collective-permute-done.12.refs_1_, f32[32,128]{1,0:T(8,128)S(1)} %collective-permute-done.13.refs_2_, ...), custom_call_target="tpu_custom_call" | custom-call | tf_op jit(solution)/shard_map/factor/pallas_call | solution.py:183
  (14 shorter events, 0.1 us)
Async XLA Ops:
  0.6 4.7 %copy-start = (bf16[24,256,256]{2,1,0:T(8,128)(2,1)S(1)}, bf16[24,256,256]{2,1,0:T(8,128)(2,1)}, u32[]{:S(2)}) copy-start(bf16[24,256,256]{2,1,0:T(8,128)(2,1)} %tiles.1) | copy-start | bytes 9437188
  0.6 4.6 %collective-permute-start.1 = (bf16[64,256]{1,0:T(8,128)(2,1)}, bf16[64,256]{1,0:T(8,128)(2,1)S(1)}, u32[]{:S(2)}, u32[]{:S(2)}) collective-permute-start(bf16[64,256]{1,0:T(8,128)(2,1)} %refs_0_.1), channel_id=1, source_target_pairs={{0,1},{1,0},{2,3},{3,2},{4,5},{5,4},{6,7},{7,6},{8,9},{9,8},{10,11... | collective-permute-start | bytes 98312 | tf_op jit(solution)/shard_map/ppermute | solution.py:22
  1.2 5.7 %collective-permute-start = (bf16[64,256]{1,0:T(8,128)(2,1)}, bf16[64,256]{1,0:T(8,128)(2,1)S(1)}, u32[]{:S(2)}, u32[]{:S(2)}) collective-permute-start(bf16[64,256]{1,0:T(8,128)(2,1)} %refs_0_.1), channel_id=1, source_target_pairs={{0,24},{1,25},{2,26},{3,27},{4,28},{5,29},{6,30},{7,31},{8,16},{9,... | collective-permute-start | bytes 98312 | tf_op jit(solution)/shard_map/ppermute | solution.py:22
  4.7 4.1 %collective-permute-start.3 = (bf16[64,256]{1,0:T(8,128)(2,1)}, bf16[64,256]{1,0:T(8,128)(2,1)S(1)}, u32[]{:S(2)}, u32[]{:S(2)}) collective-permute-start(bf16[64,256]{1,0:T(8,128)(2,1)} %refs_0_.1), channel_id=1, source_target_pairs={{0,16},{1,17},{2,18},{3,19},{4,20},{5,21},{6,22},{7,23},{8,24},{9,... | collective-permute-start | bytes 98312 | tf_op jit(solution)/shard_map/ppermute | solution.py:22
  5.2 1.6 %copy-start.2 = (s32[24,2]{0,1:T(2,128)S(1)}, s32[24,2]{0,1:T(2,128)}, u32[]{:S(2)}) copy-start(s32[24,2]{0,1:T(2,128)} %param.6) | copy-start | bytes 580
  5.2 3.7 %copy-start.1 = (bf16[64,256]{1,0:T(8,128)(2,1)S(1)}, bf16[64,256]{1,0:T(8,128)(2,1)}, u32[]{:S(2)}) copy-start(bf16[64,256]{1,0:T(8,128)(2,1)} %refs_0_.1) | copy-start | bytes 98308
  5.2 3.7 %collective-permute-start.2 = (bf16[64,256]{1,0:T(8,128)(2,1)S(1)}, bf16[64,256]{1,0:T(8,128)(2,1)S(1)}, u32[]{:S(2)}, u32[]{:S(2)}) collective-permute-start(bf16[64,256]{1,0:T(8,128)(2,1)S(1)} %collective-permute-done.1), channel_id=1, source_target_pairs={{0,9},{1,8},{2,11},{3,10},{4,13},{5,12},{6,15},{7,14},{8,1},{9,0},... | collective-permute-start | bytes 98312 | tf_op jit(solution)/shard_map/ppermute | solution.py:22
  9.7 1.6 %collective-permute-start.4 = (f32[4,64,256]{2,1,0:T(8,128)S(1)}, f32[4,64,256]{2,1,0:T(8,128)S(1)}, u32[]{:S(2)}, u32[]{:S(2)}) collective-permute-start(f32[4,64,256]{2,1,0:T(8,128)S(1)} %get-tuple-element.11), channel_id=1, source_target_pairs={{0,1},{1,0},{2,3},{3,2},{4,5},{5,4},{6,7},{7,6},{8,9},{9,8},{10,11... | collective-permute-start | bytes 786440 | tf_op jit(solution)/shard_map/ppermute | solution.py:22
  11.4 6.9 %collective-permute-start.7 = (f32[64,256]{1,0:T(8,128)S(1)}, f32[64,256]{1,0:T(8,128)S(1)}, u32[]{:S(2)}, u32[]{:S(2)}) collective-permute-start(f32[64,256]{1,0:T(8,128)S(1)} %get-tuple-element.14), channel_id=1, source_target_pairs={{0,6},{1,7},{2,4},{3,5},{4,2},{5,3},{6,0},{7,1},{8,14},{9,15},{10,... | collective-permute-start | bytes 196616 | tf_op jit(solution)/shard_map/ppermute | solution.py:22
  15.0 5.1 %collective-permute-start.6 = (f32[64,256]{1,0:T(8,128)S(1)}, f32[64,256]{1,0:T(8,128)S(1)}, u32[]{:S(2)}, u32[]{:S(2)}) collective-permute-start(f32[64,256]{1,0:T(8,128)S(1)} %get-tuple-element.15), channel_id=1, source_target_pairs={{0,2},{1,3},{2,0},{3,1},{4,6},{5,7},{6,4},{7,5},{8,10},{9,11},{10,... | collective-permute-start | bytes 196616 | tf_op jit(solution)/shard_map/ppermute | solution.py:22
  15.0 5.9 %collective-permute-start.5 = (f32[64,256]{1,0:T(8,128)S(1)}, f32[64,256]{1,0:T(8,128)S(1)}, u32[]{:S(2)}, u32[]{:S(2)}) collective-permute-start(f32[64,256]{1,0:T(8,128)S(1)} %get-tuple-element.16), channel_id=1, source_target_pairs={{0,4},{1,5},{2,6},{3,7},{4,0},{5,1},{6,2},{7,3},{8,12},{9,13},{10,... | collective-permute-start | bytes 196616 | tf_op jit(solution)/shard_map/ppermute | solution.py:22
  21.2 1.2 %collective-permute-start.8 = (f32[32,128]{1,0:T(8,128)S(1)}, f32[32,128]{1,0:T(8,128)S(1)}, u32[]{:S(2)}, u32[]{:S(2)}) collective-permute-start(f32[32,128]{1,0:T(8,128)S(1)} %get-tuple-element.13), channel_id=1, source_target_pairs={{0,1},{1,0},{2,3},{3,2},{4,5},{5,4},{6,7},{7,6},{8,9},{9,8},{10,11... | collective-permute-start | bytes 49160 | tf_op jit(solution)/shard_map/ppermute | solution.py:22
  22.4 4.1 %collective-permute-start.11 = (f32[32,128]{1,0:T(8,128)S(1)}, f32[32,128]{1,0:T(8,128)S(1)}, u32[]{:S(2)}, u32[]{:S(2)}) collective-permute-start(f32[32,128]{1,0:T(8,128)S(1)} %add.16), channel_id=1, source_target_pairs={{0,25},{1,24},{2,27},{3,26},{4,29},{5,28},{6,31},{7,30},{8,17},{9,... | collective-permute-start | bytes 49160 | tf_op jit(solution)/shard_map/ppermute | solution.py:22
  23.7 3.3 %collective-permute-start.10 = (f32[32,128]{1,0:T(8,128)S(1)}, f32[32,128]{1,0:T(8,128)S(1)}, u32[]{:S(2)}, u32[]{:S(2)}) collective-permute-start(f32[32,128]{1,0:T(8,128)S(1)} %add.16), channel_id=1, source_target_pairs={{0,17},{1,16},{2,19},{3,18},{4,21},{5,20},{6,23},{7,22},{8,25},{9,... | collective-permute-start | bytes 49160 | tf_op jit(solution)/shard_map/ppermute | solution.py:22
  24.2 3.2 %collective-permute-start.9 = (f32[32,128]{1,0:T(8,128)S(1)}, f32[32,128]{1,0:T(8,128)S(1)}, u32[]{:S(2)}, u32[]{:S(2)}) collective-permute-start(f32[32,128]{1,0:T(8,128)S(1)} %add.16), channel_id=1, source_target_pairs={{0,9},{1,8},{2,11},{3,10},{4,13},{5,12},{6,15},{7,14},{8,1},{9,0},... | collective-permute-start | bytes 49160 | tf_op jit(solution)/shard_map/ppermute | solution.py:22
  27.3 5.0 %collective-permute-start.14 = (f32[32,128]{1,0:T(8,128)S(1)}, f32[32,128]{1,0:T(8,128)S(1)}, u32[]{:S(2)}, u32[]{:S(2)}) collective-permute-start(f32[32,128]{1,0:T(8,128)S(1)} %add_add_fusion.refs_0_), channel_id=1, source_target_pairs={{0,7},{1,6},{2,5},{3,4},{4,3},{5,2},{6,1},{7,0},{8,15},{9,14},{10,... | collective-permute-start | bytes 49160 | tf_op jit(solution)/shard_map/ppermute | solution.py:22
  29.3 4.1 %collective-permute-start.13 = (f32[32,128]{1,0:T(8,128)S(1)}, f32[32,128]{1,0:T(8,128)S(1)}, u32[]{:S(2)}, u32[]{:S(2)}) collective-permute-start(f32[32,128]{1,0:T(8,128)S(1)} %add_add_fusion.refs_0_), channel_id=1, source_target_pairs={{0,5},{1,4},{2,7},{3,6},{4,1},{5,0},{6,3},{7,2},{8,13},{9,12},{10,... | collective-permute-start | bytes 49160 | tf_op jit(solution)/shard_map/ppermute | solution.py:22
  29.8 3.6 %collective-permute-start.12 = (f32[32,128]{1,0:T(8,128)S(1)}, f32[32,128]{1,0:T(8,128)S(1)}, u32[]{:S(2)}, u32[]{:S(2)}) collective-permute-start(f32[32,128]{1,0:T(8,128)S(1)} %add_add_fusion.refs_0_), channel_id=1, source_target_pairs={{0,3},{1,2},{2,1},{3,0},{4,7},{5,6},{6,5},{7,4},{8,11},{9,10},{10,... | collective-permute-start | bytes 49160 | tf_op jit(solution)/shard_map/ppermute | solution.py:22

commit v5 on v4

--- a/solution.py
+++ b/solution.py
@@ -74,6 +74,14 @@
             precision=EXACT,
             preferred_element_type=F32,
         )
+
+
+def hand_kernel(came, _, out):
+    out[...] = came[...]
+
+
+def sum_kernel(*refs):
+    refs[-1][...] = functools.reduce(jnp.add, [ref[...] for ref in refs[:-1]])
 
 
 def factor_kernel(y_ref, *refs):
@@ -176,9 +184,29 @@
         compiler_params=pltpu.CompilerParams(vmem_limit_bytes=4 << 20),
         name="gram",
     )(*parts)
-    grams = [gram, swap(gram, 0, 1)]
-    for masks in (*rounds("row"), *rounds("col")):
-        gram = functools.reduce(jnp.add, grams)
+    small = jax.ShapeDtypeStruct(gram.shape, F32)
+    far = swap(gram, 3, 1)
+    gram = gram + swap(gram, 0, 1)
+    near = [swap(gram, k, 1) for k in (1, 2)]
+    far = pl.pallas_call(
+        hand_kernel,
+        out_shape=small,
+        in_specs=[VMEM] * 2,
+        out_specs=VMEM,
+        compiler_params=pltpu.CompilerParams(vmem_limit_bytes=1 << 20),
+        name="hand",
+    )(far, gram)
+    fix = swap(far, 0, 1)
+    grams = [fix, far, gram] + near
+    for masks in (*list(rounds("row"))[1:], *rounds("col")):
+        gram = pl.pallas_call(
+            sum_kernel,
+            out_shape=small,
+            in_specs=[VMEM] * len(grams),
+            out_specs=VMEM,
+            compiler_params=pltpu.CompilerParams(vmem_limit_bytes=1 << 20),
+            name="sum",
+        )(*grams)
         grams = [gram] + [swap(gram, row, col) for row, col in masks]
     return pl.pallas_call(
         factor_kernel,

time: 35.5 us -> 35.3 us (level)
  waiting for transfers between devices: 13.8 us -> 12.5 us
  starting transfers between devices: 16.2 us -> 17.2 us
    ppermute x15 -> x16, waiting for transfers between devices: 13.8 us -> 12.5 us  [swap(): return lax.ppermute(x, ('row', 'col'), pairs)]
    ppermute x15 -> x16, starting transfers between devices: 16.2 us -> 17.2 us  [swap(): return lax.ppermute(x, ('row', 'col'), pairs)]
  transfers between devices with their start and end apart: 15 -> 16, of which waited for: 12 -> 11; matrix products, arithmetic and copies ran while one was open for 0% -> 0% of each run, Pallas kernels for 2% -> 2%
where the time goes in v5:
time: 35.3 us; the launch traced here: 35.1 us
  starting transfers between devices  17.2 us (49%)
  waiting for transfers between devices  12.5 us (35%)
  Pallas kernels  3.97 us (11%)
  between operations  1.38 us (4%)
    ppermute x16, starting transfers between devices, swap(): return lax.ppermute(x, ('row', 'col'), pairs)  17.2 us
    ppermute x16, waiting for transfers between devices, swap(): return lax.ppermute(x, ('row', 'col'), pairs)  12.5 us
    pallas_call x1, Pallas kernels, local(): pl.pallas_call(factor_kernel, out_shape=(jax.ShapeDtypeStruct((vectors, w...  2 us
    pallas_call x1, Pallas kernels, local(): pl.pallas_call(turn_kernel, out_shape=jax.ShapeDtypeStruct(tiles.shape[:1...  0.86 us
    pallas_call x1, Pallas kernels, local(): pl.pallas_call(functools.partial(product_kernel, (0, *order)), out_shape=...  0.79 us
  transfers between devices with their start and end apart: 16, of which 11 were waited for; matrix products, arithmetic and copies ran while one was open for 0% of the time, Pallas kernels for 2%

profile of v5, /device:TPU:0, one launch (start us, length us, event | category | flops | bytes accessed | tf_op | source)
XLA Modules:
  0.0 35.1 jit_solution(7946752016531682783)
XLA Ops:
  0.6 0.5 %collective-permute-start.1 = (bf16[64,256]{1,0:T(8,128)(2,1)}, bf16[64,256]{1,0:T(8,128)(2,1)S(1)}, u32[]{:S(2)}, u32[]{:S(2)}) collective-permute-start(bf16[64,256]{1,0:T(8,128)(2,1)} %refs_0_.1), channel_id=1, source_target_pairs={{0,1},{1,0},{2,3},{3,2},{4,5},{5,4},{6,7},{7,6},{8,9},{9,8},{10,11... | collective-permute-start | bytes 98312 | tf_op jit(solution)/shard_map/ppermute | solution.py:22
  1.2 3.5 %collective-permute-start = (bf16[64,256]{1,0:T(8,128)(2,1)}, bf16[64,256]{1,0:T(8,128)(2,1)S(1)}, u32[]{:S(2)}, u32[]{:S(2)}) collective-permute-start(bf16[64,256]{1,0:T(8,128)(2,1)} %refs_0_.1), channel_id=1, source_target_pairs={{0,24},{1,25},{2,26},{3,27},{4,28},{5,29},{6,30},{7,31},{8,16},{9,... | collective-permute-start | bytes 98312 | tf_op jit(solution)/shard_map/ppermute | solution.py:22
  4.7 0.5 %collective-permute-start.3 = (bf16[64,256]{1,0:T(8,128)(2,1)}, bf16[64,256]{1,0:T(8,128)(2,1)S(1)}, u32[]{:S(2)}, u32[]{:S(2)}) collective-permute-start(bf16[64,256]{1,0:T(8,128)(2,1)} %refs_0_.1), channel_id=1, source_target_pairs={{0,16},{1,17},{2,18},{3,19},{4,20},{5,21},{6,22},{7,23},{8,24},{9,... | collective-permute-start | bytes 98312 | tf_op jit(solution)/shard_map/ppermute | solution.py:22
  5.2 0.1 collective-permute-start.2
  5.3 0.9 %turn.1.turned = bf16[24,256,256]{2,1,0:T(8,128)(2,1)S(1)} custom-call(bf16[24,256,256]{2,1,0:T(8,128)(2,1)S(1)} %copy-done), custom_call_target="tpu_custom_call" | custom-call | flops 1000000000 | tf_op jit(solution)/shard_map/turn/pallas_call | solution.py:150
  6.8 0.0 collective-permute-done.refs_1_
  6.9 1.9 %collective-permute-done.3.refs_3_ = bf16[64,256]{1,0:T(8,128)(2,1)S(1)} collective-permute-done((bf16[64,256]{1,0:T(8,128)(2,1)}, bf16[64,256]{1,0:T(8,128)(2,1)S(1)}, u32[]{:S(2)}, u32[]{:S(2)}) %collective-permute-start.3) | collective-permute-done | bytes 32800 | tf_op jit(solution)/shard_map/ppermute | solution.py:22
  8.8 0.1 collective-permute-done.2.refs_2_
  8.9 0.8 %product.1 = (f32[4,64,256]{2,1,0:T(8,128)S(1)}, f32[4,64,256]{2,1,0:T(8,128)S(1)}) custom-call(s32[2,24]{1,0:T(2,128)S(1)} %select.1, bf16[24,256,256]{2,1,0:T(8,128)(2,1)S(1)} %turn.1.turned, bf16[64,256]{1,0:T(8,128)(2,1)S(1)} %copy-done.1, bf16[64,256]{1,0:T(8,128)(2,1)S(1)} %collective-permute-done.refs_1_, ...), custom_call_target="tpu_custom_call" | custom-call | tf_op jit(solution)/shard_map/product/pallas_call | solution.py:160
  9.7 0.2 collective-permute-start.4
  9.9 1.4 %collective-permute-done.4 = f32[4,64,256]{2,1,0:T(8,128)S(1)} collective-permute-done((f32[4,64,256]{2,1,0:T(8,128)S(1)}, f32[4,64,256]{2,1,0:T(8,128)S(1)}, u32[]{:S(2)}, u32[]{:S(2)}) %collective-permute-start.4) | collective-permute-done | bytes 262176 | tf_op jit(solution)/shard_map/ppermute | solution.py:22
  11.4 3.7 %collective-permute-start.7 = (f32[64,256]{1,0:T(8,128)S(1)}, f32[64,256]{1,0:T(8,128)S(1)}, u32[]{:S(2)}, u32[]{:S(2)}) collective-permute-start(f32[64,256]{1,0:T(8,128)S(1)} %get-tuple-element.14), channel_id=1, source_target_pairs={{0,6},{1,7},{2,4},{3,5},{4,2},{5,3},{6,0},{7,1},{8,14},{9,15},{10,... | collective-permute-start | bytes 196616 | tf_op jit(solution)/shard_map/ppermute | solution.py:22
  15.0 0.0 collective-permute-start.6
  15.0 0.8 %collective-permute-start.5 = (f32[64,256]{1,0:T(8,128)S(1)}, f32[64,256]{1,0:T(8,128)S(1)}, u32[]{:S(2)}, u32[]{:S(2)}) collective-permute-start(f32[64,256]{1,0:T(8,128)S(1)} %get-tuple-element.16), channel_id=1, source_target_pairs={{0,4},{1,5},{2,6},{3,7},{4,0},{5,1},{6,2},{7,3},{8,12},{9,13},{10,... | collective-permute-start | bytes 196616 | tf_op jit(solution)/shard_map/ppermute | solution.py:22
  15.8 2.4 %collective-permute-done.7.refs_3_ = f32[64,256]{1,0:T(8,128)S(1)} collective-permute-done((f32[64,256]{1,0:T(8,128)S(1)}, f32[64,256]{1,0:T(8,128)S(1)}, u32[]{:S(2)}, u32[]{:S(2)}) %collective-permute-start.7) | collective-permute-done | bytes 65568 | tf_op jit(solution)/shard_map/ppermute | solution.py:22
  18.2 1.9 %collective-permute-done.6.refs_2_ = f32[64,256]{1,0:T(8,128)S(1)} collective-permute-done((f32[64,256]{1,0:T(8,128)S(1)}, f32[64,256]{1,0:T(8,128)S(1)}, u32[]{:S(2)}, u32[]{:S(2)}) %collective-permute-start.6) | collective-permute-done | bytes 65568 | tf_op jit(solution)/shard_map/ppermute | solution.py:22
  20.1 0.8 %collective-permute-done.5.refs_1_ = f32[64,256]{1,0:T(8,128)S(1)} collective-permute-done((f32[64,256]{1,0:T(8,128)S(1)}, f32[64,256]{1,0:T(8,128)S(1)}, u32[]{:S(2)}, u32[]{:S(2)}) %collective-permute-start.5) | collective-permute-done | bytes 65568 | tf_op jit(solution)/shard_map/ppermute | solution.py:22
  20.9 0.3 gram.1
  21.2 0.0 collective-permute-start.9
  21.2 1.6 %collective-permute-start.8 = (f32[32,128]{1,0:T(8,128)S(1)}, f32[32,128]{1,0:T(8,128)S(1)}, u32[]{:S(2)}, u32[]{:S(2)}) collective-permute-start(f32[32,128]{1,0:T(8,128)S(1)} %get-tuple-element.13), channel_id=1, source_target_pairs={{0,25},{1,24},{2,27},{3,26},{4,29},{5,28},{6,31},{7,30},{8,17},{9,... | collective-permute-start | bytes 49160 | tf_op jit(solution)/shard_map/ppermute | solution.py:22
  22.8 0.8 %collective-permute-start.12 = (f32[32,128]{1,0:T(8,128)S(1)}, f32[32,128]{1,0:T(8,128)S(1)}, u32[]{:S(2)}, u32[]{:S(2)}) collective-permute-start(f32[32,128]{1,0:T(8,128)S(1)} %add.7._.refs_2_), channel_id=1, source_target_pairs={{0,17},{1,16},{2,19},{3,18},{4,21},{5,20},{6,23},{7,22},{8,25},{9,... | collective-permute-start | bytes 49160 | tf_op jit(solution)/shard_map/ppermute | solution.py:22
  23.7 0.9 %collective-permute-start.11 = (f32[32,128]{1,0:T(8,128)S(1)}, f32[32,128]{1,0:T(8,128)S(1)}, u32[]{:S(2)}, u32[]{:S(2)}) collective-permute-start(f32[32,128]{1,0:T(8,128)S(1)} %add.7._.refs_2_), channel_id=1, source_target_pairs={{0,9},{1,8},{2,11},{3,10},{4,13},{5,12},{6,15},{7,14},{8,1},{9,0},... | collective-permute-start | bytes 49160 | tf_op jit(solution)/shard_map/ppermute | solution.py:22
  24.6 0.7 %collective-permute-done.8.came = f32[32,128]{1,0:T(8,128)S(1)} collective-permute-done((f32[32,128]{1,0:T(8,128)S(1)}, f32[32,128]{1,0:T(8,128)S(1)}, u32[]{:S(2)}, u32[]{:S(2)}) %collective-permute-start.8) | collective-permute-done | bytes 16416 | tf_op jit(solution)/shard_map/ppermute | solution.py:22
  25.4 0.5 %collective-permute-start.10 = (f32[32,128]{1,0:T(8,128)S(1)}, f32[32,128]{1,0:T(8,128)S(1)}, u32[]{:S(2)}, u32[]{:S(2)}) collective-permute-start(f32[32,128]{1,0:T(8,128)S(1)} %hand.1.refs_1_), channel_id=1, source_target_pairs={{0,1},{1,0},{2,3},{3,2},{4,5},{5,4},{6,7},{7,6},{8,9},{9,8},{10,11... | collective-permute-start | bytes 49160 | tf_op jit(solution)/shard_map/ppermute | solution.py:22
  25.8 0.4 %collective-permute-done.12.refs_4_ = f32[32,128]{1,0:T(8,128)S(1)} collective-permute-done((f32[32,128]{1,0:T(8,128)S(1)}, f32[32,128]{1,0:T(8,128)S(1)}, u32[]{:S(2)}, u32[]{:S(2)}) %collective-permute-start.12) | collective-permute-done | bytes 16416 | tf_op jit(solution)/shard_map/ppermute | solution.py:22
  26.2 0.7 %collective-permute-done.11.refs_3_ = f32[32,128]{1,0:T(8,128)S(1)} collective-permute-done((f32[32,128]{1,0:T(8,128)S(1)}, f32[32,128]{1,0:T(8,128)S(1)}, u32[]{:S(2)}, u32[]{:S(2)}) %collective-permute-start.11) | collective-permute-done | bytes 16416 | tf_op jit(solution)/shard_map/ppermute | solution.py:22
  26.9 2.2 %collective-permute-start.15 = (f32[32,128]{1,0:T(8,128)S(1)}, f32[32,128]{1,0:T(8,128)S(1)}, u32[]{:S(2)}, u32[]{:S(2)}) collective-permute-start(f32[32,128]{1,0:T(8,128)S(1)} %sum.1.refs_0_), channel_id=1, source_target_pairs={{0,7},{1,6},{2,5},{3,4},{4,3},{5,2},{6,1},{7,0},{8,15},{9,14},{10,... | collective-permute-start | bytes 49160 | tf_op jit(solution)/shard_map/ppermute | solution.py:22
  29.0 0.4 %collective-permute-start.14 = (f32[32,128]{1,0:T(8,128)S(1)}, f32[32,128]{1,0:T(8,128)S(1)}, u32[]{:S(2)}, u32[]{:S(2)}) collective-permute-start(f32[32,128]{1,0:T(8,128)S(1)} %sum.1.refs_0_), channel_id=1, source_target_pairs={{0,5},{1,4},{2,7},{3,6},{4,1},{5,0},{6,3},{7,2},{8,13},{9,12},{10,... | collective-permute-start | bytes 49160 | tf_op jit(solution)/shard_map/ppermute | solution.py:22
  29.4 1.6 %collective-permute-start.13 = (f32[32,128]{1,0:T(8,128)S(1)}, f32[32,128]{1,0:T(8,128)S(1)}, u32[]{:S(2)}, u32[]{:S(2)}) collective-permute-start(f32[32,128]{1,0:T(8,128)S(1)} %sum.1.refs_0_), channel_id=1, source_target_pairs={{0,3},{1,2},{2,1},{3,0},{4,7},{5,6},{6,5},{7,4},{8,11},{9,10},{10,... | collective-permute-start | bytes 49160 | tf_op jit(solution)/shard_map/ppermute | solution.py:22
  31.0 0.9 %collective-permute-done.15.refs_3_ = f32[32,128]{1,0:T(8,128)S(1)} collective-permute-done((f32[32,128]{1,0:T(8,128)S(1)}, f32[32,128]{1,0:T(8,128)S(1)}, u32[]{:S(2)}, u32[]{:S(2)}) %collective-permute-start.15) | collective-permute-done | bytes 16416 | tf_op jit(solution)/shard_map/ppermute | solution.py:22
  31.9 1.2 %collective-permute-done.14.refs_2_ = f32[32,128]{1,0:T(8,128)S(1)} collective-permute-done((f32[32,128]{1,0:T(8,128)S(1)}, f32[32,128]{1,0:T(8,128)S(1)}, u32[]{:S(2)}, u32[]{:S(2)}) %collective-permute-start.14) | collective-permute-done | bytes 16416 | tf_op jit(solution)/shard_map/ppermute | solution.py:22
  33.1 2.0 %factor.1 = (f32[64,256]{1,0:T(8,128)}, f32[64,64]{1,0:T(8,128)}) custom-call(f32[64,256]{1,0:T(8,128)S(1)} %get-tuple-element.12.y_ref, f32[32,128]{1,0:T(8,128)S(1)} %sum.1.refs_0_, f32[32,128]{1,0:T(8,128)S(1)} %collective-permute-done.13.refs_1_, f32[32,128]{1,0:T(8,128)S(1)} %collective-permute-done.14.refs_2_, ...), custom_call_target="tpu_custom_call" | custom-call | tf_op jit(solution)/shard_map/factor/pallas_call | solution.py:211
  (17 shorter events, 0.1 us)
Async XLA Ops:
  0.6 4.7 %copy-start = (bf16[24,256,256]{2,1,0:T(8,128)(2,1)S(1)}, bf16[24,256,256]{2,1,0:T(8,128)(2,1)}, u32[]{:S(2)}) copy-start(bf16[24,256,256]{2,1,0:T(8,128)(2,1)} %tiles.1) | copy-start | bytes 9437188
  0.6 4.6 %collective-permute-start.1 = (bf16[64,256]{1,0:T(8,128)(2,1)}, bf16[64,256]{1,0:T(8,128)(2,1)S(1)}, u32[]{:S(2)}, u32[]{:S(2)}) collective-permute-start(bf16[64,256]{1,0:T(8,128)(2,1)} %refs_0_.1), channel_id=1, source_target_pairs={{0,1},{1,0},{2,3},{3,2},{4,5},{5,4},{6,7},{7,6},{8,9},{9,8},{10,11... | collective-permute-start | bytes 98312 | tf_op jit(solution)/shard_map/ppermute | solution.py:22
  1.2 5.7 %collective-permute-start = (bf16[64,256]{1,0:T(8,128)(2,1)}, bf16[64,256]{1,0:T(8,128)(2,1)S(1)}, u32[]{:S(2)}, u32[]{:S(2)}) collective-permute-start(bf16[64,256]{1,0:T(8,128)(2,1)} %refs_0_.1), channel_id=1, source_target_pairs={{0,24},{1,25},{2,26},{3,27},{4,28},{5,29},{6,30},{7,31},{8,16},{9,... | collective-permute-start | bytes 98312 | tf_op jit(solution)/shard_map/ppermute | solution.py:22
  4.7 4.1 %collective-permute-start.3 = (bf16[64,256]{1,0:T(8,128)(2,1)}, bf16[64,256]{1,0:T(8,128)(2,1)S(1)}, u32[]{:S(2)}, u32[]{:S(2)}) collective-permute-start(bf16[64,256]{1,0:T(8,128)(2,1)} %refs_0_.1), channel_id=1, source_target_pairs={{0,16},{1,17},{2,18},{3,19},{4,20},{5,21},{6,22},{7,23},{8,24},{9,... | collective-permute-start | bytes 98312 | tf_op jit(solution)/shard_map/ppermute | solution.py:22
  5.2 1.6 %copy-start.2 = (s32[24,2]{0,1:T(2,128)S(1)}, s32[24,2]{0,1:T(2,128)}, u32[]{:S(2)}) copy-start(s32[24,2]{0,1:T(2,128)} %param.6) | copy-start | bytes 580
  5.2 3.7 %copy-start.1 = (bf16[64,256]{1,0:T(8,128)(2,1)S(1)}, bf16[64,256]{1,0:T(8,128)(2,1)}, u32[]{:S(2)}) copy-start(bf16[64,256]{1,0:T(8,128)(2,1)} %refs_0_.1) | copy-start | bytes 98308
  5.2 3.7 %collective-permute-start.2 = (bf16[64,256]{1,0:T(8,128)(2,1)S(1)}, bf16[64,256]{1,0:T(8,128)(2,1)S(1)}, u32[]{:S(2)}, u32[]{:S(2)}) collective-permute-start(bf16[64,256]{1,0:T(8,128)(2,1)S(1)} %collective-permute-done.1), channel_id=1, source_target_pairs={{0,9},{1,8},{2,11},{3,10},{4,13},{5,12},{6,15},{7,14},{8,1},{9,0},... | collective-permute-start | bytes 98312 | tf_op jit(solution)/shard_map/ppermute | solution.py:22
  9.7 1.6 %collective-permute-start.4 = (f32[4,64,256]{2,1,0:T(8,128)S(1)}, f32[4,64,256]{2,1,0:T(8,128)S(1)}, u32[]{:S(2)}, u32[]{:S(2)}) collective-permute-start(f32[4,64,256]{2,1,0:T(8,128)S(1)} %get-tuple-element.11), channel_id=1, source_target_pairs={{0,1},{1,0},{2,3},{3,2},{4,5},{5,4},{6,7},{7,6},{8,9},{9,8},{10,11... | collective-permute-start | bytes 786440 | tf_op jit(solution)/shard_map/ppermute | solution.py:22
  11.4 6.9 %collective-permute-start.7 = (f32[64,256]{1,0:T(8,128)S(1)}, f32[64,256]{1,0:T(8,128)S(1)}, u32[]{:S(2)}, u32[]{:S(2)}) collective-permute-start(f32[64,256]{1,0:T(8,128)S(1)} %get-tuple-element.14), channel_id=1, source_target_pairs={{0,6},{1,7},{2,4},{3,5},{4,2},{5,3},{6,0},{7,1},{8,14},{9,15},{10,... | collective-permute-start | bytes 196616 | tf_op jit(solution)/shard_map/ppermute | solution.py:22
  15.0 5.1 %collective-permute-start.6 = (f32[64,256]{1,0:T(8,128)S(1)}, f32[64,256]{1,0:T(8,128)S(1)}, u32[]{:S(2)}, u32[]{:S(2)}) collective-permute-start(f32[64,256]{1,0:T(8,128)S(1)} %get-tuple-element.15), channel_id=1, source_target_pairs={{0,2},{1,3},{2,0},{3,1},{4,6},{5,7},{6,4},{7,5},{8,10},{9,11},{10,... | collective-permute-start | bytes 196616 | tf_op jit(solution)/shard_map/ppermute | solution.py:22
  15.0 5.9 %collective-permute-start.5 = (f32[64,256]{1,0:T(8,128)S(1)}, f32[64,256]{1,0:T(8,128)S(1)}, u32[]{:S(2)}, u32[]{:S(2)}) collective-permute-start(f32[64,256]{1,0:T(8,128)S(1)} %get-tuple-element.16), channel_id=1, source_target_pairs={{0,4},{1,5},{2,6},{3,7},{4,0},{5,1},{6,2},{7,3},{8,12},{9,13},{10,... | collective-permute-start | bytes 196616 | tf_op jit(solution)/shard_map/ppermute | solution.py:22
  21.2 1.6 %collective-permute-start.9 = (f32[32,128]{1,0:T(8,128)S(1)}, f32[32,128]{1,0:T(8,128)S(1)}, u32[]{:S(2)}, u32[]{:S(2)}) collective-permute-start(f32[32,128]{1,0:T(8,128)S(1)} %get-tuple-element.13), channel_id=1, source_target_pairs={{0,1},{1,0},{2,3},{3,2},{4,5},{5,4},{6,7},{7,6},{8,9},{9,8},{10,11... | collective-permute-start | bytes 49160 | tf_op jit(solution)/shard_map/ppermute | solution.py:22
  21.2 4.1 %collective-permute-start.8 = (f32[32,128]{1,0:T(8,128)S(1)}, f32[32,128]{1,0:T(8,128)S(1)}, u32[]{:S(2)}, u32[]{:S(2)}) collective-permute-start(f32[32,128]{1,0:T(8,128)S(1)} %get-tuple-element.13), channel_id=1, source_target_pairs={{0,25},{1,24},{2,27},{3,26},{4,29},{5,28},{6,31},{7,30},{8,17},{9,... | collective-permute-start | bytes 49160 | tf_op jit(solution)/shard_map/ppermute | solution.py:22
  22.8 3.3 %collective-permute-start.12 = (f32[32,128]{1,0:T(8,128)S(1)}, f32[32,128]{1,0:T(8,128)S(1)}, u32[]{:S(2)}, u32[]{:S(2)}) collective-permute-start(f32[32,128]{1,0:T(8,128)S(1)} %add.7._.refs_2_), channel_id=1, source_target_pairs={{0,17},{1,16},{2,19},{3,18},{4,21},{5,20},{6,23},{7,22},{8,25},{9,... | collective-permute-start | bytes 49160 | tf_op jit(solution)/shard_map/ppermute | solution.py:22
  23.7 3.2 %collective-permute-start.11 = (f32[32,128]{1,0:T(8,128)S(1)}, f32[32,128]{1,0:T(8,128)S(1)}, u32[]{:S(2)}, u32[]{:S(2)}) collective-permute-start(f32[32,128]{1,0:T(8,128)S(1)} %add.7._.refs_2_), channel_id=1, source_target_pairs={{0,9},{1,8},{2,11},{3,10},{4,13},{5,12},{6,15},{7,14},{8,1},{9,0},... | collective-permute-start | bytes 49160 | tf_op jit(solution)/shard_map/ppermute | solution.py:22
  25.4 1.5 %collective-permute-start.10 = (f32[32,128]{1,0:T(8,128)S(1)}, f32[32,128]{1,0:T(8,128)S(1)}, u32[]{:S(2)}, u32[]{:S(2)}) collective-permute-start(f32[32,128]{1,0:T(8,128)S(1)} %hand.1.refs_1_), channel_id=1, source_target_pairs={{0,1},{1,0},{2,3},{3,2},{4,5},{5,4},{6,7},{7,6},{8,9},{9,8},{10,11... | collective-permute-start | bytes 49160 | tf_op jit(solution)/shard_map/ppermute | solution.py:22
  26.9 5.0 %collective-permute-start.15 = (f32[32,128]{1,0:T(8,128)S(1)}, f32[32,128]{1,0:T(8,128)S(1)}, u32[]{:S(2)}, u32[]{:S(2)}) collective-permute-start(f32[32,128]{1,0:T(8,128)S(1)} %sum.1.refs_0_), channel_id=1, source_target_pairs={{0,7},{1,6},{2,5},{3,4},{4,3},{5,2},{6,1},{7,0},{8,15},{9,14},{10,... | collective-permute-start | bytes 49160 | tf_op jit(solution)/shard_map/ppermute | solution.py:22
  29.0 4.1 %collective-permute-start.14 = (f32[32,128]{1,0:T(8,128)S(1)}, f32[32,128]{1,0:T(8,128)S(1)}, u32[]{:S(2)}, u32[]{:S(2)}) collective-permute-start(f32[32,128]{1,0:T(8,128)S(1)} %sum.1.refs_0_), channel_id=1, source_target_pairs={{0,5},{1,4},{2,7},{3,6},{4,1},{5,0},{6,3},{7,2},{8,13},{9,12},{10,... | collective-permute-start | bytes 49160 | tf_op jit(solution)/shard_map/ppermute | solution.py:22
  29.4 3.7 %collective-permute-start.13 = (f32[32,128]{1,0:T(8,128)S(1)}, f32[32,128]{1,0:T(8,128)S(1)}, u32[]{:S(2)}, u32[]{:S(2)}) collective-permute-start(f32[32,128]{1,0:T(8,128)S(1)} %sum.1.refs_0_), channel_id=1, source_target_pairs={{0,3},{1,2},{2,1},{3,0},{4,7},{5,6},{6,5},{7,4},{8,11},{9,10},{10,... | collective-permute-start | bytes 49160 | tf_op jit(solution)/shard_map/ppermute | solution.py:22

commit v6 on v5

--- a/solution.py
+++ b/solution.py
@@ -20,6 +20,11 @@
         (i * n_col + j, (i ^ row) * n_col + (j ^ col)) for i in range(n_row) for j in range(n_col)
     ]
     return lax.ppermute(x, ("row", "col"), pairs)
+
+
+def split_swap(x, first, second):
+    n_col = lax.axis_size("col")
+    return lax.ppermute(x, "col", [(j, j ^ (second if j & 1 else first)) for j in range(n_col)])
 
 
 def rounds(axis):
@@ -207,7 +212,12 @@
             compiler_params=pltpu.CompilerParams(vmem_limit_bytes=1 << 20),
             name="sum",
         )(*grams)
-        grams = [gram] + [swap(gram, row, col) for row, col in masks]
+        if masks[0][1] > 1 and len(masks) == 3:
+            came = split_swap(gram, masks[1][1] - 1, masks[2][1] - 1)
+            near = swap(gram, *masks[0])
+            grams = [swap(came, 0, 1), came, gram, near]
+        else:
+            grams = [gram] + [swap(gram, row, col) for row, col in masks]
     return pl.pallas_call(
         factor_kernel,
         out_shape=(

time: 35.3 us -> 34.9 us (0.989)
  starting transfers between devices: 17.2 us -> 15.5 us
  waiting for transfers between devices: 12.5 us -> 13.9 us
    ppermute x16 -> x15, starting transfers between devices: 17.2 us -> 13.4 us  [swap(): return lax.ppermute(x, ('row', 'col'), pairs)]
    ppermute x0 -> x1, waiting for transfers between devices: none -> 2.43 us  [split_swap(): lax.ppermute(x, 'col', [(j, j ^ (second if j & 1 else first)) for j in ra...]
    ppermute x0 -> x1, starting transfers between devices: none -> 2.04 us  [split_swap(): lax.ppermute(x, 'col', [(j, j ^ (second if j & 1 else first)) for j in ra...]
    ppermute x16 -> x15, waiting for transfers between devices: 12.5 us -> 11.4 us  [swap(): return lax.ppermute(x, ('row', 'col'), pairs)]
  transfers between devices with their start and end apart: 16 -> 16, of which waited for: 11 -> 12; matrix products, arithmetic and copies ran while one was open for 0% -> 0% of each run, Pallas kernels for 2% -> 3%
where the time goes in v6:
time: 34.9 us; the launch traced here: 34.8 us
  starting transfers between devices  15.5 us (44%)
  waiting for transfers between devices  13.9 us (40%)
  Pallas kernels  3.97 us (11%)
  between operations  1.38 us (4%)
    ppermute x15, starting transfers between devices, swap(): return lax.ppermute(x, ('row', 'col'), pairs)  13.4 us
    ppermute x15, waiting for transfers between devices, swap(): return lax.ppermute(x, ('row', 'col'), pairs)  11.4 us
    ppermute x1, waiting for transfers between devices, split_swap(): lax.ppermute(x, 'col', [(j, j ^ (second if j & 1 else first)) for j in ra...  2.43 us
    ppermute x1, starting transfers between devices, split_swap(): lax.ppermute(x, 'col', [(j, j ^ (second if j & 1 else first)) for j in ra...  2.04 us
    pallas_call x1, Pallas kernels, local(): pl.pallas_call(factor_kernel, out_shape=(jax.ShapeDtypeStruct((vectors, w...  2 us
    pallas_call x1, Pallas kernels, local(): pl.pallas_call(turn_kernel, out_shape=jax.ShapeDtypeStruct(tiles.shape[:1...  0.86 us
    pallas_call x1, Pallas kernels, local(): pl.pallas_call(functools.partial(product_kernel, (0, *order)), out_shape=...  0.79 us
  transfers between devices with their start and end apart: 16, of which 12 were waited for; matrix products, arithmetic and copies ran while one was open for 0% of the time, Pallas kernels for 3%

profile of v6, /device:TPU:0, one launch (start us, length us, event | category | flops | bytes accessed | tf_op | source)
XLA Modules:
  0.0 34.8 jit_solution(16742552064247008371)
XLA Ops:
  0.6 0.5 %collective-permute-start.1 = (bf16[64,256]{1,0:T(8,128)(2,1)}, bf16[64,256]{1,0:T(8,128)(2,1)S(1)}, u32[]{:S(2)}, u32[]{:S(2)}) collective-permute-start(bf16[64,256]{1,0:T(8,128)(2,1)} %refs_0_.1), channel_id=1, source_target_pairs={{0,1},{1,0},{2,3},{3,2},{4,5},{5,4},{6,7},{7,6},{8,9},{9,8},{10,11... | collective-permute-start | bytes 98312 | tf_op jit(solution)/shard_map/ppermute | solution.py:22
  1.2 3.5 %collective-permute-start = (bf16[64,256]{1,0:T(8,128)(2,1)}, bf16[64,256]{1,0:T(8,128)(2,1)S(1)}, u32[]{:S(2)}, u32[]{:S(2)}) collective-permute-start(bf16[64,256]{1,0:T(8,128)(2,1)} %refs_0_.1), channel_id=1, source_target_pairs={{0,24},{1,25},{2,26},{3,27},{4,28},{5,29},{6,30},{7,31},{8,16},{9,... | collective-permute-start | bytes 98312 | tf_op jit(solution)/shard_map/ppermute | solution.py:22
  4.7 0.5 %collective-permute-start.3 = (bf16[64,256]{1,0:T(8,128)(2,1)}, bf16[64,256]{1,0:T(8,128)(2,1)S(1)}, u32[]{:S(2)}, u32[]{:S(2)}) collective-permute-start(bf16[64,256]{1,0:T(8,128)(2,1)} %refs_0_.1), channel_id=1, source_target_pairs={{0,16},{1,17},{2,18},{3,19},{4,20},{5,21},{6,22},{7,23},{8,24},{9,... | collective-permute-start | bytes 98312 | tf_op jit(solution)/shard_map/ppermute | solution.py:22
  5.2 0.1 collective-permute-start.2
  5.3 0.9 %turn.1.turned = bf16[24,256,256]{2,1,0:T(8,128)(2,1)S(1)} custom-call(bf16[24,256,256]{2,1,0:T(8,128)(2,1)S(1)} %copy-done), custom_call_target="tpu_custom_call" | custom-call | flops 1000000000 | tf_op jit(solution)/shard_map/turn/pallas_call | solution.py:155
  6.8 0.0 collective-permute-done.refs_1_
  6.9 1.9 %collective-permute-done.3.refs_3_ = bf16[64,256]{1,0:T(8,128)(2,1)S(1)} collective-permute-done((bf16[64,256]{1,0:T(8,128)(2,1)}, bf16[64,256]{1,0:T(8,128)(2,1)S(1)}, u32[]{:S(2)}, u32[]{:S(2)}) %collective-permute-start.3) | collective-permute-done | bytes 32800 | tf_op jit(solution)/shard_map/ppermute | solution.py:22
  8.8 0.1 collective-permute-done.2.refs_2_
  8.9 0.8 %product.1 = (f32[4,64,256]{2,1,0:T(8,128)S(1)}, f32[4,64,256]{2,1,0:T(8,128)S(1)}) custom-call(s32[2,24]{1,0:T(2,128)S(1)} %select.1, bf16[24,256,256]{2,1,0:T(8,128)(2,1)S(1)} %turn.1.turned, bf16[64,256]{1,0:T(8,128)(2,1)S(1)} %copy-done.1, bf16[64,256]{1,0:T(8,128)(2,1)S(1)} %collective-permute-done.refs_1_, ...), custom_call_target="tpu_custom_call" | custom-call | tf_op jit(solution)/shard_map/product/pallas_call | solution.py:165
  9.7 0.2 collective-permute-start.4
  9.9 1.4 %collective-permute-done.4 = f32[4,64,256]{2,1,0:T(8,128)S(1)} collective-permute-done((f32[4,64,256]{2,1,0:T(8,128)S(1)}, f32[4,64,256]{2,1,0:T(8,128)S(1)}, u32[]{:S(2)}, u32[]{:S(2)}) %collective-permute-start.4) | collective-permute-done | bytes 262176 | tf_op jit(solution)/shard_map/ppermute | solution.py:22
  11.4 3.7 %collective-permute-start.7 = (f32[64,256]{1,0:T(8,128)S(1)}, f32[64,256]{1,0:T(8,128)S(1)}, u32[]{:S(2)}, u32[]{:S(2)}) collective-permute-start(f32[64,256]{1,0:T(8,128)S(1)} %get-tuple-element.14), channel_id=1, source_target_pairs={{0,6},{1,7},{2,4},{3,5},{4,2},{5,3},{6,0},{7,1},{8,14},{9,15},{10,... | collective-permute-start | bytes 196616 | tf_op jit(solution)/shard_map/ppermute | solution.py:22
  15.0 0.8 %collective-permute-start.5 = (f32[64,256]{1,0:T(8,128)S(1)}, f32[64,256]{1,0:T(8,128)S(1)}, u32[]{:S(2)}, u32[]{:S(2)}) collective-permute-start(f32[64,256]{1,0:T(8,128)S(1)} %get-tuple-element.16), channel_id=1, source_target_pairs={{0,4},{1,5},{2,6},{3,7},{4,0},{5,1},{6,2},{7,3},{8,12},{9,13},{10,... | collective-permute-start | bytes 196616 | tf_op jit(solution)/shard_map/ppermute | solution.py:22
  15.8 2.4 %collective-permute-done.7.refs_3_ = f32[64,256]{1,0:T(8,128)S(1)} collective-permute-done((f32[64,256]{1,0:T(8,128)S(1)}, f32[64,256]{1,0:T(8,128)S(1)}, u32[]{:S(2)}, u32[]{:S(2)}) %collective-permute-start.7) | collective-permute-done | bytes 65568 | tf_op jit(solution)/shard_map/ppermute | solution.py:22
  18.2 1.9 %collective-permute-done.6.refs_2_ = f32[64,256]{1,0:T(8,128)S(1)} collective-permute-done((f32[64,256]{1,0:T(8,128)S(1)}, f32[64,256]{1,0:T(8,128)S(1)}, u32[]{:S(2)}, u32[]{:S(2)}) %collective-permute-start.6) | collective-permute-done | bytes 65568 | tf_op jit(solution)/shard_map/ppermute | solution.py:22
  20.1 0.8 %collective-permute-done.5.refs_1_ = f32[64,256]{1,0:T(8,128)S(1)} collective-permute-done((f32[64,256]{1,0:T(8,128)S(1)}, f32[64,256]{1,0:T(8,128)S(1)}, u32[]{:S(2)}, u32[]{:S(2)}) %collective-permute-start.5) | collective-permute-done | bytes 65568 | tf_op jit(solution)/shard_map/ppermute | solution.py:22
  20.9 0.3 gram.1
  21.2 0.0 collective-permute-start.9
  21.2 1.6 %collective-permute-start.8 = (f32[32,128]{1,0:T(8,128)S(1)}, f32[32,128]{1,0:T(8,128)S(1)}, u32[]{:S(2)}, u32[]{:S(2)}) collective-permute-start(f32[32,128]{1,0:T(8,128)S(1)} %get-tuple-element.13), channel_id=1, source_target_pairs={{0,25},{1,24},{2,27},{3,26},{4,29},{5,28},{6,31},{7,30},{8,17},{9,... | collective-permute-start | bytes 49160 | tf_op jit(solution)/shard_map/ppermute | solution.py:22
  22.8 0.8 %collective-permute-start.12 = (f32[32,128]{1,0:T(8,128)S(1)}, f32[32,128]{1,0:T(8,128)S(1)}, u32[]{:S(2)}, u32[]{:S(2)}) collective-permute-start(f32[32,128]{1,0:T(8,128)S(1)} %add.7._.refs_2_), channel_id=1, source_target_pairs={{0,17},{1,16},{2,19},{3,18},{4,21},{5,20},{6,23},{7,22},{8,25},{9,... | collective-permute-start | bytes 49160 | tf_op jit(solution)/shard_map/ppermute | solution.py:22
  23.7 0.9 %collective-permute-start.11 = (f32[32,128]{1,0:T(8,128)S(1)}, f32[32,128]{1,0:T(8,128)S(1)}, u32[]{:S(2)}, u32[]{:S(2)}) collective-permute-start(f32[32,128]{1,0:T(8,128)S(1)} %add.7._.refs_2_), channel_id=1, source_target_pairs={{0,9},{1,8},{2,11},{3,10},{4,13},{5,12},{6,15},{7,14},{8,1},{9,0},... | collective-permute-start | bytes 49160 | tf_op jit(solution)/shard_map/ppermute | solution.py:22
  24.6 0.7 %collective-permute-done.8.came = f32[32,128]{1,0:T(8,128)S(1)} collective-permute-done((f32[32,128]{1,0:T(8,128)S(1)}, f32[32,128]{1,0:T(8,128)S(1)}, u32[]{:S(2)}, u32[]{:S(2)}) %collective-permute-start.8) | collective-permute-done | bytes 16416 | tf_op jit(solution)/shard_map/ppermute | solution.py:22
  25.4 0.5 %collective-permute-start.10 = (f32[32,128]{1,0:T(8,128)S(1)}, f32[32,128]{1,0:T(8,128)S(1)}, u32[]{:S(2)}, u32[]{:S(2)}) collective-permute-start(f32[32,128]{1,0:T(8,128)S(1)} %hand.1.refs_1_), channel_id=1, source_target_pairs={{0,1},{1,0},{2,3},{3,2},{4,5},{5,4},{6,7},{7,6},{8,9},{9,8},{10,11... | collective-permute-start | bytes 49160 | tf_op jit(solution)/shard_map/ppermute | solution.py:22
  25.8 0.4 %collective-permute-done.12.refs_4_ = f32[32,128]{1,0:T(8,128)S(1)} collective-permute-done((f32[32,128]{1,0:T(8,128)S(1)}, f32[32,128]{1,0:T(8,128)S(1)}, u32[]{:S(2)}, u32[]{:S(2)}) %collective-permute-start.12) | collective-permute-done | bytes 16416 | tf_op jit(solution)/shard_map/ppermute | solution.py:22
  26.2 0.7 %collective-permute-done.11.refs_3_ = f32[32,128]{1,0:T(8,128)S(1)} collective-permute-done((f32[32,128]{1,0:T(8,128)S(1)}, f32[32,128]{1,0:T(8,128)S(1)}, u32[]{:S(2)}, u32[]{:S(2)}) %collective-permute-start.11) | collective-permute-done | bytes 16416 | tf_op jit(solution)/shard_map/ppermute | solution.py:22
  26.9 2.0 %collective-permute-start.13 = (f32[32,128]{1,0:T(8,128)S(1)}, f32[32,128]{1,0:T(8,128)S(1)}, u32[]{:S(2)}, u32[]{:S(2)}) collective-permute-start(f32[32,128]{1,0:T(8,128)S(1)} %sum.1.refs_2_), channel_id=1, source_target_pairs={{0,4},{1,7},{2,6},{3,5},{4,0},{5,3},{6,2},{7,1},{8,12},{9,15},{10,... | collective-permute-start | bytes 49160 | tf_op jit(solution)/shard_map/ppermute | solution.py:27
  28.9 0.2 collective-permute-start.15
  29.1 2.4 %collective-permute-done.13.refs_1_ = f32[32,128]{1,0:T(8,128)S(1)} collective-permute-done((f32[32,128]{1,0:T(8,128)S(1)}, f32[32,128]{1,0:T(8,128)S(1)}, u32[]{:S(2)}, u32[]{:S(2)}) %collective-permute-start.13) | collective-permute-done | bytes 16416 | tf_op jit(solution)/shard_map/ppermute | solution.py:27
  31.6 0.1 collective-permute-start.14
  31.7 0.4 %collective-permute-done.15.refs_3_ = f32[32,128]{1,0:T(8,128)S(1)} collective-permute-done((f32[32,128]{1,0:T(8,128)S(1)}, f32[32,128]{1,0:T(8,128)S(1)}, u32[]{:S(2)}, u32[]{:S(2)}) %collective-permute-start.15) | collective-permute-done | bytes 16416 | tf_op jit(solution)/shard_map/ppermute | solution.py:22
  32.1 0.7 %collective-permute-done.14.refs_0_ = f32[32,128]{1,0:T(8,128)S(1)} collective-permute-done((f32[32,128]{1,0:T(8,128)S(1)}, f32[32,128]{1,0:T(8,128)S(1)}, u32[]{:S(2)}, u32[]{:S(2)}) %collective-permute-start.14) | collective-permute-done | bytes 16416 | tf_op jit(solution)/shard_map/ppermute | solution.py:22
  32.8 2.0 %factor.1 = (f32[64,256]{1,0:T(8,128)}, f32[64,64]{1,0:T(8,128)}) custom-call(f32[64,256]{1,0:T(8,128)S(1)} %get-tuple-element.12.y_ref, f32[32,128]{1,0:T(8,128)S(1)} %collective-permute-done.14.refs_0_, f32[32,128]{1,0:T(8,128)S(1)} %collective-permute-done.13.refs_1_, f32[32,128]{1,0:T(8,128)S(1)} %sum.1.refs_2_, ...), custom_call_target="tpu_custom_call" | custom-call | tf_op jit(solution)/shard_map/factor/pallas_call | solution.py:221
  (17 shorter events, 0.1 us)
Async XLA Ops:
  0.6 4.7 %copy-start = (bf16[24,256,256]{2,1,0:T(8,128)(2,1)S(1)}, bf16[24,256,256]{2,1,0:T(8,128)(2,1)}, u32[]{:S(2)}) copy-start(bf16[24,256,256]{2,1,0:T(8,128)(2,1)} %tiles.1) | copy-start | bytes 9437188
  0.6 4.6 %collective-permute-start.1 = (bf16[64,256]{1,0:T(8,128)(2,1)}, bf16[64,256]{1,0:T(8,128)(2,1)S(1)}, u32[]{:S(2)}, u32[]{:S(2)}) collective-permute-start(bf16[64,256]{1,0:T(8,128)(2,1)} %refs_0_.1), channel_id=1, source_target_pairs={{0,1},{1,0},{2,3},{3,2},{4,5},{5,4},{6,7},{7,6},{8,9},{9,8},{10,11... | collective-permute-start | bytes 98312 | tf_op jit(solution)/shard_map/ppermute | solution.py:22
  1.2 5.7 %collective-permute-start = (bf16[64,256]{1,0:T(8,128)(2,1)}, bf16[64,256]{1,0:T(8,128)(2,1)S(1)}, u32[]{:S(2)}, u32[]{:S(2)}) collective-permute-start(bf16[64,256]{1,0:T(8,128)(2,1)} %refs_0_.1), channel_id=1, source_target_pairs={{0,24},{1,25},{2,26},{3,27},{4,28},{5,29},{6,30},{7,31},{8,16},{9,... | collective-permute-start | bytes 98312 | tf_op jit(solution)/shard_map/ppermute | solution.py:22
  4.7 4.1 %collective-permute-start.3 = (bf16[64,256]{1,0:T(8,128)(2,1)}, bf16[64,256]{1,0:T(8,128)(2,1)S(1)}, u32[]{:S(2)}, u32[]{:S(2)}) collective-permute-start(bf16[64,256]{1,0:T(8,128)(2,1)} %refs_0_.1), channel_id=1, source_target_pairs={{0,16},{1,17},{2,18},{3,19},{4,20},{5,21},{6,22},{7,23},{8,24},{9,... | collective-permute-start | bytes 98312 | tf_op jit(solution)/shard_map/ppermute | solution.py:22
  5.2 1.6 %copy-start.2 = (s32[24,2]{0,1:T(2,128)S(1)}, s32[24,2]{0,1:T(2,128)}, u32[]{:S(2)}) copy-start(s32[24,2]{0,1:T(2,128)} %param.6) | copy-start | bytes 580
  5.2 3.7 %copy-start.1 = (bf16[64,256]{1,0:T(8,128)(2,1)S(1)}, bf16[64,256]{1,0:T(8,128)(2,1)}, u32[]{:S(2)}) copy-start(bf16[64,256]{1,0:T(8,128)(2,1)} %refs_0_.1) | copy-start | bytes 98308
  5.2 3.7 %collective-permute-start.2 = (bf16[64,256]{1,0:T(8,128)(2,1)S(1)}, bf16[64,256]{1,0:T(8,128)(2,1)S(1)}, u32[]{:S(2)}, u32[]{:S(2)}) collective-permute-start(bf16[64,256]{1,0:T(8,128)(2,1)S(1)} %collective-permute-done.1), channel_id=1, source_target_pairs={{0,9},{1,8},{2,11},{3,10},{4,13},{5,12},{6,15},{7,14},{8,1},{9,0},... | collective-permute-start | bytes 98312 | tf_op jit(solution)/shard_map/ppermute | solution.py:22
  9.7 1.6 %collective-permute-start.4 = (f32[4,64,256]{2,1,0:T(8,128)S(1)}, f32[4,64,256]{2,1,0:T(8,128)S(1)}, u32[]{:S(2)}, u32[]{:S(2)}) collective-permute-start(f32[4,64,256]{2,1,0:T(8,128)S(1)} %get-tuple-element.11), channel_id=1, source_target_pairs={{0,1},{1,0},{2,3},{3,2},{4,5},{5,4},{6,7},{7,6},{8,9},{9,8},{10,11... | collective-permute-start | bytes 786440 | tf_op jit(solution)/shard_map/ppermute | solution.py:22
  11.4 6.9 %collective-permute-start.7 = (f32[64,256]{1,0:T(8,128)S(1)}, f32[64,256]{1,0:T(8,128)S(1)}, u32[]{:S(2)}, u32[]{:S(2)}) collective-permute-start(f32[64,256]{1,0:T(8,128)S(1)} %get-tuple-element.14), channel_id=1, source_target_pairs={{0,6},{1,7},{2,4},{3,5},{4,2},{5,3},{6,0},{7,1},{8,14},{9,15},{10,... | collective-permute-start | bytes 196616 | tf_op jit(solution)/shard_map/ppermute | solution.py:22
  15.0 5.1 %collective-permute-start.6 = (f32[64,256]{1,0:T(8,128)S(1)}, f32[64,256]{1,0:T(8,128)S(1)}, u32[]{:S(2)}, u32[]{:S(2)}) collective-permute-start(f32[64,256]{1,0:T(8,128)S(1)} %get-tuple-element.15), channel_id=1, source_target_pairs={{0,2},{1,3},{2,0},{3,1},{4,6},{5,7},{6,4},{7,5},{8,10},{9,11},{10,... | collective-permute-start | bytes 196616 | tf_op jit(solution)/shard_map/ppermute | solution.py:22
  15.0 5.9 %collective-permute-start.5 = (f32[64,256]{1,0:T(8,128)S(1)}, f32[64,256]{1,0:T(8,128)S(1)}, u32[]{:S(2)}, u32[]{:S(2)}) collective-permute-start(f32[64,256]{1,0:T(8,128)S(1)} %get-tuple-element.16), channel_id=1, source_target_pairs={{0,4},{1,5},{2,6},{3,7},{4,0},{5,1},{6,2},{7,3},{8,12},{9,13},{10,... | collective-permute-start | bytes 196616 | tf_op jit(solution)/shard_map/ppermute | solution.py:22
  21.2 1.6 %collective-permute-start.9 = (f32[32,128]{1,0:T(8,128)S(1)}, f32[32,128]{1,0:T(8,128)S(1)}, u32[]{:S(2)}, u32[]{:S(2)}) collective-permute-start(f32[32,128]{1,0:T(8,128)S(1)} %get-tuple-element.13), channel_id=1, source_target_pairs={{0,1},{1,0},{2,3},{3,2},{4,5},{5,4},{6,7},{7,6},{8,9},{9,8},{10,11... | collective-permute-start | bytes 49160 | tf_op jit(solution)/shard_map/ppermute | solution.py:22
  21.2 4.1 %collective-permute-start.8 = (f32[32,128]{1,0:T(8,128)S(1)}, f32[32,128]{1,0:T(8,128)S(1)}, u32[]{:S(2)}, u32[]{:S(2)}) collective-permute-start(f32[32,128]{1,0:T(8,128)S(1)} %get-tuple-element.13), channel_id=1, source_target_pairs={{0,25},{1,24},{2,27},{3,26},{4,29},{5,28},{6,31},{7,30},{8,17},{9,... | collective-permute-start | bytes 49160 | tf_op jit(solution)/shard_map/ppermute | solution.py:22
  22.8 3.3 %collective-permute-start.12 = (f32[32,128]{1,0:T(8,128)S(1)}, f32[32,128]{1,0:T(8,128)S(1)}, u32[]{:S(2)}, u32[]{:S(2)}) collective-permute-start(f32[32,128]{1,0:T(8,128)S(1)} %add.7._.refs_2_), channel_id=1, source_target_pairs={{0,17},{1,16},{2,19},{3,18},{4,21},{5,20},{6,23},{7,22},{8,25},{9,... | collective-permute-start | bytes 49160 | tf_op jit(solution)/shard_map/ppermute | solution.py:22
  23.7 3.2 %collective-permute-start.11 = (f32[32,128]{1,0:T(8,128)S(1)}, f32[32,128]{1,0:T(8,128)S(1)}, u32[]{:S(2)}, u32[]{:S(2)}) collective-permute-start(f32[32,128]{1,0:T(8,128)S(1)} %add.7._.refs_2_), channel_id=1, source_target_pairs={{0,9},{1,8},{2,11},{3,10},{4,13},{5,12},{6,15},{7,14},{8,1},{9,0},... | collective-permute-start | bytes 49160 | tf_op jit(solution)/shard_map/ppermute | solution.py:22
  25.4 1.5 %collective-permute-start.10 = (f32[32,128]{1,0:T(8,128)S(1)}, f32[32,128]{1,0:T(8,128)S(1)}, u32[]{:S(2)}, u32[]{:S(2)}) collective-permute-start(f32[32,128]{1,0:T(8,128)S(1)} %hand.1.refs_1_), channel_id=1, source_target_pairs={{0,1},{1,0},{2,3},{3,2},{4,5},{5,4},{6,7},{7,6},{8,9},{9,8},{10,11... | collective-permute-start | bytes 49160 | tf_op jit(solution)/shard_map/ppermute | solution.py:22
  26.9 4.7 %collective-permute-start.13 = (f32[32,128]{1,0:T(8,128)S(1)}, f32[32,128]{1,0:T(8,128)S(1)}, u32[]{:S(2)}, u32[]{:S(2)}) collective-permute-start(f32[32,128]{1,0:T(8,128)S(1)} %sum.1.refs_2_), channel_id=1, source_target_pairs={{0,4},{1,7},{2,6},{3,5},{4,0},{5,3},{6,2},{7,1},{8,12},{9,15},{10,... | collective-permute-start | bytes 49160 | tf_op jit(solution)/shard_map/ppermute | solution.py:27
  28.9 3.2 %collective-permute-start.15 = (f32[32,128]{1,0:T(8,128)S(1)}, f32[32,128]{1,0:T(8,128)S(1)}, u32[]{:S(2)}, u32[]{:S(2)}) collective-permute-start(f32[32,128]{1,0:T(8,128)S(1)} %sum.1.refs_2_), channel_id=1, source_target_pairs={{0,3},{1,2},{2,1},{3,0},{4,7},{5,6},{6,5},{7,4},{8,11},{9,10},{10,... | collective-permute-start | bytes 49160 | tf_op jit(solution)/shard_map/ppermute | solution.py:22
  31.6 1.2 %collective-permute-start.14 = (f32[32,128]{1,0:T(8,128)S(1)}, f32[32,128]{1,0:T(8,128)S(1)}, u32[]{:S(2)}, u32[]{:S(2)}) collective-permute-start(f32[32,128]{1,0:T(8,128)S(1)} %collective-permute-done.13.refs_1_), channel_id=1, source_target_pairs={{0,1},{1,0},{2,3},{3,2},{4,5},{5,4},{6,7},{7,6},{8,9},{9,8},{10,11... | collective-permute-start | bytes 49160 | tf_op jit(solution)/shard_map/ppermute | solution.py:22

commit v7 on v6

--- a/solution.py
+++ b/solution.py
@@ -12,6 +12,7 @@
 SMEM = pl.BlockSpec(memory_space=pltpu.SMEM)
 EXACT = lax.Precision.HIGHEST
 PANEL = 16
+DUTY, MID = (1, 3), 2
 
 
 def swap(x, row, col):
@@ -35,6 +36,14 @@
         low *= 4
 
 
+def place_of(block, mate, core, chips):
+    if chips != 4:
+        return block + mate * chips
+    duty = jnp.where(core == 0, *DUTY)
+    shared = jnp.where(block == duty, mate, 5 - mate)
+    return jnp.where(block == 0, 3 + 4 * mate, jnp.where(block == MID, 2 + 4 * mate, shared))
+
+
 def mark_kernel(out):
     out[...] = jnp.zeros_like(out)
 
@@ -43,7 +52,7 @@
     me_row, me_col = lax.axis_index("row"), lax.axis_index("col")
     n_col = lax.axis_size("col")
     apart = coords[0:1, :] ^ me_col
-    place = (apart & 1) * (n_col // 2) + (apart >> 1)
+    place = place_of(apart >> 1, apart & 1, me_col & 1, n_col // 2)
     slot = lax.broadcasted_iota(jnp.int32, apart.shape, 1)
     select[0:1, :] = jnp.where(slot < counts[0], place, n_col)
     select[1:2, :] = coords[1:2, :] ^ me_row
@@ -176,8 +185,12 @@
     )(select, turned, x_block, *pieces)
 
     chip = keep + swap(send, 0, 1)
-    far = sorted(range(1, chips), key=lambda k: (k != 2, k))
-    parts = [chip[0]] + [swap(chip[k], 0, 2 * k) for k in far]
+    if chips == 4:
+        came = split_swap(chip[:2], 2 * DUTY[0], 2 * DUTY[1])
+        mid = swap(chip[2], 0, 2 * MID)
+        parts = [swap(came[1], 0, 1), came[0], chip[3], mid]
+    else:
+        parts = [chip[0]] + [swap(chip[k], 0, 2 * k) for k in range(1, chips)]
     y, gram = pl.pallas_call(
         functools.partial(gram_kernel, 1.0 / (width * n_row * n_col)),
         out_shape=(

time: 34.9 us -> 34.8 us (level)
  starting transfers between devices: 15.5 us -> 14.4 us
  waiting for transfers between devices: 13.9 us -> 14.9 us
    ppermute x1 -> x2, waiting for transfers between devices: 2.43 us -> 5.54 us  [split_swap(): lax.ppermute(x, 'col', [(j, j ^ (second if j & 1 else first)) for j in ra...]
    ppermute x15 -> x14, waiting for transfers between devices: 11.4 us -> 9.32 us  [swap(): return lax.ppermute(x, ('row', 'col'), pairs)]
    ppermute x15 -> x14, starting transfers between devices: 13.4 us -> 11.6 us  [swap(): return lax.ppermute(x, ('row', 'col'), pairs)]
    ppermute x1 -> x2, starting transfers between devices: 2.04 us -> 2.84 us  [split_swap(): lax.ppermute(x, 'col', [(j, j ^ (second if j & 1 else first)) for j in ra...]
  transfers between devices with their start and end apart: 16 -> 16, of which waited for: 12 -> 10; matrix products, arithmetic and copies ran while one was open for 0% -> 0% of each run, Pallas kernels for 3% -> 3%
where the time goes in v7:
time: 34.8 us; the launch traced here: 34.7 us
  waiting for transfers between devices  14.9 us (43%)
  starting transfers between devices  14.4 us (41%)
  Pallas kernels  3.97 us (11%)
  between operations  1.38 us (4%)
    ppermute x14, starting transfers between devices, swap(): return lax.ppermute(x, ('row', 'col'), pairs)  11.6 us
    ppermute x14, waiting for transfers between devices, swap(): return lax.ppermute(x, ('row', 'col'), pairs)  9.32 us
    ppermute x2, waiting for transfers between devices, split_swap(): lax.ppermute(x, 'col', [(j, j ^ (second if j & 1 else first)) for j in ra...  5.54 us
    ppermute x2, starting transfers between devices, split_swap(): lax.ppermute(x, 'col', [(j, j ^ (second if j & 1 else first)) for j in ra...  2.84 us
    pallas_call x1, Pallas kernels, local(): pl.pallas_call(factor_kernel, out_shape=(jax.ShapeDtypeStruct((vectors, w...  2 us
    pallas_call x1, Pallas kernels, local(): pl.pallas_call(turn_kernel, out_shape=jax.ShapeDtypeStruct(tiles.shape[:1...  0.86 us
    pallas_call x1, Pallas kernels, local(): pl.pallas_call(functools.partial(product_kernel, (0, *order)), out_shape=...  0.79 us
  transfers between devices with their start and end apart: 16, of which 10 were waited for; matrix products, arithmetic and copies ran while one was open for 0% of the time, Pallas kernels for 3%

profile of v7, /device:TPU:0, one launch (start us, length us, event | category | flops | bytes accessed | tf_op | source)
XLA Modules:
  0.0 34.7 jit_solution(14814380341488625951)
XLA Ops:
  0.6 0.5 %collective-permute-start.1 = (bf16[64,256]{1,0:T(8,128)(2,1)}, bf16[64,256]{1,0:T(8,128)(2,1)S(1)}, u32[]{:S(2)}, u32[]{:S(2)}) collective-permute-start(bf16[64,256]{1,0:T(8,128)(2,1)} %refs_0_.1), channel_id=1, source_target_pairs={{0,1},{1,0},{2,3},{3,2},{4,5},{5,4},{6,7},{7,6},{8,9},{9,8},{10,11... | collective-permute-start | bytes 98312 | tf_op jit(solution)/shard_map/ppermute | solution.py:23
  1.2 3.5 %collective-permute-start = (bf16[64,256]{1,0:T(8,128)(2,1)}, bf16[64,256]{1,0:T(8,128)(2,1)S(1)}, u32[]{:S(2)}, u32[]{:S(2)}) collective-permute-start(bf16[64,256]{1,0:T(8,128)(2,1)} %refs_0_.1), channel_id=1, source_target_pairs={{0,24},{1,25},{2,26},{3,27},{4,28},{5,29},{6,30},{7,31},{8,16},{9,... | collective-permute-start | bytes 98312 | tf_op jit(solution)/shard_map/ppermute | solution.py:23
  4.7 0.5 %collective-permute-start.3 = (bf16[64,256]{1,0:T(8,128)(2,1)}, bf16[64,256]{1,0:T(8,128)(2,1)S(1)}, u32[]{:S(2)}, u32[]{:S(2)}) collective-permute-start(bf16[64,256]{1,0:T(8,128)(2,1)} %refs_0_.1), channel_id=1, source_target_pairs={{0,16},{1,17},{2,18},{3,19},{4,20},{5,21},{6,22},{7,23},{8,24},{9,... | collective-permute-start | bytes 98312 | tf_op jit(solution)/shard_map/ppermute | solution.py:23
  5.2 0.1 collective-permute-start.2
  5.3 0.9 %turn.1.turned = bf16[24,256,256]{2,1,0:T(8,128)(2,1)S(1)} custom-call(bf16[24,256,256]{2,1,0:T(8,128)(2,1)S(1)} %copy-done), custom_call_target="tpu_custom_call" | custom-call | flops 1000000000 | tf_op jit(solution)/shard_map/turn/pallas_call | solution.py:164
  6.8 0.0 collective-permute-done.refs_1_
  6.9 1.9 %collective-permute-done.3.refs_3_ = bf16[64,256]{1,0:T(8,128)(2,1)S(1)} collective-permute-done((bf16[64,256]{1,0:T(8,128)(2,1)}, bf16[64,256]{1,0:T(8,128)(2,1)S(1)}, u32[]{:S(2)}, u32[]{:S(2)}) %collective-permute-start.3) | collective-permute-done | bytes 32800 | tf_op jit(solution)/shard_map/ppermute | solution.py:23
  8.8 0.1 collective-permute-done.2.refs_2_
  8.9 0.8 %product.1 = (f32[4,64,256]{2,1,0:T(8,128)S(1)}, f32[4,64,256]{2,1,0:T(8,128)S(1)}) custom-call(s32[2,24]{1,0:T(2,128)S(1)} %select.1, bf16[24,256,256]{2,1,0:T(8,128)(2,1)S(1)} %turn.1.turned, bf16[64,256]{1,0:T(8,128)(2,1)S(1)} %copy-done.1, bf16[64,256]{1,0:T(8,128)(2,1)S(1)} %collective-permute-done.refs_1_, ...), custom_call_target="tpu_custom_call" | custom-call | tf_op jit(solution)/shard_map/product/pallas_call | solution.py:174
  9.7 0.2 collective-permute-start.4
  9.9 1.4 %collective-permute-done.4 = f32[4,64,256]{2,1,0:T(8,128)S(1)} collective-permute-done((f32[4,64,256]{2,1,0:T(8,128)S(1)}, f32[4,64,256]{2,1,0:T(8,128)S(1)}, u32[]{:S(2)}, u32[]{:S(2)}) %collective-permute-start.4) | collective-permute-done | bytes 262176 | tf_op jit(solution)/shard_map/ppermute | solution.py:23
  11.3 1.6 %collective-permute-start.5 = (f32[2,64,256]{2,1,0:T(8,128)S(1)}, f32[2,64,256]{2,1,0:T(8,128)S(1)}, u32[]{:S(2)}, u32[]{:S(2)}) collective-permute-start(f32[2,64,256]{2,1,0:T(8,128)S(1)} %slice.20), channel_id=1, source_target_pairs={{0,2},{1,7},{2,0},{3,5},{4,6},{5,3},{6,4},{7,1},{8,10},{9,15},{10,... | collective-permute-start | bytes 393224 | tf_op jit(solution)/shard_map/ppermute | solution.py:28
  13.0 2.7 %collective-permute-start.7 = (f32[64,256]{1,0:T(8,128)S(1)}, f32[64,256]{1,0:T(8,128)S(1)}, u32[]{:S(2)}, u32[]{:S(2)}) collective-permute-start(f32[64,256]{1,0:T(8,128)S(1)} %get-tuple-element.14), channel_id=1, source_target_pairs={{0,4},{1,5},{2,6},{3,7},{4,0},{5,1},{6,2},{7,3},{8,12},{9,13},{10,... | collective-permute-start | bytes 196616 | tf_op jit(solution)/shard_map/ppermute | solution.py:23
  15.7 2.0 %collective-permute-done.5 = f32[2,64,256]{2,1,0:T(8,128)S(1)} collective-permute-done((f32[2,64,256]{2,1,0:T(8,128)S(1)}, f32[2,64,256]{2,1,0:T(8,128)S(1)}, u32[]{:S(2)}, u32[]{:S(2)}) %collective-permute-start.5) | collective-permute-done | bytes 131104 | tf_op jit(solution)/shard_map/ppermute | solution.py:28
  17.7 0.1 collective-permute-start.6
  17.8 2.8 %collective-permute-done.7.refs_3_ = f32[64,256]{1,0:T(8,128)S(1)} collective-permute-done((f32[64,256]{1,0:T(8,128)S(1)}, f32[64,256]{1,0:T(8,128)S(1)}, u32[]{:S(2)}, u32[]{:S(2)}) %collective-permute-start.7) | collective-permute-done | bytes 65568 | tf_op jit(solution)/shard_map/ppermute | solution.py:23
  20.6 0.3 gram.1
  20.9 0.1 collective-permute-start.9
  21.0 1.5 %collective-permute-start.8 = (f32[32,128]{1,0:T(8,128)S(1)}, f32[32,128]{1,0:T(8,128)S(1)}, u32[]{:S(2)}, u32[]{:S(2)}) collective-permute-start(f32[32,128]{1,0:T(8,128)S(1)} %get-tuple-element.13), channel_id=1, source_target_pairs={{0,25},{1,24},{2,27},{3,26},{4,29},{5,28},{6,31},{7,30},{8,17},{9,... | collective-permute-start | bytes 49160 | tf_op jit(solution)/shard_map/ppermute | solution.py:23
  22.5 0.9 %collective-permute-start.12 = (f32[32,128]{1,0:T(8,128)S(1)}, f32[32,128]{1,0:T(8,128)S(1)}, u32[]{:S(2)}, u32[]{:S(2)}) collective-permute-start(f32[32,128]{1,0:T(8,128)S(1)} %add.7._.refs_2_), channel_id=1, source_target_pairs={{0,17},{1,16},{2,19},{3,18},{4,21},{5,20},{6,23},{7,22},{8,25},{9,... | collective-permute-start | bytes 49160 | tf_op jit(solution)/shard_map/ppermute | solution.py:23
  23.4 0.9 %collective-permute-start.11 = (f32[32,128]{1,0:T(8,128)S(1)}, f32[32,128]{1,0:T(8,128)S(1)}, u32[]{:S(2)}, u32[]{:S(2)}) collective-permute-start(f32[32,128]{1,0:T(8,128)S(1)} %add.7._.refs_2_), channel_id=1, source_target_pairs={{0,9},{1,8},{2,11},{3,10},{4,13},{5,12},{6,15},{7,14},{8,1},{9,0},... | collective-permute-start | bytes 49160 | tf_op jit(solution)/shard_map/ppermute | solution.py:23
  24.3 0.8 %collective-permute-done.8.came = f32[32,128]{1,0:T(8,128)S(1)} collective-permute-done((f32[32,128]{1,0:T(8,128)S(1)}, f32[32,128]{1,0:T(8,128)S(1)}, u32[]{:S(2)}, u32[]{:S(2)}) %collective-permute-start.8) | collective-permute-done | bytes 16416 | tf_op jit(solution)/shard_map/ppermute | solution.py:23
  25.1 0.4 %collective-permute-start.10 = (f32[32,128]{1,0:T(8,128)S(1)}, f32[32,128]{1,0:T(8,128)S(1)}, u32[]{:S(2)}, u32[]{:S(2)}) collective-permute-start(f32[32,128]{1,0:T(8,128)S(1)} %hand.1.refs_1_), channel_id=1, source_target_pairs={{0,1},{1,0},{2,3},{3,2},{4,5},{5,4},{6,7},{7,6},{8,9},{9,8},{10,11... | collective-permute-start | bytes 49160 | tf_op jit(solution)/shard_map/ppermute | solution.py:23
  25.5 0.3 collective-permute-done.12.refs_4_
  25.8 0.7 %collective-permute-done.11.refs_3_ = f32[32,128]{1,0:T(8,128)S(1)} collective-permute-done((f32[32,128]{1,0:T(8,128)S(1)}, f32[32,128]{1,0:T(8,128)S(1)}, u32[]{:S(2)}, u32[]{:S(2)}) %collective-permute-start.11) | collective-permute-done | bytes 16416 | tf_op jit(solution)/shard_map/ppermute | solution.py:23
  26.5 0.0 collective-permute-done.10.refs_0_
  26.5 1.2 %collective-permute-start.13 = (f32[32,128]{1,0:T(8,128)S(1)}, f32[32,128]{1,0:T(8,128)S(1)}, u32[]{:S(2)}, u32[]{:S(2)}) collective-permute-start(f32[32,128]{1,0:T(8,128)S(1)} %sum.1.refs_2_), channel_id=1, source_target_pairs={{0,4},{1,7},{2,6},{3,5},{4,0},{5,3},{6,2},{7,1},{8,12},{9,15},{10,... | collective-permute-start | bytes 49160 | tf_op jit(solution)/shard_map/ppermute | solution.py:28
  27.7 0.2 collective-permute-start.15
  28.0 3.5 %collective-permute-done.13.refs_1_ = f32[32,128]{1,0:T(8,128)S(1)} collective-permute-done((f32[32,128]{1,0:T(8,128)S(1)}, f32[32,128]{1,0:T(8,128)S(1)}, u32[]{:S(2)}, u32[]{:S(2)}) %collective-permute-start.13) | collective-permute-done | bytes 16416 | tf_op jit(solution)/shard_map/ppermute | solution.py:28
  31.5 0.0 collective-permute-done.15.refs_3_
  31.5 1.2 %collective-permute-done.14.refs_0_ = f32[32,128]{1,0:T(8,128)S(1)} collective-permute-done((f32[32,128]{1,0:T(8,128)S(1)}, f32[32,128]{1,0:T(8,128)S(1)}, u32[]{:S(2)}, u32[]{:S(2)}) %collective-permute-start.14) | collective-permute-done | bytes 16416 | tf_op jit(solution)/shard_map/ppermute | solution.py:23
  32.7 2.0 %factor.1 = (f32[64,256]{1,0:T(8,128)}, f32[64,64]{1,0:T(8,128)}) custom-call(f32[64,256]{1,0:T(8,128)S(1)} %get-tuple-element.12.y_ref, f32[32,128]{1,0:T(8,128)S(1)} %collective-permute-done.14.refs_0_, f32[32,128]{1,0:T(8,128)S(1)} %collective-permute-done.13.refs_1_, f32[32,128]{1,0:T(8,128)S(1)} %sum.1.refs_2_, ...), custom_call_target="tpu_custom_call" | custom-call | tf_op jit(solution)/shard_map/factor/pallas_call | solution.py:234
  (19 shorter events, 0.1 us)
Async XLA Ops:
  0.6 4.7 %copy-start = (bf16[24,256,256]{2,1,0:T(8,128)(2,1)S(1)}, bf16[24,256,256]{2,1,0:T(8,128)(2,1)}, u32[]{:S(2)}) copy-start(bf16[24,256,256]{2,1,0:T(8,128)(2,1)} %tiles.1) | copy-start | bytes 9437188
  0.6 4.6 %collective-permute-start.1 = (bf16[64,256]{1,0:T(8,128)(2,1)}, bf16[64,256]{1,0:T(8,128)(2,1)S(1)}, u32[]{:S(2)}, u32[]{:S(2)}) collective-permute-start(bf16[64,256]{1,0:T(8,128)(2,1)} %refs_0_.1), channel_id=1, source_target_pairs={{0,1},{1,0},{2,3},{3,2},{4,5},{5,4},{6,7},{7,6},{8,9},{9,8},{10,11... | collective-permute-start | bytes 98312 | tf_op jit(solution)/shard_map/ppermute | solution.py:23
  1.2 5.7 %collective-permute-start = (bf16[64,256]{1,0:T(8,128)(2,1)}, bf16[64,256]{1,0:T(8,128)(2,1)S(1)}, u32[]{:S(2)}, u32[]{:S(2)}) collective-permute-start(bf16[64,256]{1,0:T(8,128)(2,1)} %refs_0_.1), channel_id=1, source_target_pairs={{0,24},{1,25},{2,26},{3,27},{4,28},{5,29},{6,30},{7,31},{8,16},{9,... | collective-permute-start | bytes 98312 | tf_op jit(solution)/shard_map/ppermute | solution.py:23
  4.7 4.1 %collective-permute-start.3 = (bf16[64,256]{1,0:T(8,128)(2,1)}, bf16[64,256]{1,0:T(8,128)(2,1)S(1)}, u32[]{:S(2)}, u32[]{:S(2)}) collective-permute-start(bf16[64,256]{1,0:T(8,128)(2,1)} %refs_0_.1), channel_id=1, source_target_pairs={{0,16},{1,17},{2,18},{3,19},{4,20},{5,21},{6,22},{7,23},{8,24},{9,... | collective-permute-start | bytes 98312 | tf_op jit(solution)/shard_map/ppermute | solution.py:23
  5.2 1.6 %copy-start.2 = (s32[24,2]{0,1:T(2,128)S(1)}, s32[24,2]{0,1:T(2,128)}, u32[]{:S(2)}) copy-start(s32[24,2]{0,1:T(2,128)} %param.6) | copy-start | bytes 580
  5.2 3.7 %copy-start.1 = (bf16[64,256]{1,0:T(8,128)(2,1)S(1)}, bf16[64,256]{1,0:T(8,128)(2,1)}, u32[]{:S(2)}) copy-start(bf16[64,256]{1,0:T(8,128)(2,1)} %refs_0_.1) | copy-start | bytes 98308
  5.2 3.7 %collective-permute-start.2 = (bf16[64,256]{1,0:T(8,128)(2,1)S(1)}, bf16[64,256]{1,0:T(8,128)(2,1)S(1)}, u32[]{:S(2)}, u32[]{:S(2)}) collective-permute-start(bf16[64,256]{1,0:T(8,128)(2,1)S(1)} %collective-permute-done.1), channel_id=1, source_target_pairs={{0,9},{1,8},{2,11},{3,10},{4,13},{5,12},{6,15},{7,14},{8,1},{9,0},... | collective-permute-start | bytes 98312 | tf_op jit(solution)/shard_map/ppermute | solution.py:23
  9.7 1.6 %collective-permute-start.4 = (f32[4,64,256]{2,1,0:T(8,128)S(1)}, f32[4,64,256]{2,1,0:T(8,128)S(1)}, u32[]{:S(2)}, u32[]{:S(2)}) collective-permute-start(f32[4,64,256]{2,1,0:T(8,128)S(1)} %get-tuple-element.11), channel_id=1, source_target_pairs={{0,1},{1,0},{2,3},{3,2},{4,5},{5,4},{6,7},{7,6},{8,9},{9,8},{10,11... | collective-permute-start | bytes 786440 | tf_op jit(solution)/shard_map/ppermute | solution.py:23
  11.3 6.3 %collective-permute-start.5 = (f32[2,64,256]{2,1,0:T(8,128)S(1)}, f32[2,64,256]{2,1,0:T(8,128)S(1)}, u32[]{:S(2)}, u32[]{:S(2)}) collective-permute-start(f32[2,64,256]{2,1,0:T(8,128)S(1)} %slice.20), channel_id=1, source_target_pairs={{0,2},{1,7},{2,0},{3,5},{4,6},{5,3},{6,4},{7,1},{8,10},{9,15},{10,... | collective-permute-start | bytes 393224 | tf_op jit(solution)/shard_map/ppermute | solution.py:28
  13.0 7.6 %collective-permute-start.7 = (f32[64,256]{1,0:T(8,128)S(1)}, f32[64,256]{1,0:T(8,128)S(1)}, u32[]{:S(2)}, u32[]{:S(2)}) collective-permute-start(f32[64,256]{1,0:T(8,128)S(1)} %get-tuple-element.14), channel_id=1, source_target_pairs={{0,4},{1,5},{2,6},{3,7},{4,0},{5,1},{6,2},{7,3},{8,12},{9,13},{10,... | collective-permute-start | bytes 196616 | tf_op jit(solution)/shard_map/ppermute | solution.py:23
  17.7 2.9 %collective-permute-start.6 = (f32[64,256]{1,0:T(8,128)S(1)}, f32[64,256]{1,0:T(8,128)S(1)}, u32[]{:S(2)}, u32[]{:S(2)}) collective-permute-start(f32[64,256]{1,0:T(8,128)S(1)} %get-tuple-element.17), channel_id=1, source_target_pairs={{0,1},{1,0},{2,3},{3,2},{4,5},{5,4},{6,7},{7,6},{8,9},{9,8},{10,11... | collective-permute-start | bytes 196616 | tf_op jit(solution)/shard_map/ppermute | solution.py:23
  20.9 1.6 %collective-permute-start.9 = (f32[32,128]{1,0:T(8,128)S(1)}, f32[32,128]{1,0:T(8,128)S(1)}, u32[]{:S(2)}, u32[]{:S(2)}) collective-permute-start(f32[32,128]{1,0:T(8,128)S(1)} %get-tuple-element.13), channel_id=1, source_target_pairs={{0,1},{1,0},{2,3},{3,2},{4,5},{5,4},{6,7},{7,6},{8,9},{9,8},{10,11... | collective-permute-start | bytes 49160 | tf_op jit(solution)/shard_map/ppermute | solution.py:23
  21.0 4.1 %collective-permute-start.8 = (f32[32,128]{1,0:T(8,128)S(1)}, f32[32,128]{1,0:T(8,128)S(1)}, u32[]{:S(2)}, u32[]{:S(2)}) collective-permute-start(f32[32,128]{1,0:T(8,128)S(1)} %get-tuple-element.13), channel_id=1, source_target_pairs={{0,25},{1,24},{2,27},{3,26},{4,29},{5,28},{6,31},{7,30},{8,17},{9,... | collective-permute-start | bytes 49160 | tf_op jit(solution)/shard_map/ppermute | solution.py:23
  22.5 3.3 %collective-permute-start.12 = (f32[32,128]{1,0:T(8,128)S(1)}, f32[32,128]{1,0:T(8,128)S(1)}, u32[]{:S(2)}, u32[]{:S(2)}) collective-permute-start(f32[32,128]{1,0:T(8,128)S(1)} %add.7._.refs_2_), channel_id=1, source_target_pairs={{0,17},{1,16},{2,19},{3,18},{4,21},{5,20},{6,23},{7,22},{8,25},{9,... | collective-permute-start | bytes 49160 | tf_op jit(solution)/shard_map/ppermute | solution.py:23
  23.4 3.2 %collective-permute-start.11 = (f32[32,128]{1,0:T(8,128)S(1)}, f32[32,128]{1,0:T(8,128)S(1)}, u32[]{:S(2)}, u32[]{:S(2)}) collective-permute-start(f32[32,128]{1,0:T(8,128)S(1)} %add.7._.refs_2_), channel_id=1, source_target_pairs={{0,9},{1,8},{2,11},{3,10},{4,13},{5,12},{6,15},{7,14},{8,1},{9,0},... | collective-permute-start | bytes 49160 | tf_op jit(solution)/shard_map/ppermute | solution.py:23
  25.1 1.4 %collective-permute-start.10 = (f32[32,128]{1,0:T(8,128)S(1)}, f32[32,128]{1,0:T(8,128)S(1)}, u32[]{:S(2)}, u32[]{:S(2)}) collective-permute-start(f32[32,128]{1,0:T(8,128)S(1)} %hand.1.refs_1_), channel_id=1, source_target_pairs={{0,1},{1,0},{2,3},{3,2},{4,5},{5,4},{6,7},{7,6},{8,9},{9,8},{10,11... | collective-permute-start | bytes 49160 | tf_op jit(solution)/shard_map/ppermute | solution.py:23
  26.5 5.0 %collective-permute-start.13 = (f32[32,128]{1,0:T(8,128)S(1)}, f32[32,128]{1,0:T(8,128)S(1)}, u32[]{:S(2)}, u32[]{:S(2)}) collective-permute-start(f32[32,128]{1,0:T(8,128)S(1)} %sum.1.refs_2_), channel_id=1, source_target_pairs={{0,4},{1,7},{2,6},{3,5},{4,0},{5,3},{6,2},{7,1},{8,12},{9,15},{10,... | collective-permute-start | bytes 49160 | tf_op jit(solution)/shard_map/ppermute | solution.py:28
  27.7 3.8 %collective-permute-start.15 = (f32[32,128]{1,0:T(8,128)S(1)}, f32[32,128]{1,0:T(8,128)S(1)}, u32[]{:S(2)}, u32[]{:S(2)}) collective-permute-start(f32[32,128]{1,0:T(8,128)S(1)} %sum.1.refs_2_), channel_id=1, source_target_pairs={{0,3},{1,2},{2,1},{3,0},{4,7},{5,6},{6,5},{7,4},{8,11},{9,10},{10,... | collective-permute-start | bytes 49160 | tf_op jit(solution)/shard_map/ppermute | solution.py:23
  31.5 1.2 %collective-permute-start.14 = (f32[32,128]{1,0:T(8,128)S(1)}, f32[32,128]{1,0:T(8,128)S(1)}, u32[]{:S(2)}, u32[]{:S(2)}) collective-permute-start(f32[32,128]{1,0:T(8,128)S(1)} %collective-permute-done.13.refs_1_), channel_id=1, source_target_pairs={{0,1},{1,0},{2,3},{3,2},{4,5},{5,4},{6,7},{7,6},{8,9},{9,8},{10,11... | collective-permute-start | bytes 49160 | tf_op jit(solution)/shard_map/ppermute | solution.py:23

commit v8 on v7

--- a/solution.py
+++ b/solution.py
@@ -64,15 +64,16 @@
 
 
 def product_kernel(order, select, turned, *refs):
-    pieces, (keep, send, x_all, rows) = refs[: len(order)], refs[len(order) :]
+    pieces, outs, (x_all, rows) = refs[: len(order)], refs[len(order) : -2], refs[-2:]
     for k, piece in zip(order, pieces):
         x_all[k] = piece[...]
     rows[...] = jnp.zeros_like(rows)
     for s in range(turned.shape[0]):
         rows[select[0, s]] += jnp.dot(x_all[select[1, s]], turned[s], preferred_element_type=F32)
-    half = keep.shape[0]
-    keep[...] = rows[:half]
-    send[...] = rows[half : 2 * half]
+    at = 0
+    for out in outs:
+        out[...] = rows[at : at + out.shape[0]]
+        at += out.shape[0]
 
 
 def gram_kernel(scale, *refs):
@@ -170,12 +171,12 @@
         cost_estimate=pl.CostEstimate(flops=10**9, bytes_accessed=0, transcendentals=0),
         name="turn",
     )(tiles)
-    part = jax.ShapeDtypeStruct((chips, vectors, width), F32)
-    keep, send = pl.pallas_call(
+    part = jax.ShapeDtypeStruct((chips // 2, vectors, width), F32)
+    keep_first, keep_rest, send_first, send_rest = pl.pallas_call(
         functools.partial(product_kernel, (0, *order)),
-        out_shape=(part, part),
+        out_shape=(part,) * 4,
         in_specs=[VMEM] * (2 + n_row),
-        out_specs=(VMEM, VMEM),
+        out_specs=(VMEM,) * 4,
         scratch_shapes=[
             pltpu.VMEM((n_row, vectors, width), x_block.dtype),
             pltpu.VMEM((n_col + 1, vectors, width), F32),
@@ -184,12 +185,14 @@
         name="product",
     )(select, turned, x_block, *pieces)
 
-    chip = keep + swap(send, 0, 1)
+    first = keep_first + swap(send_first, 0, 1)
+    rest = keep_rest + swap(send_rest, 0, 1)
     if chips == 4:
-        came = split_swap(chip[:2], 2 * DUTY[0], 2 * DUTY[1])
-        mid = swap(chip[2], 0, 2 * MID)
-        parts = [swap(came[1], 0, 1), came[0], chip[3], mid]
+        came = split_swap(first, 2 * DUTY[0], 2 * DUTY[1])
+        mid = swap(rest[0], 0, 2 * MID)
+        parts = [swap(came[1], 0, 1), came[0], rest[1], mid]
     else:
+        chip = [*first, *rest]
         parts = [chip[0]] + [swap(chip[k], 0, 2 * k) for k in range(1, chips)]
     y, gram = pl.pallas_call(
         functools.partial(gram_kernel, 1.0 / (width * n_row * n_col)),

time: 34.8 us -> 34.6 us (level)
  waiting for transfers between devices: 14.9 us -> 14 us
  starting transfers between devices: 14.4 us -> 15 us
    ppermute x14 -> x15, waiting for transfers between devices: 9.32 us -> 8.61 us  [swap(): return lax.ppermute(x, ('row', 'col'), pairs)]
    ppermute x14 -> x15, starting transfers between devices: 11.6 us -> 12.1 us  [swap(): return lax.ppermute(x, ('row', 'col'), pairs)]
  transfers between devices with their start and end apart: 16 -> 17, of which waited for: 10 -> 10; matrix products, arithmetic and copies ran while one was open for 0% -> 0% of each run, Pallas kernels for 3% -> 3%
where the time goes in v8:
time: 34.6 us; the launch traced here: 34.5 us
  starting transfers between devices  15 us (43%)
  waiting for transfers between devices  14 us (40%)
  Pallas kernels  3.97 us (11%)
  between operations  1.38 us (4%)
    ppermute x15, starting transfers between devices, swap(): return lax.ppermute(x, ('row', 'col'), pairs)  12.1 us
    ppermute x15, waiting for transfers between devices, swap(): return lax.ppermute(x, ('row', 'col'), pairs)  8.61 us
    ppermute x2, waiting for transfers between devices, split_swap(): lax.ppermute(x, 'col', [(j, j ^ (second if j & 1 else first)) for j in ra...  5.44 us
    ppermute x2, starting transfers between devices, split_swap(): lax.ppermute(x, 'col', [(j, j ^ (second if j & 1 else first)) for j in ra...  2.89 us
    pallas_call x1, Pallas kernels, local(): pl.pallas_call(factor_kernel, out_shape=(jax.ShapeDtypeStruct((vectors, w...  2 us
    pallas_call x1, Pallas kernels, local(): pl.pallas_call(turn_kernel, out_shape=jax.ShapeDtypeStruct(tiles.shape[:1...  0.86 us
    pallas_call x1, Pallas kernels, local(): pl.pallas_call(functools.partial(product_kernel, (0, *order)), out_shape=...  0.79 us
  transfers between devices with their start and end apart: 17, of which 10 were waited for; matrix products, arithmetic and copies ran while one was open for 0% of the time, Pallas kernels for 3%

profile of v8, /device:TPU:0, one launch (start us, length us, event | category | flops | bytes accessed | tf_op | source)
XLA Modules:
  0.0 34.5 jit_solution(15653599073888805637)
XLA Ops:
  0.6 0.5 %collective-permute-start.1 = (bf16[64,256]{1,0:T(8,128)(2,1)}, bf16[64,256]{1,0:T(8,128)(2,1)S(1)}, u32[]{:S(2)}, u32[]{:S(2)}) collective-permute-start(bf16[64,256]{1,0:T(8,128)(2,1)} %refs_0_.1), channel_id=1, source_target_pairs={{0,1},{1,0},{2,3},{3,2},{4,5},{5,4},{6,7},{7,6},{8,9},{9,8},{10,11... | collective-permute-start | bytes 98312 | tf_op jit(solution)/shard_map/ppermute | solution.py:23
  1.2 3.5 %collective-permute-start = (bf16[64,256]{1,0:T(8,128)(2,1)}, bf16[64,256]{1,0:T(8,128)(2,1)S(1)}, u32[]{:S(2)}, u32[]{:S(2)}) collective-permute-start(bf16[64,256]{1,0:T(8,128)(2,1)} %refs_0_.1), channel_id=1, source_target_pairs={{0,24},{1,25},{2,26},{3,27},{4,28},{5,29},{6,30},{7,31},{8,16},{9,... | collective-permute-start | bytes 98312 | tf_op jit(solution)/shard_map/ppermute | solution.py:23
  4.7 0.5 %collective-permute-start.3 = (bf16[64,256]{1,0:T(8,128)(2,1)}, bf16[64,256]{1,0:T(8,128)(2,1)S(1)}, u32[]{:S(2)}, u32[]{:S(2)}) collective-permute-start(bf16[64,256]{1,0:T(8,128)(2,1)} %refs_0_.1), channel_id=1, source_target_pairs={{0,16},{1,17},{2,18},{3,19},{4,20},{5,21},{6,22},{7,23},{8,24},{9,... | collective-permute-start | bytes 98312 | tf_op jit(solution)/shard_map/ppermute | solution.py:23
  5.2 0.1 collective-permute-start.2
  5.3 0.9 %turn.1.turned = bf16[24,256,256]{2,1,0:T(8,128)(2,1)S(1)} custom-call(bf16[24,256,256]{2,1,0:T(8,128)(2,1)S(1)} %copy-done), custom_call_target="tpu_custom_call" | custom-call | flops 1000000000 | tf_op jit(solution)/shard_map/turn/pallas_call | solution.py:165
  6.8 0.0 collective-permute-done.refs_1_
  6.9 1.9 %collective-permute-done.3.refs_3_ = bf16[64,256]{1,0:T(8,128)(2,1)S(1)} collective-permute-done((bf16[64,256]{1,0:T(8,128)(2,1)}, bf16[64,256]{1,0:T(8,128)(2,1)S(1)}, u32[]{:S(2)}, u32[]{:S(2)}) %collective-permute-start.3) | collective-permute-done | bytes 32800 | tf_op jit(solution)/shard_map/ppermute | solution.py:23
  8.8 0.1 collective-permute-done.2.refs_2_
  8.9 0.8 %product.1 = (f32[2,64,256]{2,1,0:T(8,128)S(1)}, f32[2,64,256]{2,1,0:T(8,128)S(1)}, f32[2,64,256]{2,1,0:T(8,128)S(1)}, f32[2,64,256]{2,1,0:T(8,128)S(1)}) custom-call(s32[2,24]{1,0:T(2,128)S(1)} %select.1, bf16[24,256,256]{2,1,0:T(8,128)(2,1)S(1)} %turn.1.turned, bf16[64,256]{1,0:T(8,128)(2,1)S(1)} %copy-done.1, ...), custom_call_target="tpu_custom_call" | custom-call | tf_op jit(solution)/shard_map/product/pallas_call | solution.py:175
  9.7 0.2 collective-permute-start.4
  9.9 0.4 %collective-permute-start.7 = (f32[2,64,256]{2,1,0:T(8,128)S(1)}, f32[2,64,256]{2,1,0:T(8,128)S(1)}, u32[]{:S(2)}, u32[]{:S(2)}) collective-permute-start(f32[2,64,256]{2,1,0:T(8,128)S(1)} %get-tuple-element.15), channel_id=1, source_target_pairs={{0,1},{1,0},{2,3},{3,2},{4,5},{5,4},{6,7},{7,6},{8,9},{9,8},{10,11... | collective-permute-start | bytes 393224 | tf_op jit(solution)/shard_map/ppermute | solution.py:23
  10.3 0.8 %collective-permute-done.4 = f32[2,64,256]{2,1,0:T(8,128)S(1)} collective-permute-done((f32[2,64,256]{2,1,0:T(8,128)S(1)}, f32[2,64,256]{2,1,0:T(8,128)S(1)}, u32[]{:S(2)}, u32[]{:S(2)}) %collective-permute-start.4) | collective-permute-done | bytes 131104 | tf_op jit(solution)/shard_map/ppermute | solution.py:23
  11.1 1.6 %collective-permute-start.5 = (f32[2,64,256]{2,1,0:T(8,128)S(1)}, f32[2,64,256]{2,1,0:T(8,128)S(1)}, u32[]{:S(2)}, u32[]{:S(2)}) collective-permute-start(f32[2,64,256]{2,1,0:T(8,128)S(1)} %add.9), channel_id=1, source_target_pairs={{0,2},{1,7},{2,0},{3,5},{4,6},{5,3},{6,4},{7,1},{8,10},{9,15},{10,... | collective-permute-start | bytes 393224 | tf_op jit(solution)/shard_map/ppermute | solution.py:28
  12.8 2.7 %collective-permute-start.8 = (f32[64,256]{1,0:T(8,128)S(1)}, f32[64,256]{1,0:T(8,128)S(1)}, u32[]{:S(2)}, u32[]{:S(2)}) collective-permute-start(f32[64,256]{1,0:T(8,128)S(1)} %get-tuple-element.18), channel_id=1, source_target_pairs={{0,4},{1,5},{2,6},{3,7},{4,0},{5,1},{6,2},{7,3},{8,12},{9,13},{10,... | collective-permute-start | bytes 196616 | tf_op jit(solution)/shard_map/ppermute | solution.py:23
  15.5 2.0 %collective-permute-done.5 = f32[2,64,256]{2,1,0:T(8,128)S(1)} collective-permute-done((f32[2,64,256]{2,1,0:T(8,128)S(1)}, f32[2,64,256]{2,1,0:T(8,128)S(1)}, u32[]{:S(2)}, u32[]{:S(2)}) %collective-permute-start.5) | collective-permute-done | bytes 131104 | tf_op jit(solution)/shard_map/ppermute | solution.py:28
  17.5 0.1 collective-permute-start.6
  17.6 2.8 %collective-permute-done.8.refs_3_ = f32[64,256]{1,0:T(8,128)S(1)} collective-permute-done((f32[64,256]{1,0:T(8,128)S(1)}, f32[64,256]{1,0:T(8,128)S(1)}, u32[]{:S(2)}, u32[]{:S(2)}) %collective-permute-start.8) | collective-permute-done | bytes 65568 | tf_op jit(solution)/shard_map/ppermute | solution.py:23
  20.3 0.0 collective-permute-done.6.refs_0_
  20.3 0.3 gram.1
  20.6 0.1 collective-permute-start.10
  20.8 1.5 %collective-permute-start.9 = (f32[32,128]{1,0:T(8,128)S(1)}, f32[32,128]{1,0:T(8,128)S(1)}, u32[]{:S(2)}, u32[]{:S(2)}) collective-permute-start(f32[32,128]{1,0:T(8,128)S(1)} %get-tuple-element.17), channel_id=1, source_target_pairs={{0,25},{1,24},{2,27},{3,26},{4,29},{5,28},{6,31},{7,30},{8,17},{9,... | collective-permute-start | bytes 49160 | tf_op jit(solution)/shard_map/ppermute | solution.py:23
  22.3 0.9 %collective-permute-start.13 = (f32[32,128]{1,0:T(8,128)S(1)}, f32[32,128]{1,0:T(8,128)S(1)}, u32[]{:S(2)}, u32[]{:S(2)}) collective-permute-start(f32[32,128]{1,0:T(8,128)S(1)} %add.11._.refs_2_), channel_id=1, source_target_pairs={{0,17},{1,16},{2,19},{3,18},{4,21},{5,20},{6,23},{7,22},{8,25},{9,... | collective-permute-start | bytes 49160 | tf_op jit(solution)/shard_map/ppermute | solution.py:23
  23.1 1.0 %collective-permute-start.12 = (f32[32,128]{1,0:T(8,128)S(1)}, f32[32,128]{1,0:T(8,128)S(1)}, u32[]{:S(2)}, u32[]{:S(2)}) collective-permute-start(f32[32,128]{1,0:T(8,128)S(1)} %add.11._.refs_2_), channel_id=1, source_target_pairs={{0,9},{1,8},{2,11},{3,10},{4,13},{5,12},{6,15},{7,14},{8,1},{9,0},... | collective-permute-start | bytes 49160 | tf_op jit(solution)/shard_map/ppermute | solution.py:23
  24.1 0.7 %collective-permute-done.9.came = f32[32,128]{1,0:T(8,128)S(1)} collective-permute-done((f32[32,128]{1,0:T(8,128)S(1)}, f32[32,128]{1,0:T(8,128)S(1)}, u32[]{:S(2)}, u32[]{:S(2)}) %collective-permute-start.9) | collective-permute-done | bytes 16416 | tf_op jit(solution)/shard_map/ppermute | solution.py:23
  24.8 0.4 %collective-permute-start.11 = (f32[32,128]{1,0:T(8,128)S(1)}, f32[32,128]{1,0:T(8,128)S(1)}, u32[]{:S(2)}, u32[]{:S(2)}) collective-permute-start(f32[32,128]{1,0:T(8,128)S(1)} %hand.1.refs_1_), channel_id=1, source_target_pairs={{0,1},{1,0},{2,3},{3,2},{4,5},{5,4},{6,7},{7,6},{8,9},{9,8},{10,11... | collective-permute-start | bytes 49160 | tf_op jit(solution)/shard_map/ppermute | solution.py:23
  25.3 0.3 collective-permute-done.13.refs_4_
  25.6 0.7 %collective-permute-done.12.refs_3_ = f32[32,128]{1,0:T(8,128)S(1)} collective-permute-done((f32[32,128]{1,0:T(8,128)S(1)}, f32[32,128]{1,0:T(8,128)S(1)}, u32[]{:S(2)}, u32[]{:S(2)}) %collective-permute-start.12) | collective-permute-done | bytes 16416 | tf_op jit(solution)/shard_map/ppermute | solution.py:23
  26.3 1.3 %collective-permute-start.14 = (f32[32,128]{1,0:T(8,128)S(1)}, f32[32,128]{1,0:T(8,128)S(1)}, u32[]{:S(2)}, u32[]{:S(2)}) collective-permute-start(f32[32,128]{1,0:T(8,128)S(1)} %sum.1.refs_2_), channel_id=1, source_target_pairs={{0,4},{1,7},{2,6},{3,5},{4,0},{5,3},{6,2},{7,1},{8,12},{9,15},{10,... | collective-permute-start | bytes 49160 | tf_op jit(solution)/shard_map/ppermute | solution.py:28
  27.6 0.2 collective-permute-start.16
  27.8 3.5 %collective-permute-done.14.refs_1_ = f32[32,128]{1,0:T(8,128)S(1)} collective-permute-done((f32[32,128]{1,0:T(8,128)S(1)}, f32[32,128]{1,0:T(8,128)S(1)}, u32[]{:S(2)}, u32[]{:S(2)}) %collective-permute-start.14) | collective-permute-done | bytes 16416 | tf_op jit(solution)/shard_map/ppermute | solution.py:28
  31.3 1.2 %collective-permute-done.15.refs_0_ = f32[32,128]{1,0:T(8,128)S(1)} collective-permute-done((f32[32,128]{1,0:T(8,128)S(1)}, f32[32,128]{1,0:T(8,128)S(1)}, u32[]{:S(2)}, u32[]{:S(2)}) %collective-permute-start.15) | collective-permute-done | bytes 16416 | tf_op jit(solution)/shard_map/ppermute | solution.py:23
  32.5 2.0 %factor.1 = (f32[64,256]{1,0:T(8,128)}, f32[64,64]{1,0:T(8,128)}) custom-call(f32[64,256]{1,0:T(8,128)S(1)} %get-tuple-element.16.y_ref, f32[32,128]{1,0:T(8,128)S(1)} %collective-permute-done.15.refs_0_, f32[32,128]{1,0:T(8,128)S(1)} %collective-permute-done.14.refs_1_, f32[32,128]{1,0:T(8,128)S(1)} %sum.1.refs_2_, ...), custom_call_target="tpu_custom_call" | custom-call | tf_op jit(solution)/shard_map/factor/pallas_call | solution.py:237
  (21 shorter events, 0.1 us)
Async XLA Ops:
  0.6 4.7 %copy-start = (bf16[24,256,256]{2,1,0:T(8,128)(2,1)S(1)}, bf16[24,256,256]{2,1,0:T(8,128)(2,1)}, u32[]{:S(2)}) copy-start(bf16[24,256,256]{2,1,0:T(8,128)(2,1)} %tiles.1) | copy-start | bytes 9437188
  0.6 4.6 %collective-permute-start.1 = (bf16[64,256]{1,0:T(8,128)(2,1)}, bf16[64,256]{1,0:T(8,128)(2,1)S(1)}, u32[]{:S(2)}, u32[]{:S(2)}) collective-permute-start(bf16[64,256]{1,0:T(8,128)(2,1)} %refs_0_.1), channel_id=1, source_target_pairs={{0,1},{1,0},{2,3},{3,2},{4,5},{5,4},{6,7},{7,6},{8,9},{9,8},{10,11... | collective-permute-start | bytes 98312 | tf_op jit(solution)/shard_map/ppermute | solution.py:23
  1.2 5.7 %collective-permute-start = (bf16[64,256]{1,0:T(8,128)(2,1)}, bf16[64,256]{1,0:T(8,128)(2,1)S(1)}, u32[]{:S(2)}, u32[]{:S(2)}) collective-permute-start(bf16[64,256]{1,0:T(8,128)(2,1)} %refs_0_.1), channel_id=1, source_target_pairs={{0,24},{1,25},{2,26},{3,27},{4,28},{5,29},{6,30},{7,31},{8,16},{9,... | collective-permute-start | bytes 98312 | tf_op jit(solution)/shard_map/ppermute | solution.py:23
  4.7 4.1 %collective-permute-start.3 = (bf16[64,256]{1,0:T(8,128)(2,1)}, bf16[64,256]{1,0:T(8,128)(2,1)S(1)}, u32[]{:S(2)}, u32[]{:S(2)}) collective-permute-start(bf16[64,256]{1,0:T(8,128)(2,1)} %refs_0_.1), channel_id=1, source_target_pairs={{0,16},{1,17},{2,18},{3,19},{4,20},{5,21},{6,22},{7,23},{8,24},{9,... | collective-permute-start | bytes 98312 | tf_op jit(solution)/shard_map/ppermute | solution.py:23
  5.2 1.6 %copy-start.2 = (s32[24,2]{0,1:T(2,128)S(1)}, s32[24,2]{0,1:T(2,128)}, u32[]{:S(2)}) copy-start(s32[24,2]{0,1:T(2,128)} %param.6) | copy-start | bytes 580
  5.2 3.7 %copy-start.1 = (bf16[64,256]{1,0:T(8,128)(2,1)S(1)}, bf16[64,256]{1,0:T(8,128)(2,1)}, u32[]{:S(2)}) copy-start(bf16[64,256]{1,0:T(8,128)(2,1)} %refs_0_.1) | copy-start | bytes 98308
  5.2 3.7 %collective-permute-start.2 = (bf16[64,256]{1,0:T(8,128)(2,1)S(1)}, bf16[64,256]{1,0:T(8,128)(2,1)S(1)}, u32[]{:S(2)}, u32[]{:S(2)}) collective-permute-start(bf16[64,256]{1,0:T(8,128)(2,1)S(1)} %collective-permute-done.1), channel_id=1, source_target_pairs={{0,9},{1,8},{2,11},{3,10},{4,13},{5,12},{6,15},{7,14},{8,1},{9,0},... | collective-permute-start | bytes 98312 | tf_op jit(solution)/shard_map/ppermute | solution.py:23
  9.7 1.4 %collective-permute-start.4 = (f32[2,64,256]{2,1,0:T(8,128)S(1)}, f32[2,64,256]{2,1,0:T(8,128)S(1)}, u32[]{:S(2)}, u32[]{:S(2)}) collective-permute-start(f32[2,64,256]{2,1,0:T(8,128)S(1)} %get-tuple-element.13), channel_id=1, source_target_pairs={{0,1},{1,0},{2,3},{3,2},{4,5},{5,4},{6,7},{7,6},{8,9},{9,8},{10,11... | collective-permute-start | bytes 393224 | tf_op jit(solution)/shard_map/ppermute | solution.py:23
  9.9 2.9 %collective-permute-start.7 = (f32[2,64,256]{2,1,0:T(8,128)S(1)}, f32[2,64,256]{2,1,0:T(8,128)S(1)}, u32[]{:S(2)}, u32[]{:S(2)}) collective-permute-start(f32[2,64,256]{2,1,0:T(8,128)S(1)} %get-tuple-element.15), channel_id=1, source_target_pairs={{0,1},{1,0},{2,3},{3,2},{4,5},{5,4},{6,7},{7,6},{8,9},{9,8},{10,11... | collective-permute-start | bytes 393224 | tf_op jit(solution)/shard_map/ppermute | solution.py:23
  11.1 6.3 %collective-permute-start.5 = (f32[2,64,256]{2,1,0:T(8,128)S(1)}, f32[2,64,256]{2,1,0:T(8,128)S(1)}, u32[]{:S(2)}, u32[]{:S(2)}) collective-permute-start(f32[2,64,256]{2,1,0:T(8,128)S(1)} %add.9), channel_id=1, source_target_pairs={{0,2},{1,7},{2,0},{3,5},{4,6},{5,3},{6,4},{7,1},{8,10},{9,15},{10,... | collective-permute-start | bytes 393224 | tf_op jit(solution)/shard_map/ppermute | solution.py:28
  12.8 7.5 %collective-permute-start.8 = (f32[64,256]{1,0:T(8,128)S(1)}, f32[64,256]{1,0:T(8,128)S(1)}, u32[]{:S(2)}, u32[]{:S(2)}) collective-permute-start(f32[64,256]{1,0:T(8,128)S(1)} %get-tuple-element.18), channel_id=1, source_target_pairs={{0,4},{1,5},{2,6},{3,7},{4,0},{5,1},{6,2},{7,3},{8,12},{9,13},{10,... | collective-permute-start | bytes 196616 | tf_op jit(solution)/shard_map/ppermute | solution.py:23
  17.5 2.9 %collective-permute-start.6 = (f32[64,256]{1,0:T(8,128)S(1)}, f32[64,256]{1,0:T(8,128)S(1)}, u32[]{:S(2)}, u32[]{:S(2)}) collective-permute-start(f32[64,256]{1,0:T(8,128)S(1)} %get-tuple-element.21), channel_id=1, source_target_pairs={{0,1},{1,0},{2,3},{3,2},{4,5},{5,4},{6,7},{7,6},{8,9},{9,8},{10,11... | collective-permute-start | bytes 196616 | tf_op jit(solution)/shard_map/ppermute | solution.py:23
  20.6 1.6 %collective-permute-start.10 = (f32[32,128]{1,0:T(8,128)S(1)}, f32[32,128]{1,0:T(8,128)S(1)}, u32[]{:S(2)}, u32[]{:S(2)}) collective-permute-start(f32[32,128]{1,0:T(8,128)S(1)} %get-tuple-element.17), channel_id=1, source_target_pairs={{0,1},{1,0},{2,3},{3,2},{4,5},{5,4},{6,7},{7,6},{8,9},{9,8},{10,11... | collective-permute-start | bytes 49160 | tf_op jit(solution)/shard_map/ppermute | solution.py:23
  20.8 4.1 %collective-permute-start.9 = (f32[32,128]{1,0:T(8,128)S(1)}, f32[32,128]{1,0:T(8,128)S(1)}, u32[]{:S(2)}, u32[]{:S(2)}) collective-permute-start(f32[32,128]{1,0:T(8,128)S(1)} %get-tuple-element.17), channel_id=1, source_target_pairs={{0,25},{1,24},{2,27},{3,26},{4,29},{5,28},{6,31},{7,30},{8,17},{9,... | collective-permute-start | bytes 49160 | tf_op jit(solution)/shard_map/ppermute | solution.py:23
  22.3 3.3 %collective-permute-start.13 = (f32[32,128]{1,0:T(8,128)S(1)}, f32[32,128]{1,0:T(8,128)S(1)}, u32[]{:S(2)}, u32[]{:S(2)}) collective-permute-start(f32[32,128]{1,0:T(8,128)S(1)} %add.11._.refs_2_), channel_id=1, source_target_pairs={{0,17},{1,16},{2,19},{3,18},{4,21},{5,20},{6,23},{7,22},{8,25},{9,... | collective-permute-start | bytes 49160 | tf_op jit(solution)/shard_map/ppermute | solution.py:23
  23.1 3.2 %collective-permute-start.12 = (f32[32,128]{1,0:T(8,128)S(1)}, f32[32,128]{1,0:T(8,128)S(1)}, u32[]{:S(2)}, u32[]{:S(2)}) collective-permute-start(f32[32,128]{1,0:T(8,128)S(1)} %add.11._.refs_2_), channel_id=1, source_target_pairs={{0,9},{1,8},{2,11},{3,10},{4,13},{5,12},{6,15},{7,14},{8,1},{9,0},... | collective-permute-start | bytes 49160 | tf_op jit(solution)/shard_map/ppermute | solution.py:23
  24.8 1.5 %collective-permute-start.11 = (f32[32,128]{1,0:T(8,128)S(1)}, f32[32,128]{1,0:T(8,128)S(1)}, u32[]{:S(2)}, u32[]{:S(2)}) collective-permute-start(f32[32,128]{1,0:T(8,128)S(1)} %hand.1.refs_1_), channel_id=1, source_target_pairs={{0,1},{1,0},{2,3},{3,2},{4,5},{5,4},{6,7},{7,6},{8,9},{9,8},{10,11... | collective-permute-start | bytes 49160 | tf_op jit(solution)/shard_map/ppermute | solution.py:23
  26.3 5.0 %collective-permute-start.14 = (f32[32,128]{1,0:T(8,128)S(1)}, f32[32,128]{1,0:T(8,128)S(1)}, u32[]{:S(2)}, u32[]{:S(2)}) collective-permute-start(f32[32,128]{1,0:T(8,128)S(1)} %sum.1.refs_2_), channel_id=1, source_target_pairs={{0,4},{1,7},{2,6},{3,5},{4,0},{5,3},{6,2},{7,1},{8,12},{9,15},{10,... | collective-permute-start | bytes 49160 | tf_op jit(solution)/shard_map/ppermute | solution.py:28
  27.6 3.7 %collective-permute-start.16 = (f32[32,128]{1,0:T(8,128)S(1)}, f32[32,128]{1,0:T(8,128)S(1)}, u32[]{:S(2)}, u32[]{:S(2)}) collective-permute-start(f32[32,128]{1,0:T(8,128)S(1)} %sum.1.refs_2_), channel_id=1, source_target_pairs={{0,3},{1,2},{2,1},{3,0},{4,7},{5,6},{6,5},{7,4},{8,11},{9,10},{10,... | collective-permute-start | bytes 49160 | tf_op jit(solution)/shard_map/ppermute | solution.py:23
  31.3 1.2 %collective-permute-start.15 = (f32[32,128]{1,0:T(8,128)S(1)}, f32[32,128]{1,0:T(8,128)S(1)}, u32[]{:S(2)}, u32[]{:S(2)}) collective-permute-start(f32[32,128]{1,0:T(8,128)S(1)} %collective-permute-done.14.refs_1_), channel_id=1, source_target_pairs={{0,1},{1,0},{2,3},{3,2},{4,5},{5,4},{6,7},{7,6},{8,9},{9,8},{10,11... | collective-permute-start | bytes 49160 | tf_op jit(solution)/shard_map/ppermute | solution.py:23

commit v9 on v8

--- a/solution.py
+++ b/solution.py
@@ -81,14 +81,10 @@
     y = functools.reduce(jnp.add, [part[...] for part in parts])
     y_out[...] = y
     half = y.shape[0] // 2
-    for k in range(2):
-        gram_out[:, k * 2 * half : (k + 1) * 2 * half] = scale * lax.dot_general(
-            y[k * half : (k + 1) * half],
-            y,
-            (((1,), (1,)), ((), ())),
-            precision=EXACT,
-            preferred_element_type=F32,
-        )
+    gram = scale * lax.dot_general(
+        y, y, (((1,), (1,)), ((), ())), precision=EXACT, preferred_element_type=F32
+    )
+    gram_out[...] = jnp.concatenate([gram[:half], gram[half:]], axis=1)
 
 
 def hand_kernel(came, _, out):

time: 34.6 us -> 34.6 us (level)
  no operation moved by 1% of the time
where the time goes in v9:
time: 34.6 us; the launch traced here: 34.4 us
  starting transfers between devices  14.9 us (43%)
  waiting for transfers between devices  14.2 us (41%)
  Pallas kernels  3.95 us (11%)
  between operations  1.38 us (4%)
    ppermute x15, starting transfers between devices, swap(): return lax.ppermute(x, ('row', 'col'), pairs)  12 us
    ppermute x15, waiting for transfers between devices, swap(): return lax.ppermute(x, ('row', 'col'), pairs)  8.73 us
    ppermute x2, waiting for transfers between devices, split_swap(): lax.ppermute(x, 'col', [(j, j ^ (second if j & 1 else first)) for j in ra...  5.44 us
    ppermute x2, starting transfers between devices, split_swap(): lax.ppermute(x, 'col', [(j, j ^ (second if j & 1 else first)) for j in ra...  2.89 us
    pallas_call x1, Pallas kernels, local(): pl.pallas_call(factor_kernel, out_shape=(jax.ShapeDtypeStruct((vectors, w...  2 us
    pallas_call x1, Pallas kernels, local(): pl.pallas_call(turn_kernel, out_shape=jax.ShapeDtypeStruct(tiles.shape[:1...  0.86 us
    pallas_call x1, Pallas kernels, local(): pl.pallas_call(functools.partial(product_kernel, (0, *order)), out_shape=...  0.79 us
  transfers between devices with their start and end apart: 17, of which 10 were waited for; matrix products, arithmetic and copies ran while one was open for 0% of the time, Pallas kernels for 3%

profile of v9, /device:TPU:0, one launch (start us, length us, event | category | flops | bytes accessed | tf_op | source)
XLA Modules:
  0.0 34.4 jit_solution(13933124413414785593)
XLA Ops:
  0.6 0.5 %collective-permute-start.1 = (bf16[64,256]{1,0:T(8,128)(2,1)}, bf16[64,256]{1,0:T(8,128)(2,1)S(1)}, u32[]{:S(2)}, u32[]{:S(2)}) collective-permute-start(bf16[64,256]{1,0:T(8,128)(2,1)} %refs_0_.1), channel_id=1, source_target_pairs={{0,1},{1,0},{2,3},{3,2},{4,5},{5,4},{6,7},{7,6},{8,9},{9,8},{10,11... | collective-permute-start | bytes 98312 | tf_op jit(solution)/shard_map/ppermute | solution.py:23
  1.2 3.5 %collective-permute-start = (bf16[64,256]{1,0:T(8,128)(2,1)}, bf16[64,256]{1,0:T(8,128)(2,1)S(1)}, u32[]{:S(2)}, u32[]{:S(2)}) collective-permute-start(bf16[64,256]{1,0:T(8,128)(2,1)} %refs_0_.1), channel_id=1, source_target_pairs={{0,24},{1,25},{2,26},{3,27},{4,28},{5,29},{6,30},{7,31},{8,16},{9,... | collective-permute-start | bytes 98312 | tf_op jit(solution)/shard_map/ppermute | solution.py:23
  4.7 0.5 %collective-permute-start.3 = (bf16[64,256]{1,0:T(8,128)(2,1)}, bf16[64,256]{1,0:T(8,128)(2,1)S(1)}, u32[]{:S(2)}, u32[]{:S(2)}) collective-permute-start(bf16[64,256]{1,0:T(8,128)(2,1)} %refs_0_.1), channel_id=1, source_target_pairs={{0,16},{1,17},{2,18},{3,19},{4,20},{5,21},{6,22},{7,23},{8,24},{9,... | collective-permute-start | bytes 98312 | tf_op jit(solution)/shard_map/ppermute | solution.py:23
  5.2 0.0 collective-permute-done.1
  5.2 0.1 collective-permute-start.2
  5.3 0.9 %turn.1.turned = bf16[24,256,256]{2,1,0:T(8,128)(2,1)S(1)} custom-call(bf16[24,256,256]{2,1,0:T(8,128)(2,1)S(1)} %copy-done), custom_call_target="tpu_custom_call" | custom-call | flops 1000000000 | tf_op jit(solution)/shard_map/turn/pallas_call | solution.py:161
  6.8 0.0 collective-permute-done.refs_1_
  6.9 1.9 %collective-permute-done.3.refs_3_ = bf16[64,256]{1,0:T(8,128)(2,1)S(1)} collective-permute-done((bf16[64,256]{1,0:T(8,128)(2,1)}, bf16[64,256]{1,0:T(8,128)(2,1)S(1)}, u32[]{:S(2)}, u32[]{:S(2)}) %collective-permute-start.3) | collective-permute-done | bytes 32800 | tf_op jit(solution)/shard_map/ppermute | solution.py:23
  8.8 0.1 collective-permute-done.2.refs_2_
  8.9 0.8 %product.1 = (f32[2,64,256]{2,1,0:T(8,128)S(1)}, f32[2,64,256]{2,1,0:T(8,128)S(1)}, f32[2,64,256]{2,1,0:T(8,128)S(1)}, f32[2,64,256]{2,1,0:T(8,128)S(1)}) custom-call(s32[2,24]{1,0:T(2,128)S(1)} %select.1, bf16[24,256,256]{2,1,0:T(8,128)(2,1)S(1)} %turn.1.turned, bf16[64,256]{1,0:T(8,128)(2,1)S(1)} %copy-done.1, ...), custom_call_target="tpu_custom_call" | custom-call | tf_op jit(solution)/shard_map/product/pallas_call | solution.py:171
  9.7 0.2 collective-permute-start.4
  9.9 0.4 %collective-permute-start.7 = (f32[2,64,256]{2,1,0:T(8,128)S(1)}, f32[2,64,256]{2,1,0:T(8,128)S(1)}, u32[]{:S(2)}, u32[]{:S(2)}) collective-permute-start(f32[2,64,256]{2,1,0:T(8,128)S(1)} %get-tuple-element.15), channel_id=1, source_target_pairs={{0,1},{1,0},{2,3},{3,2},{4,5},{5,4},{6,7},{7,6},{8,9},{9,8},{10,11... | collective-permute-start | bytes 393224 | tf_op jit(solution)/shard_map/ppermute | solution.py:23
  10.3 0.8 %collective-permute-done.4 = f32[2,64,256]{2,1,0:T(8,128)S(1)} collective-permute-done((f32[2,64,256]{2,1,0:T(8,128)S(1)}, f32[2,64,256]{2,1,0:T(8,128)S(1)}, u32[]{:S(2)}, u32[]{:S(2)}) %collective-permute-start.4) | collective-permute-done | bytes 131104 | tf_op jit(solution)/shard_map/ppermute | solution.py:23
  11.1 1.6 %collective-permute-start.5 = (f32[2,64,256]{2,1,0:T(8,128)S(1)}, f32[2,64,256]{2,1,0:T(8,128)S(1)}, u32[]{:S(2)}, u32[]{:S(2)}) collective-permute-start(f32[2,64,256]{2,1,0:T(8,128)S(1)} %add.9), channel_id=1, source_target_pairs={{0,2},{1,7},{2,0},{3,5},{4,6},{5,3},{6,4},{7,1},{8,10},{9,15},{10,... | collective-permute-start | bytes 393224 | tf_op jit(solution)/shard_map/ppermute | solution.py:28
  12.8 2.7 %collective-permute-start.8 = (f32[64,256]{1,0:T(8,128)S(1)}, f32[64,256]{1,0:T(8,128)S(1)}, u32[]{:S(2)}, u32[]{:S(2)}) collective-permute-start(f32[64,256]{1,0:T(8,128)S(1)} %get-tuple-element.18), channel_id=1, source_target_pairs={{0,4},{1,5},{2,6},{3,7},{4,0},{5,1},{6,2},{7,3},{8,12},{9,13},{10,... | collective-permute-start | bytes 196616 | tf_op jit(solution)/shard_map/ppermute | solution.py:23
  15.5 2.0 %collective-permute-done.5 = f32[2,64,256]{2,1,0:T(8,128)S(1)} collective-permute-done((f32[2,64,256]{2,1,0:T(8,128)S(1)}, f32[2,64,256]{2,1,0:T(8,128)S(1)}, u32[]{:S(2)}, u32[]{:S(2)}) %collective-permute-start.5) | collective-permute-done | bytes 131104 | tf_op jit(solution)/shard_map/ppermute | solution.py:28
  17.5 0.1 collective-permute-start.6
  17.6 2.8 %collective-permute-done.8.refs_3_ = f32[64,256]{1,0:T(8,128)S(1)} collective-permute-done((f32[64,256]{1,0:T(8,128)S(1)}, f32[64,256]{1,0:T(8,128)S(1)}, u32[]{:S(2)}, u32[]{:S(2)}) %collective-permute-start.8) | collective-permute-done | bytes 65568 | tf_op jit(solution)/shard_map/ppermute | solution.py:23
  20.3 0.3 gram.1
  20.6 0.1 collective-permute-start.10
  20.7 1.5 %collective-permute-start.9 = (f32[32,128]{1,0:T(8,128)S(1)}, f32[32,128]{1,0:T(8,128)S(1)}, u32[]{:S(2)}, u32[]{:S(2)}) collective-permute-start(f32[32,128]{1,0:T(8,128)S(1)} %get-tuple-element.17), channel_id=1, source_target_pairs={{0,25},{1,24},{2,27},{3,26},{4,29},{5,28},{6,31},{7,30},{8,17},{9,... | collective-permute-start | bytes 49160 | tf_op jit(solution)/shard_map/ppermute | solution.py:23
  22.2 0.9 %collective-permute-start.13 = (f32[32,128]{1,0:T(8,128)S(1)}, f32[32,128]{1,0:T(8,128)S(1)}, u32[]{:S(2)}, u32[]{:S(2)}) collective-permute-start(f32[32,128]{1,0:T(8,128)S(1)} %add.11._.refs_2_), channel_id=1, source_target_pairs={{0,17},{1,16},{2,19},{3,18},{4,21},{5,20},{6,23},{7,22},{8,25},{9,... | collective-permute-start | bytes 49160 | tf_op jit(solution)/shard_map/ppermute | solution.py:23
  23.1 0.9 %collective-permute-start.12 = (f32[32,128]{1,0:T(8,128)S(1)}, f32[32,128]{1,0:T(8,128)S(1)}, u32[]{:S(2)}, u32[]{:S(2)}) collective-permute-start(f32[32,128]{1,0:T(8,128)S(1)} %add.11._.refs_2_), channel_id=1, source_target_pairs={{0,9},{1,8},{2,11},{3,10},{4,13},{5,12},{6,15},{7,14},{8,1},{9,0},... | collective-permute-start | bytes 49160 | tf_op jit(solution)/shard_map/ppermute | solution.py:23
  24.0 0.8 %collective-permute-done.9.came = f32[32,128]{1,0:T(8,128)S(1)} collective-permute-done((f32[32,128]{1,0:T(8,128)S(1)}, f32[32,128]{1,0:T(8,128)S(1)}, u32[]{:S(2)}, u32[]{:S(2)}) %collective-permute-start.9) | collective-permute-done | bytes 16416 | tf_op jit(solution)/shard_map/ppermute | solution.py:23
  24.8 0.4 %collective-permute-start.11 = (f32[32,128]{1,0:T(8,128)S(1)}, f32[32,128]{1,0:T(8,128)S(1)}, u32[]{:S(2)}, u32[]{:S(2)}) collective-permute-start(f32[32,128]{1,0:T(8,128)S(1)} %hand.1.refs_1_), channel_id=1, source_target_pairs={{0,1},{1,0},{2,3},{3,2},{4,5},{5,4},{6,7},{7,6},{8,9},{9,8},{10,11... | collective-permute-start | bytes 49160 | tf_op jit(solution)/shard_map/ppermute | solution.py:23
  25.2 0.3 %collective-permute-done.13.refs_4_ = f32[32,128]{1,0:T(8,128)S(1)} collective-permute-done((f32[32,128]{1,0:T(8,128)S(1)}, f32[32,128]{1,0:T(8,128)S(1)}, u32[]{:S(2)}, u32[]{:S(2)}) %collective-permute-start.13) | collective-permute-done | bytes 16416 | tf_op jit(solution)/shard_map/ppermute | solution.py:23
  25.6 0.7 %collective-permute-done.12.refs_3_ = f32[32,128]{1,0:T(8,128)S(1)} collective-permute-done((f32[32,128]{1,0:T(8,128)S(1)}, f32[32,128]{1,0:T(8,128)S(1)}, u32[]{:S(2)}, u32[]{:S(2)}) %collective-permute-start.12) | collective-permute-done | bytes 16416 | tf_op jit(solution)/shard_map/ppermute | solution.py:23
  26.3 1.3 %collective-permute-start.14 = (f32[32,128]{1,0:T(8,128)S(1)}, f32[32,128]{1,0:T(8,128)S(1)}, u32[]{:S(2)}, u32[]{:S(2)}) collective-permute-start(f32[32,128]{1,0:T(8,128)S(1)} %sum.1.refs_2_), channel_id=1, source_target_pairs={{0,4},{1,7},{2,6},{3,5},{4,0},{5,3},{6,2},{7,1},{8,12},{9,15},{10,... | collective-permute-start | bytes 49160 | tf_op jit(solution)/shard_map/ppermute | solution.py:28
  27.5 0.2 collective-permute-start.16
  27.8 3.5 %collective-permute-done.14.refs_1_ = f32[32,128]{1,0:T(8,128)S(1)} collective-permute-done((f32[32,128]{1,0:T(8,128)S(1)}, f32[32,128]{1,0:T(8,128)S(1)}, u32[]{:S(2)}, u32[]{:S(2)}) %collective-permute-start.14) | collective-permute-done | bytes 16416 | tf_op jit(solution)/shard_map/ppermute | solution.py:28
  31.2 1.2 %collective-permute-done.15.refs_0_ = f32[32,128]{1,0:T(8,128)S(1)} collective-permute-done((f32[32,128]{1,0:T(8,128)S(1)}, f32[32,128]{1,0:T(8,128)S(1)}, u32[]{:S(2)}, u32[]{:S(2)}) %collective-permute-start.15) | collective-permute-done | bytes 16416 | tf_op jit(solution)/shard_map/ppermute | solution.py:23
  32.4 2.0 %factor.1 = (f32[64,256]{1,0:T(8,128)}, f32[64,64]{1,0:T(8,128)}) custom-call(f32[64,256]{1,0:T(8,128)S(1)} %get-tuple-element.16.y_ref, f32[32,128]{1,0:T(8,128)S(1)} %collective-permute-done.15.refs_0_, f32[32,128]{1,0:T(8,128)S(1)} %collective-permute-done.14.refs_1_, f32[32,128]{1,0:T(8,128)S(1)} %sum.1.refs_2_, ...), custom_call_target="tpu_custom_call" | custom-call | tf_op jit(solution)/shard_map/factor/pallas_call | solution.py:233
  (21 shorter events, 0.1 us)
Async XLA Ops:
  0.6 4.7 %copy-start = (bf16[24,256,256]{2,1,0:T(8,128)(2,1)S(1)}, bf16[24,256,256]{2,1,0:T(8,128)(2,1)}, u32[]{:S(2)}) copy-start(bf16[24,256,256]{2,1,0:T(8,128)(2,1)} %tiles.1) | copy-start | bytes 9437188
  0.6 4.6 %collective-permute-start.1 = (bf16[64,256]{1,0:T(8,128)(2,1)}, bf16[64,256]{1,0:T(8,128)(2,1)S(1)}, u32[]{:S(2)}, u32[]{:S(2)}) collective-permute-start(bf16[64,256]{1,0:T(8,128)(2,1)} %refs_0_.1), channel_id=1, source_target_pairs={{0,1},{1,0},{2,3},{3,2},{4,5},{5,4},{6,7},{7,6},{8,9},{9,8},{10,11... | collective-permute-start | bytes 98312 | tf_op jit(solution)/shard_map/ppermute | solution.py:23
  1.2 5.7 %collective-permute-start = (bf16[64,256]{1,0:T(8,128)(2,1)}, bf16[64,256]{1,0:T(8,128)(2,1)S(1)}, u32[]{:S(2)}, u32[]{:S(2)}) collective-permute-start(bf16[64,256]{1,0:T(8,128)(2,1)} %refs_0_.1), channel_id=1, source_target_pairs={{0,24},{1,25},{2,26},{3,27},{4,28},{5,29},{6,30},{7,31},{8,16},{9,... | collective-permute-start | bytes 98312 | tf_op jit(solution)/shard_map/ppermute | solution.py:23
  4.7 4.1 %collective-permute-start.3 = (bf16[64,256]{1,0:T(8,128)(2,1)}, bf16[64,256]{1,0:T(8,128)(2,1)S(1)}, u32[]{:S(2)}, u32[]{:S(2)}) collective-permute-start(bf16[64,256]{1,0:T(8,128)(2,1)} %refs_0_.1), channel_id=1, source_target_pairs={{0,16},{1,17},{2,18},{3,19},{4,20},{5,21},{6,22},{7,23},{8,24},{9,... | collective-permute-start | bytes 98312 | tf_op jit(solution)/shard_map/ppermute | solution.py:23
  5.2 1.6 %copy-start.2 = (s32[24,2]{0,1:T(2,128)S(1)}, s32[24,2]{0,1:T(2,128)}, u32[]{:S(2)}) copy-start(s32[24,2]{0,1:T(2,128)} %param.6) | copy-start | bytes 580
  5.2 3.7 %copy-start.1 = (bf16[64,256]{1,0:T(8,128)(2,1)S(1)}, bf16[64,256]{1,0:T(8,128)(2,1)}, u32[]{:S(2)}) copy-start(bf16[64,256]{1,0:T(8,128)(2,1)} %refs_0_.1) | copy-start | bytes 98308
  5.2 3.7 %collective-permute-start.2 = (bf16[64,256]{1,0:T(8,128)(2,1)S(1)}, bf16[64,256]{1,0:T(8,128)(2,1)S(1)}, u32[]{:S(2)}, u32[]{:S(2)}) collective-permute-start(bf16[64,256]{1,0:T(8,128)(2,1)S(1)} %collective-permute-done.1), channel_id=1, source_target_pairs={{0,9},{1,8},{2,11},{3,10},{4,13},{5,12},{6,15},{7,14},{8,1},{9,0},... | collective-permute-start | bytes 98312 | tf_op jit(solution)/shard_map/ppermute | solution.py:23
  9.7 1.4 %collective-permute-start.4 = (f32[2,64,256]{2,1,0:T(8,128)S(1)}, f32[2,64,256]{2,1,0:T(8,128)S(1)}, u32[]{:S(2)}, u32[]{:S(2)}) collective-permute-start(f32[2,64,256]{2,1,0:T(8,128)S(1)} %get-tuple-element.13), channel_id=1, source_target_pairs={{0,1},{1,0},{2,3},{3,2},{4,5},{5,4},{6,7},{7,6},{8,9},{9,8},{10,11... | collective-permute-start | bytes 393224 | tf_op jit(solution)/shard_map/ppermute | solution.py:23
  9.9 2.9 %collective-permute-start.7 = (f32[2,64,256]{2,1,0:T(8,128)S(1)}, f32[2,64,256]{2,1,0:T(8,128)S(1)}, u32[]{:S(2)}, u32[]{:S(2)}) collective-permute-start(f32[2,64,256]{2,1,0:T(8,128)S(1)} %get-tuple-element.15), channel_id=1, source_target_pairs={{0,1},{1,0},{2,3},{3,2},{4,5},{5,4},{6,7},{7,6},{8,9},{9,8},{10,11... | collective-permute-start | bytes 393224 | tf_op jit(solution)/shard_map/ppermute | solution.py:23
  11.1 6.3 %collective-permute-start.5 = (f32[2,64,256]{2,1,0:T(8,128)S(1)}, f32[2,64,256]{2,1,0:T(8,128)S(1)}, u32[]{:S(2)}, u32[]{:S(2)}) collective-permute-start(f32[2,64,256]{2,1,0:T(8,128)S(1)} %add.9), channel_id=1, source_target_pairs={{0,2},{1,7},{2,0},{3,5},{4,6},{5,3},{6,4},{7,1},{8,10},{9,15},{10,... | collective-permute-start | bytes 393224 | tf_op jit(solution)/shard_map/ppermute | solution.py:28
  12.8 7.5 %collective-permute-start.8 = (f32[64,256]{1,0:T(8,128)S(1)}, f32[64,256]{1,0:T(8,128)S(1)}, u32[]{:S(2)}, u32[]{:S(2)}) collective-permute-start(f32[64,256]{1,0:T(8,128)S(1)} %get-tuple-element.18), channel_id=1, source_target_pairs={{0,4},{1,5},{2,6},{3,7},{4,0},{5,1},{6,2},{7,3},{8,12},{9,13},{10,... | collective-permute-start | bytes 196616 | tf_op jit(solution)/shard_map/ppermute | solution.py:23
  17.5 2.9 %collective-permute-start.6 = (f32[64,256]{1,0:T(8,128)S(1)}, f32[64,256]{1,0:T(8,128)S(1)}, u32[]{:S(2)}, u32[]{:S(2)}) collective-permute-start(f32[64,256]{1,0:T(8,128)S(1)} %get-tuple-element.21), channel_id=1, source_target_pairs={{0,1},{1,0},{2,3},{3,2},{4,5},{5,4},{6,7},{7,6},{8,9},{9,8},{10,11... | collective-permute-start | bytes 196616 | tf_op jit(solution)/shard_map/ppermute | solution.py:23
  20.6 1.6 %collective-permute-start.10 = (f32[32,128]{1,0:T(8,128)S(1)}, f32[32,128]{1,0:T(8,128)S(1)}, u32[]{:S(2)}, u32[]{:S(2)}) collective-permute-start(f32[32,128]{1,0:T(8,128)S(1)} %get-tuple-element.17), channel_id=1, source_target_pairs={{0,1},{1,0},{2,3},{3,2},{4,5},{5,4},{6,7},{7,6},{8,9},{9,8},{10,11... | collective-permute-start | bytes 49160 | tf_op jit(solution)/shard_map/ppermute | solution.py:23
  20.7 4.1 %collective-permute-start.9 = (f32[32,128]{1,0:T(8,128)S(1)}, f32[32,128]{1,0:T(8,128)S(1)}, u32[]{:S(2)}, u32[]{:S(2)}) collective-permute-start(f32[32,128]{1,0:T(8,128)S(1)} %get-tuple-element.17), channel_id=1, source_target_pairs={{0,25},{1,24},{2,27},{3,26},{4,29},{5,28},{6,31},{7,30},{8,17},{9,... | collective-permute-start | bytes 49160 | tf_op jit(solution)/shard_map/ppermute | solution.py:23
  22.2 3.3 %collective-permute-start.13 = (f32[32,128]{1,0:T(8,128)S(1)}, f32[32,128]{1,0:T(8,128)S(1)}, u32[]{:S(2)}, u32[]{:S(2)}) collective-permute-start(f32[32,128]{1,0:T(8,128)S(1)} %add.11._.refs_2_), channel_id=1, source_target_pairs={{0,17},{1,16},{2,19},{3,18},{4,21},{5,20},{6,23},{7,22},{8,25},{9,... | collective-permute-start | bytes 49160 | tf_op jit(solution)/shard_map/ppermute | solution.py:23
  23.1 3.2 %collective-permute-start.12 = (f32[32,128]{1,0:T(8,128)S(1)}, f32[32,128]{1,0:T(8,128)S(1)}, u32[]{:S(2)}, u32[]{:S(2)}) collective-permute-start(f32[32,128]{1,0:T(8,128)S(1)} %add.11._.refs_2_), channel_id=1, source_target_pairs={{0,9},{1,8},{2,11},{3,10},{4,13},{5,12},{6,15},{7,14},{8,1},{9,0},... | collective-permute-start | bytes 49160 | tf_op jit(solution)/shard_map/ppermute | solution.py:23
  24.8 1.4 %collective-permute-start.11 = (f32[32,128]{1,0:T(8,128)S(1)}, f32[32,128]{1,0:T(8,128)S(1)}, u32[]{:S(2)}, u32[]{:S(2)}) collective-permute-start(f32[32,128]{1,0:T(8,128)S(1)} %hand.1.refs_1_), channel_id=1, source_target_pairs={{0,1},{1,0},{2,3},{3,2},{4,5},{5,4},{6,7},{7,6},{8,9},{9,8},{10,11... | collective-permute-start | bytes 49160 | tf_op jit(solution)/shard_map/ppermute | solution.py:23
  26.3 5.0 %collective-permute-start.14 = (f32[32,128]{1,0:T(8,128)S(1)}, f32[32,128]{1,0:T(8,128)S(1)}, u32[]{:S(2)}, u32[]{:S(2)}) collective-permute-start(f32[32,128]{1,0:T(8,128)S(1)} %sum.1.refs_2_), channel_id=1, source_target_pairs={{0,4},{1,7},{2,6},{3,5},{4,0},{5,3},{6,2},{7,1},{8,12},{9,15},{10,... | collective-permute-start | bytes 49160 | tf_op jit(solution)/shard_map/ppermute | solution.py:28
  27.5 3.7 %collective-permute-start.16 = (f32[32,128]{1,0:T(8,128)S(1)}, f32[32,128]{1,0:T(8,128)S(1)}, u32[]{:S(2)}, u32[]{:S(2)}) collective-permute-start(f32[32,128]{1,0:T(8,128)S(1)} %sum.1.refs_2_), channel_id=1, source_target_pairs={{0,3},{1,2},{2,1},{3,0},{4,7},{5,6},{6,5},{7,4},{8,11},{9,10},{10,... | collective-permute-start | bytes 49160 | tf_op jit(solution)/shard_map/ppermute | solution.py:23
  31.2 1.2 %collective-permute-start.15 = (f32[32,128]{1,0:T(8,128)S(1)}, f32[32,128]{1,0:T(8,128)S(1)}, u32[]{:S(2)}, u32[]{:S(2)}) collective-permute-start(f32[32,128]{1,0:T(8,128)S(1)} %collective-permute-done.14.refs_1_), channel_id=1, source_target_pairs={{0,1},{1,0},{2,3},{3,2},{4,5},{5,4},{6,7},{7,6},{8,9},{9,8},{10,11... | collective-permute-start | bytes 49160 | tf_op jit(solution)/shard_map/ppermute | solution.py:23
